TPU v7x, 32 devices: a whole 2x2x4 slice. The times are simulated.
32 devices in a mesh: dir: 2 (over core), wide: 16 (over z, y, x).
Axes of the slice: x: 2, y: 2, z: 4, core: 2. Of those that a mesh axis runs over, the one named last changes fastest.
Arguments:
- tokens: bfloat16 [16, 1176, 384], P('wide'), may hold values from -6 to 6
- cotangent: bfloat16 [16, 1176, 384], P('wide', 'dir'), may hold values from -6 to 6
- view_counts: int32 [16], P('wide'), may hold values from 2 to 3, as said below
- view_strides: int32 [16, 3], P('wide'), may hold values from 1 to 4
- view_offsets: int32 [16, 3], P('wide'), may hold values from 0 to 1176, as said below
- in_proj: float32 [384, 1536], P('wide'), may hold values from -0.3125 to 0.3125
- in_proj_first: float32 [384, 1536], P('wide'), may hold values from -8 to 8
- in_proj_second: float32 [384, 1536], P('wide'), may hold values from 9.897216 to 39.5136
- out_proj: float32 [768, 384], P('wide'), may hold values from -0.625 to 0.625
- out_proj_first: float32 [768, 384], P('wide'), may hold values from -16 to 16
- out_proj_second: float32 [768, 384], P('wide'), may hold values from 39.5136 to 158.0544
- norm_gain: float32 [384], P('wide'), may hold values from 0.5 to 1.5
- norm_gain_first: float32 [384], P('wide'), may hold values from -48 to 48
- norm_gain_second: float32 [384], P('wide'), may hold values from 248.3712 to 989.7216
- state_proj: float32 [2, 768, 56], P('dir', 'wide'), may hold values from -0.21875 to 0.21875
- state_proj_first: float32 [2, 768, 56], P('dir', 'wide'), may hold values from -4 to 4
- state_proj_second: float32 [2, 768, 56], P('dir', 'wide'), may hold values from 2.483712 to 9.897216
- step_proj: float32 [2, 24, 768], P('dir', None, 'wide'), may hold values from -1.25 to 1.25
- step_proj_first: float32 [2, 24, 768], P('dir', None, 'wide'), may hold values from -1.75 to 1.75
- step_proj_second: float32 [2, 24, 768], P('dir', None, 'wide'), may hold values from 0.395136 to 1.580544
- log_decay: float32 [2, 16, 768], P('dir', None, 'wide'), may hold values from 0 to 2.8
- log_decay_first: float32 [2, 16, 768], P('dir', None, 'wide'), may hold values from -1.75 to 1.75
- log_decay_second: float32 [2, 16, 768], P('dir', None, 'wide'), may hold values from 0.395136 to 1.580544
- channels: float32 [2, 7, 768], P('dir', None, 'wide'), may hold values from -7 to 2
- channels_first: float32 [2, 7, 768], P('dir', None, 'wide'), may hold values from -4 to 4
- channels_second: float32 [2, 7, 768], P('dir', None, 'wide'), may hold values from 2.483712 to 9.897216
Outputs:
- block_out: float32 [16, 1176, 384], P('wide', 'dir')
- token_grad: float32 [16, 1176, 384], P('wide', 'dir')
- step_stats: float32 [2, 2, 768], P('dir', None, 'wide')
- new_in_proj: float32 [384, 1536], P('wide')
- new_in_first: float32 [384, 1536], P('wide')
- new_in_second: float32 [384, 1536], P('wide')
- new_out_proj: float32 [768, 384], P('wide')
- new_out_first: float32 [768, 384], P('wide')
- new_out_second: float32 [768, 384], P('wide')
- new_gain: float32 [384], P('wide')
- new_gain_first: float32 [384], P('wide')
- new_gain_second: float32 [384], P('wide')
- new_state_proj: float32 [2, 768, 56], P('dir', 'wide')
- new_state_first: float32 [2, 768, 56], P('dir', 'wide')
- new_state_second: float32 [2, 768, 56], P('dir', 'wide')
- new_step_proj: float32 [2, 24, 768], P('dir', None, 'wide')
- new_step_first: float32 [2, 24, 768], P('dir', None, 'wide')
- new_step_second: float32 [2, 24, 768], P('dir', None, 'wide')
- new_log_decay: float32 [2, 16, 768], P('dir', None, 'wide')
- new_decay_first: float32 [2, 16, 768], P('dir', None, 'wide')
- new_decay_second: float32 [2, 16, 768], P('dir', None, 'wide')
- new_channels: float32 [2, 7, 768], P('dir', None, 'wide')
- new_chan_first: float32 [2, 7, 768], P('dir', None, 'wide')
- new_chan_second: float32 [2, 7, 768], P('dir', None, 'wide')
Inputs may be any that keep to these rules, and one draw needn't show every extreme that they name: `view_counts`: both counts occur in every draw. `view_offsets`: a video's views start at increasing offsets, lie inside its 1176 slots and do not intersect; entries at or past its view count equal 1176. `view_strides`: strides at or past a video's view count are not used.
All inputs are finite; a program needn't handle non-finite values.
Results may differ from a plain program's by a relative error of at most 0.015.
The roundings to bfloat16 on the way count: a program that leaves them out, or rounds other values in their place, can miss the bound.
Values may be sent and summed in bfloat16 or wider, within the bound.
A program may use at most 512 MiB of HBM per device.

v0:
```python
from functools import partial
import math

import jax
import jax.numpy as jnp
from jax import lax
from jax.sharding import PartitionSpec as P

PATCHES = 196
BLOCK = 28
STEP = 10
VIEW_TOK = 392


EPS_NORM = 1e-06
BETA_ONE = 0.9
BETA_TWO = 0.95
EPS_ADAM = 1e-08
RATES = (0.15, 0.1, 2.5, 0.12, 0.2, 1.0, 2.5)
DECAYS = (0.1, 0.1, 0.0, 0.1, 0.1, 0.0, 0.0)


def in_blocks(array, dim, size):
    before, after = (array.shape[:dim], array.shape[dim + 1 :])
    return jnp.moveaxis(array.reshape(*before, size, -1, *after), dim, 0)


def sum_at_owner(array, axis, dim):
    blocks = in_blocks(array, dim, lax.axis_size(axis))
    arrived = lax.all_to_all(blocks, axis, split_axis=0, concat_axis=0, tiled=True)
    return arrived.astype(jnp.float32).sum(axis=0)


def side_by_side(arrays, axis, dim, along):
    both = jnp.concatenate(arrays, axis=along)
    whole, at, outs = (sum_at_owner(both, axis, dim), 0, [])
    for a in arrays:
        outs.append(lax.slice_in_dim(whole, at, at + a.shape[along], axis=along))
        at += a.shape[along]
    return tuple(outs)


def layout(view_count, strides, offsets, slot_count, view_len, patches):
    places = jnp.arange(slot_count, dtype=jnp.int32)
    live_mask = jnp.zeros((slot_count,), jnp.float32)
    labels = jnp.full((slot_count,), -1, jnp.int32)
    clock_time = jnp.zeros((slot_count,), jnp.float32)
    for view_index in range(strides.shape[0]):
        view_start = offsets[view_index]
        inside = (
            (places >= view_start) & (places < view_start + view_len) & (view_index < view_count)
        )
        frame_no = (places - view_start) // patches
        live_mask = jnp.where(inside, 1.0, live_mask)
        labels = jnp.where(inside, view_index, labels)
        clock_time = jnp.where(
            inside, (frame_no * strides[view_index]).astype(jnp.float32), clock_time
        )
    return (live_mask, labels, clock_time)


def time_embed(clock_time, model_width):
    half_width = model_width // 2
    frequency = jnp.exp(-math.log(10000.0) * jnp.arange(half_width, dtype=jnp.float32) / half_width)
    angles = clock_time[:, None] * frequency[None, :]
    return jnp.concatenate([jnp.sin(angles), jnp.cos(angles)], 1)


def lag_masks(labels, tap_count):
    mask_rows = []
    for back_step in range(tap_count):
        before = jnp.concatenate(
            [jnp.full((back_step,), -2, jnp.int32), labels[: labels.shape[0] - back_step]]
        )
        mask_rows.append((before == labels).astype(jnp.float32))
    return jnp.stack(mask_rows)


def convolve(inner_rows, tap_rows, bias_row, lag_rows):
    total = bias_row[None, :] + tap_rows[0][None, :] * inner_rows
    for back_step in range(1, tap_rows.shape[0]):
        shifted = jnp.concatenate(
            [
                jnp.zeros((back_step, inner_rows.shape[1]), inner_rows.dtype),
                inner_rows[:-back_step],
            ],
            0,
        )
        total = total + tap_rows[back_step][None, :] * shifted * lag_rows[back_step][:, None]
    return jax.nn.silu(total)


def softstep(step_pre, bias_row):
    return jax.nn.softplus(step_pre + bias_row[None, :])


def lead_dot(left_side, right_side):
    return lax.dot_general(
        left_side, right_side, (((0,), (0,)), ((), ())), preferred_element_type=jnp.float32
    )


def tail_dot(left_side, right_side):
    return lax.dot_general(
        left_side, right_side, (((1,), (1,)), ((), ())), preferred_element_type=jnp.float32
    )


def orient(stream, values):
    return jnp.where(stream == 1, jnp.flip(values, 0), values)


def block_scan(acted_rows, step_size, b_rows, c_rows, log_rate, skip_row, keep_rows, block_len):
    decay_rate = -jnp.exp(log_rate)
    slot_count, inner_width = acted_rows.shape
    count_blocks = slot_count // block_len

    def by_position(values):
        return jnp.swapaxes(values.reshape((count_blocks, block_len) + values.shape[1:]), 0, 1)

    steps_now = by_position(step_size)
    driven = by_position(step_size * acted_rows)
    b_now = by_position(b_rows)
    c_now = by_position(c_rows)
    keep_now = by_position(keep_rows)

    @jax.checkpoint
    def advance(carried, inputs_now):
        step_row, drive_row, b_row, keep_row = inputs_now
        factor = jnp.exp(step_row[:, None, :] * decay_rate[None]) * keep_row[:, None, None]
        return factor * carried + drive_row[:, None, :] * b_row[:, :, None]

    def local_step(carried, inputs_now):
        return (advance(carried, inputs_now), None)

    initial = jnp.zeros((count_blocks,) + decay_rate.shape, jnp.float32)
    block_ends, _ = lax.scan(local_step, initial, (steps_now, driven, b_now, keep_now))
    whole_step = jnp.sum(steps_now, 0)
    unbroken = jnp.min(keep_now, 0)
    through = jnp.exp(whole_step[:, None, :] * decay_rate[None]) * unbroken[:, None, None]

    def combine(earlier, later):
        return (earlier[0] * later[0], later[0] * earlier[1] + later[1])

    _, reached = lax.associative_scan(combine, (through, block_ends))
    starts = jnp.concatenate([jnp.zeros_like(reached[:1]), reached[:-1]], 0)

    def full_step(carried, inputs_now):
        carried = advance(carried, inputs_now[:4])
        return (carried, jnp.sum(inputs_now[4][:, :, None] * carried, 1))

    _, outputs = lax.scan(full_step, starts, (steps_now, driven, b_now, keep_now, c_now))
    return (
        jnp.swapaxes(outputs, 0, 1).reshape(slot_count, inner_width)
        + skip_row[None, :] * acted_rows
    )


def adam_step(weight, gradient, first_moment, second, step_rate, decay_rate):
    first_moment = BETA_ONE * first_moment + (1.0 - BETA_ONE) * gradient
    second = BETA_TWO * second + (1.0 - BETA_TWO) * gradient * gradient
    first_hat = first_moment / (1.0 - BETA_ONE**STEP)
    second_hat = second / (1.0 - BETA_TWO**STEP)
    weight = weight - step_rate * (
        first_hat / (jnp.sqrt(second_hat) + EPS_ADAM) + decay_rate * weight
    )
    return (weight, first_moment, second)


def local(
    tokens,
    cotangent,
    view_counts,
    view_strides,
    view_offsets,
    in_proj,
    in_proj_first,
    in_proj_second,
    out_proj,
    out_proj_first,
    out_proj_second,
    norm_gain,
    norm_gain_first,
    norm_gain_second,
    state_proj,
    state_proj_first,
    state_proj_second,
    step_proj,
    step_proj_first,
    step_proj_second,
    log_decay,
    log_decay_first,
    log_decay_second,
    channels,
    channels_first,
    channels_second,
):
    stream = lax.axis_index("dir")
    wide_count = lax.axis_size("wide")
    w_in, w_out, gain_low, proj_low, step_low, decay_low, chan_low = (
        lax.all_gather(in_proj.astype(jnp.bfloat16), "wide", axis=0, tiled=True),
        lax.all_gather(out_proj.astype(jnp.bfloat16), "wide", axis=0, tiled=True),
        lax.all_gather(norm_gain.astype(jnp.bfloat16), "wide", axis=0, tiled=True),
        lax.all_gather(state_proj.astype(jnp.bfloat16), "wide", axis=1, tiled=True),
        lax.all_gather(step_proj.astype(jnp.bfloat16), "wide", axis=2, tiled=True),
        lax.all_gather(log_decay.astype(jnp.bfloat16), "wide", axis=2, tiled=True),
        lax.all_gather(channels.astype(jnp.bfloat16), "wide", axis=2, tiled=True),
    )
    model_width = w_in.shape[0]
    inner_width = w_out.shape[0]
    rank_width = step_low.shape[1]
    state_width = decay_low.shape[1]
    tap_count = chan_low.shape[1] - 3
    slot_count = tokens.shape[1]
    half_rows = cotangent.shape[1]
    first_row = stream * half_rows
    live_mask, labels, clock_time = layout(
        view_counts[0], view_strides[0], view_offsets[0], slot_count, VIEW_TOK, PATCHES
    )
    residual = tokens[0].astype(jnp.float32) + live_mask[:, None] * time_embed(
        clock_time, model_width
    )
    scale_rows = lax.rsqrt(jnp.mean(residual * residual, -1, keepdims=True) + EPS_NORM)
    unit_rows = residual * scale_rows
    gain = gain_low.astype(jnp.float32)
    normed = (unit_rows * gain[None, :]).astype(jnp.bfloat16)
    inner_x = jnp.dot(normed, w_in[:, :inner_width], preferred_element_type=jnp.float32)
    normed_half = lax.dynamic_slice_in_dim(normed, first_row, half_rows, 0)
    gate_in = jnp.dot(normed_half, w_in[:, inner_width:], preferred_element_type=jnp.float32)
    labels_oriented = orient(stream, labels)
    live_oriented = orient(stream, live_mask)
    lag_rows = lag_masks(labels_oriented, tap_count)
    chan_rows = chan_low[0].astype(jnp.float32)
    acted_rows, conv_back = jax.vjp(
        partial(convolve, lag_rows=lag_rows),
        orient(stream, inner_x),
        chan_rows[:tap_count],
        chan_rows[tap_count],
    )
    acted_low = acted_rows.astype(jnp.bfloat16)
    projected = jnp.dot(acted_low, proj_low[0], preferred_element_type=jnp.float32)
    step_in = projected[:, :rank_width].astype(jnp.bfloat16)
    step_pre = jnp.dot(step_in, step_low[0], preferred_element_type=jnp.float32)
    step_size, soft_back = jax.vjp(softstep, step_pre, chan_rows[tap_count + 1])
    b_rows = projected[:, rank_width : rank_width + state_width]
    c_rows = projected[:, rank_width + state_width :]
    scan_apply = partial(block_scan, keep_rows=lag_rows[1], block_len=BLOCK)
    result, scan_back = jax.vjp(
        scan_apply,
        acted_rows,
        step_size,
        b_rows,
        c_rows,
        decay_low[0].astype(jnp.float32),
        chan_rows[tap_count + 2],
    )
    step_stats = (
        jnp.stack(
            [
                jnp.sum(live_oriented[:, None] * step_size, 0),
                jnp.sum(live_oriented[:, None] * step_size * step_size, 0),
            ]
        )
        / VIEW_TOK
    )
    stats_total = lax.psum(step_stats, "wide")
    mixed_half = lax.psum_scatter(
        orient(stream, result).astype(jnp.bfloat16), "dir", scatter_dimension=0, tiled=True
    ).astype(jnp.float32)
    gate_sig = jax.nn.sigmoid(gate_in)
    gated_low = (mixed_half * gate_in * gate_sig).astype(jnp.bfloat16)
    branch = jnp.dot(gated_low, w_out, preferred_element_type=jnp.float32)
    residual_half = lax.dynamic_slice_in_dim(residual, first_row, half_rows, 0)
    live_half = lax.dynamic_slice_in_dim(live_mask, first_row, half_rows, 0)
    block_half = residual_half + live_half[:, None] * branch
    upstream = cotangent[0].astype(jnp.float32)
    branch_grad = (live_half[:, None] * upstream).astype(jnp.bfloat16)
    grad_out_proj = lead_dot(gated_low, branch_grad)
    gated_grad = tail_dot(branch_grad, w_out)
    mixed_grad = (gated_grad * gate_in * gate_sig).astype(jnp.bfloat16)
    gate_grad = (gated_grad * mixed_half * gate_sig * (1.0 + gate_in * (1.0 - gate_sig))).astype(
        jnp.bfloat16
    )
    spread = lax.all_gather(mixed_grad, "dir", axis=0, tiled=True)
    acted_scan_grad, step_grad, b_grad, c_grad, decay_grad, skip_grad = scan_back(
        orient(stream, spread.astype(jnp.float32))
    )
    pre_grad, step_bias_grad = soft_back(step_grad)
    pre_low = pre_grad.astype(jnp.bfloat16)
    grad_step_proj = lead_dot(step_in, pre_low)
    step_in_grad = tail_dot(pre_low, step_low[0])
    proj_grad = jnp.concatenate([step_in_grad, b_grad, c_grad], 1).astype(jnp.bfloat16)
    grad_state_proj = lead_dot(acted_low, proj_grad)
    acted_grad = acted_scan_grad + tail_dot(proj_grad, proj_low[0])
    inner_grad, tap_grad, conv_bias_grad = conv_back(acted_grad)
    inner_low = orient(stream, inner_grad).astype(jnp.bfloat16)
    grad_channels = jnp.concatenate(
        [tap_grad, conv_bias_grad[None], step_bias_grad[None], skip_grad[None]], 0
    )
    normed_part = tail_dot(inner_low, w_in[:, :inner_width])
    gate_part = tail_dot(gate_grad, w_in[:, inner_width:])
    own_rows = lax.dynamic_slice_in_dim(normed_part, first_row, half_rows, 0) + gate_part
    normed_part = lax.dynamic_update_slice_in_dim(normed_part, own_rows, first_row, 0)
    normed_grad = lax.psum_scatter(
        normed_part.astype(jnp.bfloat16), "dir", scatter_dimension=0, tiled=True
    ).astype(jnp.float32)
    grad_in_proj = jnp.concatenate(
        [lead_dot(normed, inner_low), lead_dot(normed_half, gate_grad)], 1
    )
    unit_half = lax.dynamic_slice_in_dim(unit_rows, first_row, half_rows, 0)
    scale_half = lax.dynamic_slice_in_dim(scale_rows, first_row, half_rows, 0)
    grad_gain = jnp.sum(normed_grad * unit_half, 0)
    unit_grad = normed_grad * gain[None, :]
    token_grad = upstream + scale_half * (
        unit_grad - unit_half * jnp.mean(unit_grad * unit_half, -1, keepdims=True)
    )
    grad_in_proj, grad_out_proj, grad_gain = (
        lax.psum(grad_in_proj.astype(jnp.bfloat16), "dir").astype(jnp.float32),
        lax.psum(grad_out_proj.astype(jnp.bfloat16), "dir").astype(jnp.float32),
        lax.psum(grad_gain.astype(jnp.bfloat16), "dir").astype(jnp.float32),
    )
    shard_size = step_stats.shape[1] // wide_count
    stats_shard = lax.dynamic_slice_in_dim(
        stats_total, lax.axis_index("wide") * shard_size, shard_size, 1
    )
    shard_in, shard_out, shard_gain, shard_state, shard_step, shard_decay, shard_chan = (
        sum_at_owner(grad_in_proj.astype(jnp.bfloat16), "wide", 0),
        sum_at_owner(grad_out_proj.astype(jnp.bfloat16), "wide", 0),
        sum_at_owner(grad_gain.astype(jnp.bfloat16), "wide", 0),
        sum_at_owner(grad_state_proj.astype(jnp.bfloat16), "wide", 0),
        *side_by_side(
            (
                grad_step_proj.astype(jnp.bfloat16),
                decay_grad.astype(jnp.bfloat16),
                grad_channels.astype(jnp.bfloat16),
            ),
            "wide",
            1,
            0,
        ),
    )
    new_in_proj, new_in_first, new_in_second = adam_step(
        in_proj, shard_in, in_proj_first, in_proj_second, RATES[0], DECAYS[0]
    )
    new_out_proj, new_out_first, new_out_second = adam_step(
        out_proj, shard_out, out_proj_first, out_proj_second, RATES[1], DECAYS[1]
    )
    new_gain, new_gain_first, new_gain_second = adam_step(
        norm_gain, shard_gain, norm_gain_first, norm_gain_second, RATES[2], DECAYS[2]
    )
    new_state_proj, new_state_first, new_state_second = adam_step(
        state_proj, shard_state[None], state_proj_first, state_proj_second, RATES[3], DECAYS[3]
    )
    new_step_proj, new_step_first, new_step_second = adam_step(
        step_proj, shard_step[None], step_proj_first, step_proj_second, RATES[4], DECAYS[4]
    )
    new_log_decay, new_decay_first, new_decay_second = adam_step(
        log_decay, shard_decay[None], log_decay_first, log_decay_second, RATES[5], DECAYS[5]
    )
    new_channels, new_chan_first, new_chan_second = adam_step(
        channels, shard_chan[None], channels_first, channels_second, RATES[6], DECAYS[6]
    )
    return (
        block_half[None],
        token_grad[None],
        stats_shard[None],
        new_in_proj,
        new_in_first,
        new_in_second,
        new_out_proj,
        new_out_first,
        new_out_second,
        new_gain,
        new_gain_first,
        new_gain_second,
        new_state_proj,
        new_state_first,
        new_state_second,
        new_step_proj,
        new_step_first,
        new_step_second,
        new_log_decay,
        new_decay_first,
        new_decay_second,
        new_channels,
        new_chan_first,
        new_chan_second,
    )


def solution(mesh):
    return jax.shard_map(
        local,
        mesh=mesh,
        in_specs=(
            P("wide", None, None),
            P("wide", "dir", None),
            P("wide"),
            P("wide", None),
            P("wide", None),
            P("wide", None),
            P("wide", None),
            P("wide", None),
            P("wide", None),
            P("wide", None),
            P("wide", None),
            P("wide"),
            P("wide"),
            P("wide"),
            P("dir", "wide", None),
            P("dir", "wide", None),
            P("dir", "wide", None),
            P("dir", None, "wide"),
            P("dir", None, "wide"),
            P("dir", None, "wide"),
            P("dir", None, "wide"),
            P("dir", None, "wide"),
            P("dir", None, "wide"),
            P("dir", None, "wide"),
            P("dir", None, "wide"),
            P("dir", None, "wide"),
        ),
        out_specs=(
            P("wide", "dir", None),
            P("wide", "dir", None),
            P("dir", None, "wide"),
            P("wide", None),
            P("wide", None),
            P("wide", None),
            P("wide", None),
            P("wide", None),
            P("wide", None),
            P("wide"),
            P("wide"),
            P("wide"),
            P("dir", "wide", None),
            P("dir", "wide", None),
            P("dir", "wide", None),
            P("dir", None, "wide"),
            P("dir", None, "wide"),
            P("dir", None, "wide"),
            P("dir", None, "wide"),
            P("dir", None, "wide"),
            P("dir", None, "wide"),
            P("dir", None, "wide"),
            P("dir", None, "wide"),
            P("dir", None, "wide"),
        ),
        check_vma=False,
    )
```

profile of v0, /device:TPU:0, one launch (start us, length us, event | category | flops | bytes accessed | tf_op | source)
XLA Modules:
  0.0 2141.7 jit_solution(18426961112055089663)
XLA Ops:
  33.2 43.8 %all-reduce.57 = bf16[384]{0:T(512)(128)(2,1)S(1)} all-reduce(bf16[384]{0:T(512)(128)(2,1)S(1)} %dynamic-update-slice), channel_id=1, replica_groups=mesh['dir'=2,'wide'=16] {'wide'}, use_global_device_ids=true, to_apply=%add.57 | all-reduce | flops 384 | bytes 1536
  77.5 37.7 %all_gather.29 = bf16[1,16,768]{1,0,2:T(2,128)(2,1)S(1)} all-gather(bf16[1,16,48]{1,0,2:T(2,128)(2,1)S(1)} %copy.167), channel_id=1, replica_groups=mesh['dir'=2,'wide'=16] {'wide'}, dimensions={2}, use_global_device_ids=true | all-gather | bytes 26112 | tf_op jit(solution)/shard_map/all_gather | solution.py:206
  115.4 42.1 %all_gather.24 = bf16[1,7,768]{1,0,2:T(2,128)(2,1)} all-gather(bf16[1,7,48]{1,0,2:T(2,128)(2,1)S(1)} %copy.163), channel_id=1, replica_groups=mesh['dir'=2,'wide'=16] {'wide'}, dimensions={2}, use_global_device_ids=true | all-gather | bytes 11424 | tf_op jit(solution)/shard_map/all_gather | solution.py:207
  157.5 39.0 %all_gather.27 = bf16[1,768,56]{2,1,0:T(8,128)(2,1)} all-gather(bf16[1,48,56]{2,1,0:T(8,128)(2,1)S(1)} %convert_element_type.170), channel_id=1, replica_groups=mesh['dir'=2,'wide'=16] {'wide'}, dimensions={1}, use_global_device_ids=true | all-gather | bytes 91392 | tf_op jit(solution)/shard_map/all_gather | solution.py:204
  202.4 40.5 %all_gather.30 = bf16[768,384]{1,0:T(8,128)(2,1)S(1)} all-gather(bf16[48,384]{1,0:T(8,128)(2,1)S(1)} %convert_element_type.177), channel_id=1, replica_groups=mesh['dir'=2,'wide'=16] {'wide'}, dimensions={0}, use_global_device_ids=true | all-gather | bytes 626688 | tf_op jit(solution)/shard_map/all_gather | solution.py:202
  254.1 40.5 %all_gather.28 = bf16[1,24,768]{1,0,2:T(2,128)(2,1)} all-gather(bf16[1,24,48]{1,0,2:T(2,128)(2,1)S(1)} %copy.164), channel_id=1, replica_groups=mesh['dir'=2,'wide'=16] {'wide'}, dimensions={2}, use_global_device_ids=true | all-gather | bytes 39168 | tf_op jit(solution)/shard_map/all_gather | solution.py:205
  299.7 17.1 slice_reduce_fusion
  320.8 30.3 %rev.21 = f32[1176,768]{1,0:T(8,128)} reverse(f32[1176,768]{1,0:T(8,128)} %fusion.43), dimensions={0} | reverse | bytes 7225344 | tf_op jit(solution)/shard_map/jit(_flip)/rev | solution.py:110
  359.1 30.3 %rev.24 = f32[1176,768]{1,0:T(8,128)} reverse(f32[1176,768]{1,0:T(8,128)} %reshape.403), dimensions={0} | reverse | bytes 7225344 | tf_op jit(solution)/shard_map/jit(_flip)/rev | solution.py:110
  389.4 12.8 multiply_reduce_fusion.10
  424.4 9.7 copy_bitcast_fusion.1
  434.8 18.5 broadcast.458.clone
  453.3 116.4 %while.80 = (s32[]{:T(128)}, f32[42,16,768]{2,1,0:T(8,128)S(1)}, f32[28,42,16,768]{3,2,1,0:T(8,128)}, f32[28,42,768]{2,1,0:T(8,128)}, f32[1,16,768]{2,1,0:T(8,12...) while((s32[]{:T(128)}, f32[42,16,768]{2,1,0:T(8,128)S(1)}, ...), condition=%wide.region_2.3_spmd.clone, body=%wide.region_1.2_spmd.clone.sunk | while | flops 3612675 | bytes 9090036 | solution.py:137
  622.0 12.1 pad.346
  636.3 12.1 pad.272
  652.4 18.5 broadcast.458
  670.9 18.5 broadcast.458.clone.1
  691.9 321.1 %while.79 = (s32[]{:T(128)}, f32[42,16,768]{2,1,0:T(8,128)}, f32[28,42,768]{2,1,0:T(8,128)}, f32[28,42,16,768]{3,2,1,0:T(8,128)}, f32[28,42,16,768]{3,2,1,0:T(8,...) while((s32[]{:T(128)}, f32[42,16,768]{2,1,0:T(8,128)}, ...), condition=%wide.region_7.8_spmd, body=%wide.region_5.7_spmd.sunk | while | flops 3580418 | bytes 11618177 | solution.py:152
  1029.7 397.2 %while.81 = (s32[]{:T(128)}, f32[16,768]{1,0:T(8,128)S(1)}, f32[42,16,768]{2,1,0:T(8,128)}, f32[28,42,768]{2,1,0:T(8,128)}, f32[28,42,768]{2,1,0:T(8,128)}, /*in...) while((s32[]{:T(128)}, f32[16,768]{1,0:T(8,128)S(1)}, ...), condition=%wide.region_15.16_spmd.clone, body=%wide.region_9.15_spmd.clone.sunk | while | flops 9752260 | bytes 18794856 | solution.py:152
  1527.9 12.1 pad.230
  1540.0 7.5 pad.204
  1556.6 273.0 %while.82 = (s32[]{:T(128)}, f32[16,768]{1,0:T(8,128)S(1)}, f32[42,16,768]{2,1,0:T(8,128)}, f32[28,42,768]{2,1,0:T(8,128)}, f32[28,42,768]{2,1,0:T(8,128)}, /*in...) while((s32[]{:T(128)}, f32[16,768]{1,0:T(8,128)S(1)}, ...), condition=%wide.region_21.22_spmd.clone, body=%wide.region_16.21_spmd.clone.sunk | while | flops 7172452 | bytes 28728556 | solution.py:137
  1842.8 9.0 pad.242
  1851.8 8.1 pad.243
  1859.9 11.7 pad.231
  1888.4 7.2 fusion.105
  1898.8 15.2 fusion.102
  1919.9 19.2 rev.25
  1956.2 19.1 rev.23
  2045.1 10.7 all_to_all.29
  2060.4 42.6 %psum.28 = f32[2,768]{1,0:T(2,128)S(1)} all-reduce(f32[2,768]{1,0:T(2,128)S(1)} %maximum_multiply_fusion.1), channel_id=1, replica_groups=mesh['dir'=2,'wide'=16] {'wide'}, use_global_device_ids=true, to_apply=%region_27.28 | all-reduce | flops 1536 | bytes 12288 | tf_op jit(solution)/shard_map/psum | solution.py:266
  2122.0 11.8 all-to-all-done
  (1596 shorter events, 1520.3 us)
Async XLA Ops:
  7.2 239.2 %all-gather.4.cloned.1.call-start = ((), (), s32[]{:S(2)}) async-start(), calls=%async_computation.5 | async-start | bytes 1253376 | tf_op jit(solution)/shard_map/all_gather | solution.py:201
  8.8 346.6 %all-gather.6.cloned.1.call-start = ((), (), s32[]{:S(2)}) async-start(), calls=%async_computation.6 | async-start | bytes 2727936 | tf_op jit(solution)/shard_map/all_gather | solution.py:284
  22.1 55.1 %copy-start.72 = (f32[48,384]{1,0:T(8,128)S(1)}, f32[48,384]{1,0:T(8,128)}, u32[]{:S(2)}) copy-start(f32[48,384]{1,0:T(8,128)} %param.42) | copy-start | bytes 221188
  22.1 55.1 %copy-start.117 = (f32[1,7,48]{2,0,1:T(1,128)S(1)}, f32[1,7,48]{2,0,1:T(1,128)}, u32[]{:S(2)}) copy-start(f32[1,7,48]{2,0,1:T(1,128)} %param.57) | copy-start | bytes 4036
  22.1 55.2 %copy-start.82 = (f32[1,48,56]{2,1,0:T(8,128)S(1)}, f32[1,48,56]{2,1,0:T(8,128)}, u32[]{:S(2)}) copy-start(f32[1,48,56]{2,1,0:T(8,128)} %param.48) | copy-start | bytes 32260
  22.1 55.3 %copy-start.108 = (f32[1,16,48]{2,1,0:T(8,128)S(1)}, f32[1,16,48]{2,1,0:T(8,128)}, u32[]{:S(2)}) copy-start(f32[1,16,48]{2,1,0:T(8,128)} %param.54) | copy-start | bytes 9220
  26.4 216.6 %copy-start.50 = (bf16[1,588,384]{2,1,0:T(8,128)(2,1)S(1)}, bf16[1,588,384]{2,1,0:T(8,128)(2,1)}, u32[]{:S(2)}) copy-start(bf16[1,588,384]{2,1,0:T(8,128)(2,1)} %param.35) | copy-start | bytes 1354756
  29.6 216.8 %copy-start.90 = (f32[1176]{0:T(1024)}, f32[1176]{0:T(1024)S(1)}, u32[]{:S(2)}) copy-start(f32[1176]{0:T(1024)S(1)} %add_rsqrt_fusion) | copy-start | bytes 14116
  77.0 169.4 %copy-start.106 = (f32[384]{0:T(512)}, f32[384]{0:T(512)S(1)}, u32[]{:S(2)}) copy-start(f32[384]{0:T(512)S(1)} %convert_element_type.163) | copy-start | bytes 4612
  77.1 167.8 %copy-start.104 = (f32[588]{0:T(1024)}, f32[588]{0:T(1024)S(1)}, u32[]{:S(2)}) copy-start(f32[588]{0:T(1024)S(1)} %dynamic_slice.169) | copy-start | bytes 7060
  115.4 129.5 %copy-start.65 = (bf16[1,16,768]{2,1,0:T(8,128)(2,1)}, bf16[1,16,768]{2,1,0:T(8,128)(2,1)S(1)}, u32[]{:S(2)}) copy-start(bf16[1,16,768]{2,1,0:T(8,128)(2,1)S(1)} %copy.168) | copy-start | bytes 73732
  115.4 129.5 %copy-start.15 = (f32[1176,384]{1,0:T(8,128)S(1)}, f32[1176,384]{1,0:T(8,128)}, u32[]{:S(2)}) copy-start(f32[1176,384]{1,0:T(8,128)} %get-tuple-element.1329) | copy-start | bytes 5419012
  201.7 187.6 %copy-start.86 = (f32[1176]{0:T(1024)}, f32[1176]{0:T(1024)S(1)}, u32[]{:S(2)}) copy-start(f32[1176]{0:T(1024)S(1)} %get-tuple-element.1397) | copy-start | bytes 14116
  201.7 187.6 %copy-start.110 = (f32[1176]{0:T(1024)}, f32[1176]{0:T(1024)S(1)}, u32[]{:S(2)}) copy-start(f32[1176]{0:T(1024)S(1)} %get-tuple-element.1398) | copy-start | bytes 14116
  246.4 70.4 %copy-start.17 = (bf16[1176,384]{1,0:T(8,128)(2,1)}, bf16[1176,384]{1,0:T(8,128)(2,1)S(1)}, u32[]{:S(2)}) copy-start(bf16[1176,384]{1,0:T(8,128)(2,1)S(1)} %get-tuple-element.1326) | copy-start | bytes 2709508
  249.7 48.0 %copy-start.136 = (u32[32]{0:T(128)S(1)}, u32[32]{0:T(128)}, u32[]{:S(2)}) copy-start(u32[32]{0:T(128)} %constant.457) | copy-start | bytes 388
  251.2 1804.6 %all-reduce.65.cloned.1.call-start = ((), (), s32[]{:S(2)}) async-start(), calls=%async_computation.7 | async-start | bytes 3538944 | tf_op jit(solution)/shard_map/psum | solution.py:318
  316.8 72.6 %copy-start.96 = (f32[768]{0:T(1024)}, f32[768]{0:T(1024)S(1)}, u32[]{:S(2)}) copy-start(f32[768]{0:T(1024)S(1)} %get-tuple-element.1182) | copy-start | bytes 9220
  316.8 72.6 %copy-start.98 = (f32[768]{0:T(1024)}, f32[768]{0:T(1024)S(1)}, u32[]{:S(2)}) copy-start(f32[768]{0:T(1024)S(1)} %get-tuple-element.1181) | copy-start | bytes 9220
  316.8 72.6 %copy-start.100 = (f32[768]{0:T(1024)}, f32[768]{0:T(1024)S(1)}, u32[]{:S(2)}) copy-start(f32[768]{0:T(1024)S(1)} %get-tuple-element.1179) | copy-start | bytes 9220
  316.8 72.6 %copy-start.102 = (f32[768]{0:T(1024)}, f32[768]{0:T(1024)S(1)}, u32[]{:S(2)}) copy-start(f32[768]{0:T(1024)S(1)} %get-tuple-element.1180) | copy-start | bytes 9220
  424.4 145.3 %copy-start.53 = (f32[42,768]{1,0:T(8,128)}, f32[42,768]{1,0:T(8,128)S(1)}, u32[]{:S(2)}) copy-start(f32[42,768]{1,0:T(8,128)S(1)} %fusion.98) | copy-start | bytes 387076
  453.3 116.4 %copy-start.60 = (f32[16,768]{1,0:T(8,128)S(1)}, f32[16,768]{1,0:T(8,128)}, u32[]{:S(2)}) copy-start(f32[16,768]{1,0:T(8,128)} %get-tuple-element.1393) | copy-start | bytes 147460
  453.3 116.4 %copy-start.125 = (f32[42]{0:T(128)S(1)}, f32[42]{0:T(128)}, u32[]{:S(2)}) copy-start(f32[42]{0:T(128)} %reduce_min.9) | copy-start | bytes 508
  1983.2 7.8 collective-permute-start
  2014.4 3.1 collective-permute-start.1
  2023.4 10.6 all-to-all-start.2
  2034.1 11.0 all-to-all-start.4
  2037.6 66.0 %copy-start.16 = (f32[1176,384]{1,0:T(8,128)S(1)}, f32[1176,384]{1,0:T(8,128)}, u32[]{:S(2)}) copy-start(f32[1176,384]{1,0:T(8,128)} %get-tuple-element.1329) | copy-start | bytes 5419012
  2037.7 66.0 %copy-start.25 = (bf16[768,384]{1,0:T(8,128)(2,1)S(1)}, bf16[768,384]{1,0:T(8,128)(2,1)}, u32[]{:S(2)}) copy-start(bf16[768,384]{1,0:T(8,128)(2,1)} %copy-done.24) | copy-start | bytes 1769476
  2055.8 55.0 %all-to-all-start.1 = ((bf16[16,48,384]{2,1,0:T(8,128)(2,1)}), bf16[16,48,384]{2,1,0:T(8,128)(2,1)}, u32[]{:S(2)}, u32[]{:S(2)}) async-start(bf16[16,48,384]{2,1,0:T(8,128)(2,1)} %get-tuple-element.1281), calls=%async_computation.1 | async-start | bytes 1179648 | tf_op jit(solution)/shard_map/all_to_all | solution.py:30
  2110.8 22.9 %all-to-all-start = ((bf16[16,24,1536]{2,1,0:T(8,128)(2,1)}), bf16[16,24,1536]{2,1,0:T(8,128)(2,1)S(1)}, u32[]{:S(2)}, u32[]{:S(2)}) async-start(bf16[16,24,1536]{2,1,0:T(8,128)(2,1)} %get-tuple-element.1280), calls=%async_computation | async-start | bytes 2359296 | tf_op jit(solution)/shard_map/all_to_all | solution.py:30
  (173 other events, 1232.8 us)
Sparse Core Ops, SparseCore 0:
  11.4 58.9 all-gather.3
  251.3 6.0 all-gather.5
  2010.4 18.4 all-reduce.64
where the time goes:
time: 2180 us; the launch traced here: 2140 us
  local copies, waits for them, and re-layouts  1090 us (50%)
  other arithmetic  632 us (29%)
  blocking collectives  309 us (14%)
  matrix products  47.4 us (2%)
  waiting for transfers between devices  22 us (1%)
    squeeze x252, local copies, waits for them, and re-layouts, block_scan(): lax.scan(local_step, initial, (steps_now, driven, b_now, keep_now))  210 us
    dynamic_update_slice x56, other arithmetic, block_scan(): lax.scan(local_step, initial, (steps_now, driven, b_now, keep_now))  179 us
    reduce_sum x56, other arithmetic, advance(): step_row[:, None, :] * decay_rate[None]  149 us
    pad x33, local copies, waits for them, and re-layouts, block_scan(): _, reached = lax.associative_scan(combine, (through, block_ends))  145 us
    reduce_sum x56, other arithmetic, full_step(): return (carried, jnp.sum(inputs_now[4][:, :, None] * carried, 1))  132 us
    dynamic_update_slice x196, local copies, waits for them, and re-layouts, block_scan(): lax.scan(full_step, starts, (steps_now, driven, b_now, keep_now, c_now))  132 us
    squeeze x56, local copies, waits for them, and re-layouts, block_scan(): lax.scan(full_step, starts, (steps_now, driven, b_now, keep_now, c_now))  100 us
    rev x4, local copies, waits for them, and re-layouts, orient(): return jnp.where(stream == 1, jnp.flip(values, 0), values)  99 us
  transfers between devices with their start and end apart: 9, of which 4 were waited for; matrix products, arithmetic and copies ran while one was open for 6% of the time, Pallas kernels for 0%

commit v1 on v0

v1 whole, which is shorter than its diff:
```python
import functools
import math

import jax
import jax.numpy as jnp
from jax import lax
from jax.experimental import pallas as pl
from jax.experimental.pallas import tpu as pltpu
from jax.sharding import PartitionSpec as P

PATCHES = 196
STEP = 10
VIEW_TOK = 392
EPS_NORM = 1e-06
BETA_ONE = 0.9
BETA_TWO = 0.95
EPS_ADAM = 1e-08
RATES = (0.15, 0.1, 2.5, 0.12, 0.2, 1.0, 2.5)
DECAYS = (0.1, 0.1, 0.0, 0.1, 0.1, 0.0, 0.0)

F32 = jnp.float32
BF = jnp.bfloat16
LN2 = math.log(2.0)
LOG2E = 1.0 / LN2

SLOTS = 1176
R = 1184
NB = R // 16
NP = NB // 2
HALF = 588
WIN = 608
WBASE = 576
D = 384
E = 768
G6 = E // 128
N = 16
RANK = 24
HALO = 8
XR = HALO + R + HALO
RING = 4
CUT = 1e4
ROW_B, ROW_C, ROW_STEP, ROW_DECAY, ROW_CHAN, ROW_GAIN = 24, 40, 56, 80, 96, 103
NT = (((1,), (1,)), ((), ()))
TN = (((0,), (0,)), ((), ()))
VMEM = pl.BlockSpec(memory_space=pltpu.VMEM)
SMEM = pl.BlockSpec(memory_space=pltpu.SMEM)
ANY = pl.BlockSpec(memory_space=pl.ANY)


def dot(a, b):
    return jnp.dot(a, b, preferred_element_type=F32)


def dot_nt(a, b):
    return lax.dot_general(a, b, NT, preferred_element_type=F32)


def dot_tn(a, b):
    return lax.dot_general(a, b, TN, preferred_element_type=F32)


def sigmoid(v):
    return 0.5 * jnp.tanh(0.5 * v) + 0.5


def rows16(b, n=16):
    return pl.ds(pl.multiple_of(b * 16, 16), n)


def labels_of(meta, r):
    lab = jnp.full(r.shape, -1, jnp.int32)
    late = jnp.zeros(r.shape, jnp.int32)
    for k in range(3):
        start = meta[1 + k]
        inside = (r >= start) & (r < start + VIEW_TOK) & (k < meta[0])
        lab = jnp.where(inside, k, lab)
        late = jnp.where(inside, jnp.where(r >= start + PATCHES, 1, 0), late)
    lab = jnp.where(r < 0, -2, lab)
    lab = jnp.where(r >= SLOTS, -3, lab)
    return lab, late


def residual_tile(meta, tok, etab, base, n):
    r = base + lax.broadcasted_iota(jnp.int32, (n, 128), 0)
    lab, late = labels_of(meta, r)
    live = jnp.where(lab >= 0, 1.0, 0.0)
    out = []
    for c in range(3):
        cols = slice(c * 128, c * 128 + 128)
        emb = jnp.where(lab >= 0, etab[3:4, cols], 0.0)
        for k in range(3):
            emb = jnp.where((lab == k) & (late == 1), etab[k : k + 1, cols], emb)
        out.append(tok[:, cols].astype(F32) + emb)
    return out, live


def row_scale(res):
    total = sum(jnp.sum(v * v, axis=1, keepdims=True) for v in res)
    return lax.rsqrt(total * (1.0 / D) + EPS_NORM)


def fill_labels(meta, lab_ref):
    for base in range(0, XR, 8):
        r = base - HALO + lax.broadcasted_iota(jnp.int32, (8, 128), 0)
        lab_ref[base : base + 8, :] = labels_of(meta, r)[0]


def gain_row(st_ref, wide):
    per = E // wide
    own = D // wide
    i = lax.broadcasted_iota(jnp.int32, (E, D), 0)
    j = lax.broadcasted_iota(jnp.int32, (E, D), 1)
    pick = jnp.where(i == (j // own) * per + j % own, 1.0, 0.0).astype(BF)
    src = jnp.broadcast_to(st_ref[ROW_GAIN : ROW_GAIN + 1, :], (16, E)).astype(BF)
    return dot(src, pick)[0:8]


def fill_broadcast(p_ref, lane, out_ref):
    def body(sb, _):
        base = pl.multiple_of(sb * 128, 128)
        v = p_ref[pl.ds(base, 128), :].T[lane : lane + N]
        for j in range(128):
            out_ref[pl.ds(pl.multiple_of((base + j) * N, N), N), :] = (
                jnp.broadcast_to(v[:, j : j + 1], (N, 128))
            )
        return 0

    lax.fori_loop(0, 10, body, 0)


def conv_tile(x_ref, lab_ref, st_ref, c, base, n, rev):
    cols = slice(c * 128, c * 128 + 128)
    here = lab_ref[pl.ds(base + HALO, n), :]
    lagged = [x_ref[c, pl.ds(base + HALO, n), :]]
    for j in (1, 2, 3):
        at = base + HALO + (j if rev else -j)
        same = lab_ref[pl.ds(at, n), :] == here
        lagged.append(jnp.where(same, x_ref[c, pl.ds(at, n), :], 0.0))
    total = st_ref[ROW_CHAN + 4 : ROW_CHAN + 5, cols]
    for j in range(4):
        total = total + st_ref[ROW_CHAN + j : ROW_CHAN + j + 1, cols] * lagged[j]
    return total, lagged


def fwd_kernel(
    wide, meta, tok, etab, w1, s_ref,
    normed_o, x_o, act_o, al_o, dl_o, p_o, st_o, res_o, stats_o, hs_o,
    lab, dm, u, bb, cbd, hse, hso, gain_s, sem,
):
    stream = meta[4]
    st_o[...] = s_ref[...].astype(F32).T
    fill_labels(meta, lab)
    gain_s[...] = gain_row(st_o, wide)

    def norm_tile(i, _):
        base = pl.multiple_of(i * 32, 32)
        res, _l = residual_tile(meta, tok[pl.ds(base, 32), :], etab, base, 32)
        scale = row_scale(res)
        for c in range(3):
            cols = slice(c * 128, c * 128 + 128)
            normed_o[pl.ds(base, 32), cols] = (res[c] * scale * gain_s[0:1, cols]).astype(BF)
        return 0

    lax.fori_loop(0, R // 32, norm_tile, 0)
    x_o[:, 0:HALO, :] = jnp.zeros((G6, HALO, 128), F32)
    x_o[:, HALO + R : XR, :] = jnp.zeros((G6, HALO, 128), F32)
    for h in range(2):
        for c in range(0, G6, 2):
            y = dot(normed_o[h * 592 : h * 592 + 592, :], w1[:, c * 128 : c * 128 + 256])
            x_o[c, HALO + h * 592 : HALO + h * 592 + 592, :] = y[:, :128]
            x_o[c + 1, HALO + h * 592 : HALO + h * 592 + 592, :] = y[:, 128:]

    def conv(rev):
        def tile(i, _):
            base = pl.multiple_of(i * 32, 32)
            for c in range(G6):
                total, _l = conv_tile(x_o, lab, st_o, c, base, 32, rev)
                act = total * sigmoid(total)
                act_o[c, pl.ds(base, 32), :] = act
                al_o[pl.ds(base, 32), c * 128 : c * 128 + 128] = act.astype(BF)
            return 0

        lax.fori_loop(0, R // 32, tile, 0)

    @pl.when(stream == 0)
    def _():
        conv(False)

    @pl.when(stream == 1)
    def _():
        conv(True)

    p_o[R:, :] = jnp.zeros((1280 - R, 128), F32)
    col = lax.broadcasted_iota(jnp.int32, (128, 256), 1)
    row = lax.broadcasted_iota(jnp.int32, (128, 256), 0)
    spread_c = jnp.where(row == ROW_C + col % N, 1.0, 0.0).astype(BF)
    diag = (
        lax.broadcasted_iota(jnp.int32, (592, 256), 0) % N
        == lax.broadcasted_iota(jnp.int32, (592, 256), 1) // N
    )
    for h in range(2):
        rows = slice(h * 592, h * 592 + 592)
        proj = dot(al_o[rows, :], s_ref[...])
        p_o[rows, :] = proj
        low = proj.astype(BF)
        cbd[rows, :] = jnp.where(diag, dot(low, spread_c), 0.0).astype(BF)
        step_in = low[:, :RANK]
        for c in range(0, G6, 2):
            w = st_o[ROW_STEP : ROW_STEP + RANK, c * 128 : c * 128 + 256].astype(BF)
            y = dot(step_in, w)
            dl_o[c, rows, :] = y[:, :128]
            dl_o[c + 1, rows, :] = y[:, 128:]
    stats_o[...] = jnp.zeros(stats_o.shape, F32)

    def soft(rev):
        def tile(i, _):
            base = pl.multiple_of(i * 32, 32)
            here = lab[pl.ds(base + HALO, 32), :]
            before = lab[pl.ds(base + HALO + (1 if rev else -1), 32), :]
            cut = jnp.where(here == before, 0.0, CUT)
            live = jnp.where(here >= 0, 1.0, 0.0)
            real = jnp.where(here >= -1, 1.0, 0.0)
            for c in range(G6):
                cols = slice(c * 128, c * 128 + 128)
                rows = pl.ds(base, 32)
                v = dl_o[c, rows, :] + st_o[ROW_CHAN + 5 : ROW_CHAN + 6, cols]
                delta = jnp.maximum(v, 0.0) + jnp.log1p(jnp.exp(-jnp.abs(v)))
                dl_o[c, rows, :] = delta
                dm[c, rows, :] = delta + cut
                u[c, rows, :] = delta * act_o[c, rows, :] * real
                t1 = live * delta
                t2 = t1 * delta
                for s in range(4):
                    stats_o[0, :, cols] += t1[8 * s : 8 * s + 8]
                    stats_o[1, :, cols] += t2[8 * s : 8 * s + 8]
            return 0

        lax.fori_loop(0, R // 32, tile, 0)

    @pl.when(stream == 0)
    def _():
        soft(False)

    @pl.when(stream == 1)
    def _():
        soft(True)

    fill_broadcast(p_o, ROW_B, bb)
    hs = (hse, hso)

    def save(k, i):
        slot = i % RING
        return pltpu.make_async_copy(hs[k].at[slot], hs_o.at[k, i], sem.at[k, slot])

    def scan(rev):
        rate = [
            -jnp.exp(st_o[ROW_DECAY : ROW_DECAY + N, c * 128 : c * 128 + 128]) * LOG2E
            for c in range(G6)
        ]

        def block_of(t):
            return NB - 1 - t if rev else t

        def emit(t, k, slot, c):
            rows = rows16(block_of(t))
            y = dot(cbd[rows, :], hs[k][slot, :, c * 128 : c * 128 + 256])
            for h in range(2):
                cols = slice((c + h) * 128, (c + h) * 128 + 128)
                skip = st_o[ROW_CHAN + 6 : ROW_CHAN + 7, cols]
                res_o[rows, cols] = (
                    y[:, h * 128 : h * 128 + 128] + skip * act_o[c + h, rows, :]
                ).astype(BF)

        def block(t, k, slot, state, late):
            b = block_of(t)
            state = list(state)
            for n, j in enumerate(range(15, -1, -1) if rev else range(16)):
                if n % 4 == 0 and late:
                    late.pop(0)()
                q = b * 16 + j
                drive = bb[pl.ds(pl.multiple_of(q * N, N), N), :]
                for c in range(G6):
                    fade = jnp.exp2(dm[c, pl.ds(q, 1), :] * rate[c])
                    state[c] = fade * state[c] + u[c, pl.ds(q, 1), :] * drive
                    hs[k][slot, j * N : j * N + N, c * 128 : c * 128 + 128] = state[c].astype(BF)
            return tuple(state)

        def pair(i, state):
            slot = i % RING

            @pl.when(i >= RING)
            def _():
                save(0, i - RING).wait()
                save(1, i - RING).wait()

            before = jnp.maximum(2 * i - 1, 0)
            late = [
                functools.partial(emit, before, 1, jnp.maximum(i - 1, 0) % RING, c)
                for c in (0, 2, 4)
            ]
            state = block(2 * i, 0, slot, state, late)
            late = [functools.partial(emit, 2 * i, 0, slot, c) for c in (0, 2, 4)]
            state = block(2 * i + 1, 1, slot, state, late)
            save(0, i).start()
            save(1, i).start()
            return state

        hso[0] = jnp.zeros((256, E), BF)
        lax.fori_loop(0, NP, pair, tuple(jnp.zeros((N, 128), F32) for _ in range(G6)))
        for c in (0, 2, 4):
            emit(NB - 1, 1, (NP - 1) % RING, c)
        for i in range(NP - RING, NP):
            save(0, i).wait()
            save(1, i).wait()

    @pl.when(stream == 0)
    def _():
        scan(False)

    @pl.when(stream == 1)
    def _():
        scan(True)


def forward(wide, meta, tok, etab, w1, s):
    S = jax.ShapeDtypeStruct
    return pl.pallas_call(
        functools.partial(fwd_kernel, wide),
        out_shape=[
            S((R, D), BF), S((G6, XR, 128), F32), S((G6, R, 128), F32), S((R, E), BF),
            S((G6, R, 128), F32), S((1280, 128), F32), S((128, E), F32), S((R, E), BF),
            S((2, 8, E), F32), S((2, NP, 256, E), BF),
        ],
        in_specs=[SMEM] + [VMEM] * 4,
        out_specs=[VMEM] * 9 + [ANY],
        scratch_shapes=[
            pltpu.VMEM((XR, 128), jnp.int32),
            pltpu.VMEM((G6, R, 128), F32),
            pltpu.VMEM((G6, R, 128), F32),
            pltpu.VMEM((1280 * N, 128), F32),
            pltpu.VMEM((R, 256), BF),
            pltpu.VMEM((RING, 256, E), BF),
            pltpu.VMEM((RING, 256, E), BF),
            pltpu.VMEM((8, D), F32),
            pltpu.SemaphoreType.DMA((2, RING)),
        ],
        compiler_params=pltpu.CompilerParams(vmem_limit_bytes=60 * 2**20),
        name="forward",
    )(meta, tok, etab, w1, s)


def mid_kernel(
    meta, tok, etab, cot, normed, own, other, w2, wo,
    block_o, mg_o, gpart_o, gw2_o, gwo_o,
    cotw, gated, bgrad, ggrad, blk,
):
    stream = meta[4]
    wbase = pl.multiple_of(stream * WBASE, 32)
    cotw[...] = jnp.zeros(cotw.shape, F32)
    for s, off in ((0, 0), (1, WIN - HALF - 8)):

        @pl.when(stream == s)
        def _():
            cotw[off : off + HALF, :] = cot[...].astype(F32)

    win = pl.ds(wbase, WIN)

    def live_of(base, n):
        r = wbase + base + lax.broadcasted_iota(jnp.int32, (n, 128), 0)
        return jnp.where(labels_of(meta, r)[0] >= 0, 1.0, 0.0)

    def tile(i, _):
        base = pl.multiple_of(i * 32, 32)
        live = live_of(base, 32)
        for c in range(3):
            cols = slice(c * 128, c * 128 + 128)
            bgrad[pl.ds(base, 32), cols] = (live * cotw[pl.ds(base, 32), cols]).astype(BF)
        return 0

    lax.fori_loop(0, WIN // 32, tile, 0)
    for c in range(0, E, 256):
        cols = slice(c, c + 256)
        gate = dot(normed[win, :], w2[:, cols])
        mixed = own[:, cols].astype(F32) + other[:, cols].astype(F32)
        sig = sigmoid(gate)
        silu = gate * sig
        gated[:, cols] = (mixed * silu).astype(BF)
        up = dot_nt(bgrad[...], wo[cols, :])
        mg_o[:, cols] = (up * silu).astype(BF)
        ggrad[:, cols] = (up * mixed * sig * (1.0 + gate * (1.0 - sig))).astype(BF)
    for c in range(0, D, 128):
        cols = slice(c, c + 128)
        branch = dot(gated[...], wo[:, cols])
        blk[:, cols] = branch
        gpart_o[:, cols] = dot_nt(ggrad[...], w2[cols, :])
        gw2_o[cols, :] = dot_tn(normed[win, cols], ggrad[...])
    for c in range(0, E, 256):
        gwo_o[c : c + 256, :] = dot_tn(gated[:, c : c + 256], bgrad[...])

    def out_tile(i, _):
        base = pl.multiple_of(i * 32, 32)
        at = pl.multiple_of(wbase + base, 32)
        res, live = residual_tile(meta, tok[pl.ds(at, 32), :], etab, at, 32)
        for c in range(3):
            cols = slice(c * 128, c * 128 + 128)
            blk[pl.ds(base, 32), cols] = res[c] + live * blk[pl.ds(base, 32), cols]
        return 0

    lax.fori_loop(0, WIN // 32, out_tile, 0)
    for s, off in ((0, 0), (1, WIN - HALF - 8)):

        @pl.when(stream == s)
        def _():
            block_o[...] = blk[off : off + HALF, :]


def middle(meta, tok, etab, cot, normed, own, other, w2, wo):
    S = jax.ShapeDtypeStruct
    return pl.pallas_call(
        mid_kernel,
        out_shape=[
            S((HALF, D), F32), S((WIN, E), BF), S((WIN, D), F32), S((D, E), F32), S((E, D), F32),
        ],
        in_specs=[SMEM] + [VMEM] * 8,
        out_specs=[VMEM] * 5,
        scratch_shapes=[
            pltpu.VMEM((WIN, D), F32), pltpu.VMEM((WIN, E), BF), pltpu.VMEM((WIN, D), BF),
            pltpu.VMEM((WIN, E), BF), pltpu.VMEM((WIN, D), F32),
        ],
        compiler_params=pltpu.CompilerParams(vmem_limit_bytes=60 * 2**20),
        name="middle",
    )(meta, tok, etab, cot, normed, own, other, w2, wo)


def bwd_kernel(
    meta, normed, x, act, al, dl, p, st, mgo, mgx, w1, hs_in,
    npart_o, gw1_o, gs_o,
    lab, dm, dy, dyb, ub, bb, bbd, dbm, dcm, dd, zs, dacc, pgs, hse, hso, g0, g1, z0, z1, dc, sel, sums, sem,
):
    stream = meta[4]
    fill_labels(meta, lab)

    def lay(i, _):
        base = pl.multiple_of(i * 32, 32)
        for c in range(G6):
            cols = slice(c * 128, c * 128 + 128)
            lowrow = mgo[pl.ds(pl.multiple_of(jnp.minimum(base, WIN - 32), 32), 32), cols].astype(F32)
            hirow = mgx[pl.ds(pl.multiple_of(jnp.maximum(base - WBASE, 0), 32), 32), cols].astype(F32)
            v = jnp.where(base < WIN, lowrow, 0.0) + jnp.where(base >= WBASE, hirow, 0.0)
            dy[c, pl.ds(base, 32), :] = v
            dyb[pl.ds(base, 32), cols] = v.astype(BF)
        return 0

    lax.fori_loop(0, R // 32, lay, 0)
    sums[...] = jnp.zeros(sums.shape, F32)

    def prep(rev):
        def tile(i, _):
            base = pl.multiple_of(i * 32, 32)
            rows = pl.ds(base, 32)
            here = lab[pl.ds(base + HALO, 32), :]
            before = lab[pl.ds(base + HALO + (1 if rev else -1), 32), :]
            cut = jnp.where(here == before, 0.0, CUT)
            real = jnp.where(here >= -1, 1.0, 0.0)
            for c in range(G6):
                cols = slice(c * 128, c * 128 + 128)
                dm[c, rows, :] = dl[c, rows, :] + cut
                a = act[c, rows, :]
                ub[rows, cols] = (dl[c, rows, :] * a * real).astype(BF)
                t = dy[c, rows, :] * a
                sums[0, :, cols] += t[0:8] + t[8:16] + t[16:24] + t[24:32]
            return 0

        lax.fori_loop(0, R // 32, tile, 0)

    @pl.when(stream == 0)
    def _():
        prep(False)

    @pl.when(stream == 1)
    def _():
        prep(True)

    col = lax.broadcasted_iota(jnp.int32, (128, 256), 1)
    row = lax.broadcasted_iota(jnp.int32, (128, 256), 0)
    spread_b = jnp.where(row == ROW_B + col % N, 1.0, 0.0).astype(BF)
    diag = (
        lax.broadcasted_iota(jnp.int32, (592, 256), 0) % N
        == lax.broadcasted_iota(jnp.int32, (592, 256), 1) // N
    )
    for h in range(2):
        rows = slice(h * 592, h * 592 + 592)
        bbd[rows, :] = jnp.where(diag, dot(p[rows, :].astype(BF), spread_b), 0.0).astype(BF)
    fill_broadcast(p, ROW_C, bb)
    i = lax.broadcasted_iota(jnp.int32, (32, 256), 0)
    j = lax.broadcasted_iota(jnp.int32, (32, 256), 1)
    sel[...] = jnp.where(i == jnp.where(i < N, j // N, N + j % N), 1.0, 0.0).astype(BF)
    dacc[...] = jnp.zeros(dacc.shape, F32)
    hs, gs, zz = (hse, hso), (g0, g1), (z0, z1)

    def load(k, i):
        slot = i % RING
        return pltpu.make_async_copy(hs_in.at[k, i], hs[k].at[slot], sem.at[k, slot])

    def scan(rev):
        rate = [
            -jnp.exp(st[ROW_DECAY : ROW_DECAY + N, c * 128 : c * 128 + 128]) * LOG2E
            for c in range(G6)
        ]
        block_diag = (
            lax.broadcasted_iota(jnp.int32, (N, 256), 0)
            == lax.broadcasted_iota(jnp.int32, (N, 256), 1) // N
        )

        def block_of(t):
            return NB - 1 - t if rev else t

        def drive_dot(t, k, c):
            rows = rows16(block_of(t))
            y = dot(bbd[rows, :], gs[k][:, c * 128 : c * 128 + 256])
            dd[c, rows, :] = y[:, :128]
            dd[c + 1, rows, :] = y[:, 128:]

        def step_dot(t, k, c, first):
            rows = rows16(block_of(t))
            y = dot(sel[...], zz[k][:, c * 128 : c * 128 + 256])
            zs[c, rows, :] = y[:N, :128]
            zs[c + 1, rows, :] = y[:N, 128:]
            dacc[c] += jnp.where(first, 0.0, y[N:, :128])
            dacc[c + 1] += jnp.where(first, 0.0, y[N:, 128:])

        def b_dot(t, k):
            rows = rows16(block_of(t))
            dbm[rows, :] = jnp.where(block_diag, dot_nt(ub[rows, :], gs[k][...]), 0.0).astype(BF)

        def c_dot(t, k, slot):
            rows = rows16(block_of(t))
            dcm[rows, :] = jnp.where(block_diag, dot_nt(dyb[rows, :], hs[k][slot]), 0.0).astype(BF)

        def block(t, k, slot, pslot, carry, late):
            b = block_of(t)
            carry = list(carry)
            late = list(late)
            for n, j in enumerate(range(16) if rev else range(15, -1, -1)):
                if n % 2 == 0 and late:
                    late.pop(0)()
                q = b * 16 + j
                cb = bb[pl.ds(pl.multiple_of(q * N, N), N), :]
                jp = j + 1 if rev else j - 1
                if 0 <= jp < 16:
                    old_ref, old_slot = hs[k], slot
                else:
                    jp = 0 if rev else 15
                    old_ref, old_slot = hs[1 - k], pslot
                for c in range(G6):
                    cols = slice(c * 128, c * 128 + 128)
                    w = dm[c, pl.ds(q, 1), :] * rate[c]
                    fade = jnp.exp2(w)
                    g = cb * dy[c, pl.ds(q, 1), :] + carry[c]
                    carry[c] = fade * g
                    old = old_ref[old_slot, jp * N : jp * N + N, cols]
                    gs[k][j * N : j * N + N, cols] = g.astype(BF)
                    zz[k][j * N : j * N + N, cols] = (w * carry[c]).astype(BF) * old
            return tuple(carry)

        def pair(ii, carry):
            i = NP - 1 - ii
            slot = i % RING
            pslot = jnp.maximum(i - 1, 0) % RING

            @pl.when(i >= 1)
            def _():
                load(0, i - 1).wait()
                load(1, i - 1).wait()

            @pl.when(i >= 3)
            def _():
                load(0, i - 3).start()
                load(1, i - 3).start()

            one = 1 + (i >> 20)
            for k in (1, 0):
                t = 2 * i + k
                after = jnp.minimum(t + 1, NB - 1)
                first = t + 1 > NB - 1
                late = [functools.partial(drive_dot, after, 1 - k, c) for c in (0, 2, 4)]
                late += [functools.partial(step_dot, after, 1 - k, c, first) for c in (0, 2, 4)]
                late += [functools.partial(b_dot, after, 1 - k), functools.partial(c_dot, t, k, slot)]
                ps = slot if k == 1 else pslot
                carry = lax.fori_loop(
                    0, one, lambda _, cc, t=t, k=k, ps=ps, late=late: block(t, k, slot, ps, cc, late), carry
                )
            return carry

        for i in range(NP - 1, NP - 4, -1):
            load(0, i).start()
            load(1, i).start()
        load(0, NP - 1).wait()
        load(1, NP - 1).wait()
        g0[...] = jnp.zeros((256, E), BF)
        z0[...] = jnp.zeros((256, E), BF)
        lax.fori_loop(0, NP, pair, tuple(jnp.zeros((N, 128), F32) for _ in range(G6)))
        for c in (0, 2, 4):
            drive_dot(0, 0, c)
            step_dot(0, 0, c, False)
        b_dot(0, 0)

    @pl.when(stream == 0)
    def _():
        scan(False)

    @pl.when(stream == 1)
    def _():
        scan(True)

    def step_tile(i, _):
        base = pl.multiple_of(i * 32, 32)
        rows = pl.ds(base, 32)
        for c in range(G6):
            cols = slice(c * 128, c * 128 + 128)
            delta, a, d = dl[c, rows, :], act[c, rows, :], dd[c, rows, :]
            near = 1.0 - delta * (0.5 - delta * (1.0 / 6.0 - delta * (1.0 / 24.0)))
            ratio = jnp.where(delta < 0.03, near, (1.0 - jnp.exp(-delta)) / delta)
            pre = ratio * (zs[c, rows, :] * LN2 + a * d * delta)
            ub[rows, cols] = pre.astype(BF)
            dm[c, rows, :] = delta * d + st[ROW_CHAN + 6 : ROW_CHAN + 7, cols] * dy[c, rows, :]
            sums[1, :, cols] += pre[0:8] + pre[8:16] + pre[16:24] + pre[24:32]
        return 0

    lax.fori_loop(0, R // 32, step_tile, 0)
    w_step = st[ROW_STEP : ROW_STEP + RANK, :].astype(BF)
    w_b = jnp.concatenate([st[ROW_B : ROW_B + N, :]] * N, 0).astype(BF)
    w_c = jnp.concatenate([st[ROW_C : ROW_C + N, :]] * N, 0).astype(BF)
    w_s = st[0:RANK, :].astype(BF)
    for h in range(2):
        rows = slice(h * 592, h * 592 + 592)
        sg = dot_nt(ub[rows, :], w_step).astype(BF)
        pgs[rows, :] = jnp.concatenate([sg, jnp.zeros((592, 128 - RANK), BF)], 1)
        for c in range(0, G6, 2):
            cols = slice(c * 128, c * 128 + 256)
            y = dot(sg, w_s[:, cols]) + dot(dbm[rows, :], w_b[:, cols]) + dot(dcm[rows, :], w_c[:, cols])
            dm[c, rows, :] += y[:, :128]
            dm[c + 1, rows, :] += y[:, 128:]
    dc[:, 0:HALO, :] = jnp.zeros((G6, HALO, 128), F32)
    dc[:, HALO + R : XR, :] = jnp.zeros((G6, HALO, 128), F32)

    def conv(rev):
        def first(i, _):
            base = pl.multiple_of(i * 32, 32)
            for c in range(G6):
                cols = slice(c * 128, c * 128 + 128)
                total, lagged = conv_tile(x, lab, st, c, base, 32, rev)
                sig = sigmoid(total)
                v = dm[c, pl.ds(base, 32), :] * sig * (1.0 + total * (1.0 - sig))
                dc[c, pl.ds(base + HALO, 32), :] = v
                sums[2, :, cols] += v[0:8] + v[8:16] + v[16:24] + v[24:32]
                for j in range(4):
                    t = v * lagged[j]
                    sums[3 + j, :, cols] += t[0:8] + t[8:16] + t[16:24] + t[24:32]
            return 0

        def second(i, _):
            base = pl.multiple_of(i * 32, 32)
            here = lab[pl.ds(base + HALO, 32), :]
            for c in range(G6):
                cols = slice(c * 128, c * 128 + 128)
                v = dc[c, pl.ds(base + HALO, 32), :] * st[ROW_CHAN : ROW_CHAN + 1, cols]
                for j in (1, 2, 3):
                    at = base + HALO + (-j if rev else j)
                    same = lab[pl.ds(at, 32), :] == here
                    later = jnp.where(same, dc[c, pl.ds(at, 32), :], 0.0)
                    v = v + later * st[ROW_CHAN + j : ROW_CHAN + j + 1, cols]
                dyb[pl.ds(base, 32), cols] = v.astype(BF)
            return 0

        lax.fori_loop(0, R // 32, first, 0)
        lax.fori_loop(0, R // 32, second, 0)

    @pl.when(stream == 0)
    def _():
        conv(False)

    @pl.when(stream == 1)
    def _():
        conv(True)

    for h in range(2):
        rows = slice(h * 592, h * 592 + 592)
        npart_o[rows, :] = dot_nt(dyb[rows, :], w1[...])
    for c in range(0, D, 128):
        gw1_o[c : c + 128, :] = dot_tn(normed[:, c : c + 128], dyb[...])
    top = dot_tn(pgs[...], al[...])
    gb = dot_tn(dbm[...], al[...])
    gc = dot_tn(dcm[...], al[...])
    gb = sum(gb[k * N : k * N + N] for k in range(N))
    gc = sum(gc[k * N : k * N + N] for k in range(N))
    low = p[0:R, :].astype(BF)
    gstep = dot_tn(low, ub[...])[0:RANK]
    gdecay = jnp.concatenate([dacc[c] for c in range(G6)], 1) * LN2

    def total(k):
        return jnp.sum(sums[k], axis=0, keepdims=True)

    chan = [total(3 + k) for k in range(4)] + [total(2), total(1), total(0)]
    chan = jnp.concatenate(chan + [jnp.zeros((1, E), F32)], 0)
    gt = jnp.concatenate(
        [top[0:RANK], gb, gc, gstep, gdecay, chan, jnp.zeros((128 - 104, E), F32)], 0
    )
    gs_o[...] = gt.T


def backward(meta, normed, x, act, al, dl, p, st, mgo, mgx, w1, hs):
    S = jax.ShapeDtypeStruct
    big = pltpu.VMEM((G6, R, 128), F32)
    return pl.pallas_call(
        bwd_kernel,
        out_shape=[S((R, D), F32), S((D, E), F32), S((E, 128), F32)],
        in_specs=[SMEM] + [VMEM] * 10 + [ANY],
        out_specs=[VMEM] * 3,
        scratch_shapes=[
            pltpu.VMEM((XR, 128), jnp.int32), big, big,
            pltpu.VMEM((R, E), BF), pltpu.VMEM((R, E), BF),
            pltpu.VMEM((1280 * N, 128), F32),
            pltpu.VMEM((R, 256), BF), pltpu.VMEM((R, 256), BF), pltpu.VMEM((R, 256), BF),
            big, big, pltpu.VMEM((G6, N, 128), F32), pltpu.VMEM((R, 128), BF),
            pltpu.VMEM((RING, 256, E), BF), pltpu.VMEM((RING, 256, E), BF),
            pltpu.VMEM((256, E), BF), pltpu.VMEM((256, E), BF),
            pltpu.VMEM((256, E), BF), pltpu.VMEM((256, E), BF),
            pltpu.VMEM((G6, XR, 128), F32), pltpu.VMEM((32, 256), BF),
            pltpu.VMEM((7, 8, E), F32),
            pltpu.SemaphoreType.DMA((2, RING)),
        ],
        compiler_params=pltpu.CompilerParams(vmem_limit_bytes=63 * 2**20),
        name="backward",
    )(meta, normed, x, act, al, dl, p, st, mgo, mgx, w1, hs)


def end_kernel(wide, meta, tok, etab, cot, npart, other, gpart, st, tg_o, gg_o, cotw, out, gain_s, acc):
    stream = meta[4]
    wbase = pl.multiple_of(stream * WBASE, 32)
    gain_s[...] = gain_row(st, wide)
    acc[...] = jnp.zeros(acc.shape, F32)
    cotw[...] = jnp.zeros(cotw.shape, F32)
    for s, off in ((0, 0), (1, WIN - HALF - 8)):

        @pl.when(stream == s)
        def _():
            cotw[off : off + HALF, :] = cot[...].astype(F32)

    lo = stream * HALF

    def tile(i, _):
        base = pl.multiple_of(i * 32, 32)
        at = pl.multiple_of(wbase + base, 32)
        res, _l = residual_tile(meta, tok[pl.ds(at, 32), :], etab, at, 32)
        scale = row_scale(res)
        r = at + lax.broadcasted_iota(jnp.int32, (32, 128), 0)
        mine = (r >= lo) & (r < lo + HALF)
        ng, un = [], []
        for c in range(3):
            cols = slice(c * 128, c * 128 + 128)
            v = npart[pl.ds(at, 32), cols] + other[pl.ds(base, 32), cols].astype(F32) + gpart[pl.ds(base, 32), cols]
            unit = res[c] * scale
            t = jnp.where(mine, v * unit, 0.0)
            acc[:, cols] += t[0:8] + t[8:16] + t[16:24] + t[24:32]
            ng.append(v * gain_s[0:1, cols])
            un.append(unit)
        mean = sum(jnp.sum(a * b, axis=1, keepdims=True) for a, b in zip(ng, un)) * (1.0 / D)
        for c in range(3):
            cols = slice(c * 128, c * 128 + 128)
            out[pl.ds(base, 32), cols] = cotw[pl.ds(base, 32), cols] + scale * (ng[c] - un[c] * mean)
        return 0

    lax.fori_loop(0, WIN // 32, tile, 0)
    gg_o[...] = acc[...]
    for s, off in ((0, 0), (1, WIN - HALF - 8)):

        @pl.when(stream == s)
        def _():
            tg_o[...] = out[off : off + HALF, :]


def ending(wide, meta, tok, etab, cot, npart, other, gpart, st):
    S = jax.ShapeDtypeStruct
    return pl.pallas_call(
        functools.partial(end_kernel, wide),
        out_shape=[S((HALF, D), F32), S((8, D), F32)],
        in_specs=[SMEM] + [VMEM] * 7,
        out_specs=[VMEM] * 2,
        scratch_shapes=[
            pltpu.VMEM((WIN, D), F32), pltpu.VMEM((WIN, D), F32), pltpu.VMEM((8, D), F32), pltpu.VMEM((8, D), F32),
        ],
        compiler_params=pltpu.CompilerParams(vmem_limit_bytes=60 * 2**20),
        name="ending",
    )(meta, tok, etab, cot, npart, other, gpart, st)


def adam_step(weight, gradient, first_moment, second, step_rate, decay_rate):
    first_moment = BETA_ONE * first_moment + (1.0 - BETA_ONE) * gradient
    second = BETA_TWO * second + (1.0 - BETA_TWO) * gradient * gradient
    first_hat = first_moment / (1.0 - BETA_ONE**STEP)
    second_hat = second / (1.0 - BETA_TWO**STEP)
    weight = weight - step_rate * (
        first_hat / (jnp.sqrt(second_hat) + EPS_ADAM) + decay_rate * weight
    )
    return (weight, first_moment, second)


def sum_at_owner(array, axis):
    n = lax.axis_size(axis)
    blocks = array.reshape(n, array.shape[0] // n, *array.shape[1:])
    arrived = lax.all_to_all(blocks, axis, split_axis=0, concat_axis=0, tiled=True)
    return arrived.astype(F32).sum(axis=0)


def swap(array):
    return lax.ppermute(array, "dir", [(0, 1), (1, 0)])


def local(
    tokens, cotangent, view_counts, view_strides, view_offsets,
    in_proj, in_first, in_second, out_proj, out_first, out_second,
    norm_gain, gain_first, gain_second, state_proj, state_first, state_second,
    step_proj, step_first, step_second, log_decay, decay_first, decay_second,
    channels, chan_first, chan_second,
):
    stream = lax.axis_index("dir")
    wide = lax.axis_size("wide")
    rows = state_proj.shape[1]
    own_gain = norm_gain.shape[0]
    gain_col = jnp.concatenate([norm_gain, jnp.zeros((rows - own_gain,), F32)])[:, None]
    small = jnp.concatenate(
        [
            state_proj[0], step_proj[0].T, log_decay[0].T, channels[0].T, gain_col,
            jnp.zeros((rows, 128 - ROW_GAIN - 1), F32),
        ],
        1,
    ).astype(BF)
    w_in = lax.all_gather(in_proj.astype(BF), "wide", axis=0, tiled=True)
    w_out = lax.all_gather(out_proj.astype(BF), "wide", axis=0, tiled=True)
    s = lax.all_gather(small, "wide", axis=0, tiled=True)
    w1, w2 = w_in[:, :E], w_in[:, E:]

    meta = jnp.concatenate(
        [view_counts, view_offsets[0], stream[None].astype(jnp.int32), jnp.zeros((3,), jnp.int32)]
    )
    half = D // 2
    freq = jnp.exp(-math.log(10000.0) * jnp.arange(half, dtype=F32) / half)
    angles = view_strides[0].astype(F32)[:, None] * freq[None, :]
    etab = jnp.concatenate([jnp.sin(angles), jnp.cos(angles)], 1)
    rest = jnp.concatenate([jnp.zeros((1, half), F32), jnp.ones((1, half), F32)], 1)
    etab = jnp.concatenate([etab, rest, jnp.zeros((4, D), F32)], 0)
    tok = jnp.pad(tokens[0], ((0, R - SLOTS), (0, 0)))
    cot = cotangent[0]

    normed, x, act, al, dl, p, st, res, stats, hs = forward(wide, meta, tok, etab, w1, s)
    mine = lax.dynamic_slice_in_dim(res, stream * WBASE, WIN, 0)
    other = swap(lax.dynamic_slice_in_dim(res, (1 - stream) * WBASE, WIN, 0))
    block, mg, gpart, gw2, gwo = middle(meta, tok, etab, cot, normed, mine, other, w2, w_out)
    mgx = swap(mg)
    mg0 = jnp.where(stream == 0, mg, mgx)
    mg1 = jnp.where(stream == 0, mgx, mg)
    npart, gw1, gs = backward(meta, normed, x, act, al, dl, p, st, mg0, mg1, w1, hs)
    other = swap(lax.dynamic_slice_in_dim(npart, (1 - stream) * WBASE, WIN, 0).astype(BF))
    token_grad, gg = ending(wide, meta, tok, etab, cot, npart, other, gpart, st)

    gin = jnp.concatenate([gw1, gw2], 1)
    gin, gwo, gg = (
        lax.psum(gin.astype(BF), "dir"),
        lax.psum(gwo.astype(BF), "dir"),
        lax.psum(gg.sum(0).astype(BF), "dir"),
    )
    shard_in = sum_at_owner(gin, "wide")
    shard_out = sum_at_owner(gwo, "wide")
    shard_gain = sum_at_owner(gg, "wide")
    shard_small = sum_at_owner(gs.astype(BF), "wide")
    small_t = shard_small.T
    stats = stats.sum(1) / VIEW_TOK
    stats = sum_at_owner(stats.T, "wide").T

    outs = []
    for w, g, f, s2, k in (
        (in_proj, shard_in, in_first, in_second, 0),
        (out_proj, shard_out, out_first, out_second, 1),
        (norm_gain, shard_gain, gain_first, gain_second, 2),
        (state_proj, shard_small[None, :, : ROW_STEP], state_first, state_second, 3),
        (step_proj, small_t[None, ROW_STEP:ROW_DECAY], step_first, step_second, 4),
        (log_decay, small_t[None, ROW_DECAY:ROW_CHAN], decay_first, decay_second, 5),
        (channels, small_t[None, ROW_CHAN:ROW_GAIN], chan_first, chan_second, 6),
    ):
        outs += adam_step(w, g, f, s2, RATES[k], DECAYS[k])
    return (block[None], token_grad[None], stats[None], *outs)


def solution(mesh):
    row, col = P("wide", None), P("dir", None, "wide")
    mat = P("dir", "wide", None)
    weights = [row] * 6 + [P("wide")] * 3 + [mat] * 3 + [col] * 9
    return jax.shard_map(
        local,
        mesh=mesh,
        in_specs=(
            P("wide", None, None), P("wide", "dir", None), P("wide"), row, row, *weights,
        ),
        out_specs=(P("wide", "dir", None), P("wide", "dir", None), col, *weights),
        check_vma=False,
    )
```

time: 2180 us -> 359 us (0.16); the launches traced: 2140 us -> 358 us
  local copies, waits for them, and re-layouts: 1090 us -> 20.5 us
  other arithmetic: 632 us -> 17.4 us
  blocking collectives: 309 us -> 127 us
  Pallas kernels: 0 us -> 135 us
  matrix products: 47.4 us -> 0 us
    reduce_sum x123 -> x7, other arithmetic: 314 us -> 1.73 us  [the longest x5 0.9 us: sum_at_owner(): return arrived.astype(F32).sum(axis=0)]
    squeeze x308 -> x0, local copies, waits for them, and re-layouts: 310 us -> none  [the longest x252 210 us: block_scan(): lax.scan(local_step, initial, (steps_now, driven, b_now, keep_now))]
    dynamic_update_slice x56 -> x0, other arithmetic: 179 us -> none  [block_scan(): lax.scan(local_step, initial, (steps_now, driven, b_now, keep_now))]
    pad x33 -> x1, local copies, waits for them, and re-layouts: 145 us -> 2.21 us  [local(): tok = jnp.pad(tokens[0], ((0, R - SLOTS), (0, 0)))]
    mul x196 -> x0, local copies, waits for them, and re-layouts: 138 us -> none  [the longest x112 77.6 us: advance(): return factor * carried + drive_row[:, None, :] * b_row[:, :, None]]
    dynamic_update_slice x197 -> x0, local copies, waits for them, and re-layouts: 136 us -> none  [the longest x196 132 us: block_scan(): lax.scan(full_step, starts, (steps_now, driven, b_now, keep_now, c_now))]
    pallas_call x0 -> x4, Pallas kernels: none -> 135 us  [the longest x1 70.8 us: backward(): pl.pallas_call(bwd_kernel, out_shape=[S((R, D), F32), S((D, E), F32), S((...]
    all_gather x5 -> x2, blocking collectives: 200 us -> 90.7 us  [the longest x1 46.5 us: local(): s = lax.all_gather(small, 'wide', axis=0, tiled=True)]
  transfers between devices with their start and end apart: 9 -> 8, of which waited for: 4 -> 4; matrix products, arithmetic and copies ran while one was open for 6% -> 7% of each run, Pallas kernels for 0% -> 2%
where the time goes in v1:
time: 359 us; the launch traced here: 358 us
  Pallas kernels  135 us (38%)
  blocking collectives  127 us (35%)
  waiting for transfers between devices  29.7 us (8%)
  local copies, waits for them, and re-layouts  20.5 us (6%)
  other arithmetic  17.4 us (5%)
  between operations  15.1 us (4%)
  starting transfers between devices  13.6 us (4%)
    pallas_call x1, Pallas kernels, backward(): pl.pallas_call(bwd_kernel, out_shape=[S((R, D), F32), S((D, E), F32), S((...  70.8 us
    all_gather x1, blocking collectives, local(): s = lax.all_gather(small, 'wide', axis=0, tiled=True)  46.5 us
    pallas_call x1, Pallas kernels, forward(): pl.pallas_call(functools.partial(fwd_kernel, wide), out_shape=[S((R, D),...  45.8 us
    all_gather x1, blocking collectives, local(): w_out = lax.all_gather(out_proj.astype(BF), 'wide', axis=0, tiled=True)  44.2 us
    all_to_all x2, blocking collectives, sum_at_owner(): lax.all_to_all(blocks, axis, split_axis=0, concat_axis=0, tiled=True)  34.2 us
    all_to_all x3, waiting for transfers between devices, sum_at_owner(): lax.all_to_all(blocks, axis, split_axis=0, concat_axis=0, tiled=True)  21.6 us
    all_to_all x3, starting transfers between devices, sum_at_owner(): lax.all_to_all(blocks, axis, split_axis=0, concat_axis=0, tiled=True)  11.1 us
    unnamed x70, local copies, waits for them, and re-layouts  10.9 us
  transfers between devices with their start and end apart: 8, of which 4 were waited for; matrix products, arithmetic and copies ran while one was open for 7% of the time, Pallas kernels for 2%

profile of v1, /device:TPU:0, one launch (start us, length us, event | category | flops | bytes accessed | tf_op | source)
XLA Modules:
  0.0 358.1 jit_solution(12242141297462703597)
XLA Ops:
  7.3 1.6 convert_element_type.47
  10.3 0.8 copy.145
  12.8 2.2 pad.6.tok
  15.1 46.5 %all_gather.10.s_ref = bf16[768,128]{1,0:T(8,128)(2,1)} all-gather(bf16[48,128]{1,0:T(8,128)(2,1)S(1)} %concatenate.24), channel_id=1, replica_groups=mesh['dir'=2,'wide'=16] {'wide'}, dimensions={0}, use_global_device_ids=true | all-gather | bytes 208896 | tf_op jit(solution)/shard_map/all_gather | solution.py:841
  63.0 7.6 %all-gather.2.cloned.1.call-done = bf16[384,1536]{1,0:T(8,128)(2,1)} async-done(((bf16[24,1536]{1,0:T(8,128)(2,1)}), bf16[384,1536]{1,0:T(8,128)(2,1)}) %all-gather.2.cloned.1.call-update) | async-done | bytes 1179664 | tf_op jit(solution)/shard_map/all_gather | solution.py:839
  70.6 2.3 fusion.20
  72.9 45.8 %forward.1 = (bf16[1184,384]{1,0:T(8,128)(2,1)}, f32[6,1200,128]{2,1,0:T(8,128)}, f32[6,1184,128]{2,1,0:T(8,128)}, bf16[1184,768]{1,0:T(8,128)(2,1)}, f32[6,1184...) custom-call(s32[8]{0:T(128)} %pad_add_fusion.meta, ...), custom_call_target="tpu_custom_call" | custom-call | tf_op jit(solution)/shard_map/forward/pallas_call | solution.py:327
  118.7 2.6 constant_dynamic-slice_fusion
  121.3 2.2 collective-permute-start
  123.6 44.2 %all_gather.11.wo = bf16[768,384]{1,0:T(8,128)(2,1)} all-gather(bf16[48,384]{1,0:T(8,128)(2,1)S(1)} %convert_element_type.48), channel_id=1, replica_groups=mesh['dir'=2,'wide'=16] {'wide'}, dimensions={0}, use_global_device_ids=true | all-gather | bytes 626688 | tf_op jit(solution)/shard_map/all_gather | solution.py:840
  167.8 0.9 copy-done.2
  168.7 10.2 %middle.1 = (f32[588,384]{1,0:T(8,128)}, bf16[608,768]{1,0:T(8,128)(2,1)}, f32[608,384]{1,0:T(8,128)}, f32[384,768]{1,0:T(8,128)}, f32[768,384]{1,0:T(8,128)}) custom-call(s32[8]{0:T(128)} %pad_add_fusion.meta, bf16[1184,384]{1,0:T(8,128)(2,1)} %pad.6.tok, f32[8,384]{1,0:T(8,128)} %maximum_maximum_fusion.etab, bf16[588,384]{1,0:T(8,128)(2,1)} %bitcast.72, ...), custom_call_target="tpu_custom_call" | custom-call | tf_op jit(solution)/shard_map/middle/pallas_call | solution.py:419
  179.0 1.5 convert.39
  180.5 0.9 convert_element_type.51
  181.8 2.6 broadcast_select_fusion
  184.4 70.8 %backward.1 = (f32[1184,384]{1,0:T(8,128)}, f32[384,768]{1,0:T(8,128)}, f32[768,128]{1,0:T(8,128)}) custom-call(s32[8]{0:T(128)} %pad_add_fusion.meta, bf16[1184,384]{1,0:T(8,128)(2,1)} %get-tuple-element.44.normed, f32[6,1200,128]{2,1,0:T(8,128)} %get-tuple-element.47.x, f32[6,1184,128]{2,1,0:T(8,128)} %get-tuple-element.48.act, ...), custom_call_target="tpu_custom_call" | custom-call | tf_op jit(solution)/shard_map/backward/pallas_call | solution.py:715
  255.2 1.3 convert.38
  256.5 1.1 pad_maximum_fusion
  257.7 1.3 dynamic-slice_convert_fusion
  259.8 3.5 all-to-all-start
  264.0 6.6 %all-to-all-done = f32[16,48,2]{1,2,0:T(2,128)S(1)} async-done(((f32[16,48,2]{1,2,0:T(2,128)}), f32[16,48,2]{1,2,0:T(2,128)S(1)}, u32[]{:S(2)}, u32[]{:S(2)}) %all-to-all-start) | async-done | bytes 6176 | tf_op jit(solution)/shard_map/all_to_all | solution.py:812
  270.6 3.5 all-to-all-start.4
  274.9 7.8 %ending.1 = (f32[588,384]{1,0:T(8,128)}, f32[8,384]{1,0:T(8,128)}) custom-call(s32[8]{0:T(128)} %pad_add_fusion.meta, bf16[1184,384]{1,0:T(8,128)(2,1)} %pad.6.tok, f32[8,384]{1,0:T(8,128)} %maximum_maximum_fusion.etab, bf16[588,384]{1,0:T(8,128)(2,1)} %bitcast.73, f32[1184,384]{1,0:T(8,128)} %get-tuple-element.55.npart, bf16[608,384]{1,0:T(8,128)(2,1)} %copy-done.5, ...), custom_call_target="tpu_custom_call" | custom-call | tf_op jit(solution)/shard_map/ending/pallas_call | solution.py:785
  282.7 0.8 reduce_sum.67
  283.6 2.5 psum.23
  286.1 13.9 %all_to_all.29 = bf16[16,1,24]{2,1,0:T(2,128)(2,1)S(1)} all-to-all(bf16[16,1,24]{2,1,0:T(2,128)(2,1)S(1)} %copy.150), channel_id=1, replica_groups=mesh['dir'=2,'wide'=16] {'wide'}, dimensions={0} | all-to-all | bytes 1536 | tf_op jit(solution)/shard_map/all_to_all | solution.py:812
  300.0 20.2 %all_to_all.30 = bf16[16,48,384]{2,1,0:T(8,128)(2,1)S(1)} all-to-all(bf16[16,48,384]{2,1,0:T(8,128)(2,1)} %get-tuple-element.185), channel_id=1, replica_groups=mesh['dir'=2,'wide'=16] {'wide'}, dimensions={0} | all-to-all | bytes 1179648 | tf_op jit(solution)/shard_map/all_to_all | solution.py:812
  320.3 4.1 %all-to-all-start.1 = ((bf16[16,24,1536]{2,1,0:T(8,128)(2,1)}), bf16[16,24,1536]{2,1,0:T(8,128)(2,1)S(1)}, u32[]{:S(2)}, u32[]{:S(2)}) async-start(bf16[16,24,1536]{2,1,0:T(8,128)(2,1)} %get-tuple-element.184), calls=%async_computation.1 | async-start | bytes 2359296 | tf_op jit(solution)/shard_map/all_to_all | solution.py:812
  325.0 1.8 copy.156
  330.7 3.1 copy.157
  335.2 15.0 %all-to-all-done.1 = bf16[16,24,1536]{2,1,0:T(8,128)(2,1)S(1)} async-done(((bf16[16,24,1536]{2,1,0:T(8,128)(2,1)}), bf16[16,24,1536]{2,1,0:T(8,128)(2,1)S(1)}, u32[]{:S(2)}, u32[]{:S(2)}) %all-to-all-start.1) | async-done | bytes 1179680 | tf_op jit(solution)/shard_map/all_to_all | solution.py:812
  350.4 0.8 multiply_subtract_fusion
  (111 shorter events, 13.0 us)
Async XLA Ops:
  7.2 55.1 %copy-start.25 = (f32[1,384]{1,0:T(1,128)S(1)}, f32[1,384]{1,0:T(1,128)}, u32[]{:S(2)}) copy-start(f32[1,384]{1,0:T(1,128)} %constant.27.clone.1) | copy-start | bytes 4612
  7.2 7.8 %copy-start.10 = (f32[1,48,56]{2,1,0:T(8,128)S(1)}, f32[1,48,56]{2,1,0:T(8,128)}, u32[]{:S(2)}) copy-start(f32[1,48,56]{2,1,0:T(8,128)} %param.40) | copy-start | bytes 32260
  7.2 54.4 %copy-start.26 = (s32[1,3]{1,0:T(1,128)S(1)}, s32[1,3]{1,0:T(1,128)}, u32[]{:S(2)}) copy-start(s32[1,3]{1,0:T(1,128)} %param.30) | copy-start | bytes 40
  7.2 55.0 %copy-start.30 = (s32[1,3]{1,0:T(1,128)S(1)}, s32[1,3]{1,0:T(1,128)}, u32[]{:S(2)}) copy-start(s32[1,3]{1,0:T(1,128)} %param.29) | copy-start | bytes 40
  7.2 63.4 %all-gather.2.cloned.1.call-start = ((), (), s32[]{:S(2)}) async-start(), calls=%async_computation.5 | async-start | bytes 1253376 | tf_op jit(solution)/shard_map/all_gather | solution.py:839
  8.9 291.2 %all-reduce.5.cloned.1.call-start = ((), (), s32[]{:S(2)}) async-start(), calls=%async_computation.6 | async-start | bytes 3538944 | tf_op jit(solution)/shard_map/psum | solution.py:869
  121.3 46.4 %collective-permute-start = (bf16[608,768]{1,0:T(8,128)(2,1)S(1)}, bf16[608,768]{1,0:T(8,128)(2,1)S(1)}, u32[]{:S(2)}, u32[]{:S(2)}) collective-permute-start(bf16[608,768]{1,0:T(8,128)(2,1)S(1)} %get-tuple-element.209), channel_id=1, source_target_pairs={{0,16},{16,0},{1,17},{17,1},{2,18},{18,2},{3,19},{19,3},{4,20},{20... | collective-permute-start | bytes 2801672 | tf_op jit(solution)/shard_map/ppermute | solution.py:817
  178.9 2.9 collective-permute-start.1
  259.0 15.1 %collective-permute-start.2 = (bf16[608,384]{1,0:T(8,128)(2,1)S(1)}, bf16[608,384]{1,0:T(8,128)(2,1)S(1)}, u32[]{:S(2)}, u32[]{:S(2)}) collective-permute-start(bf16[608,384]{1,0:T(8,128)(2,1)S(1)} %dynamic-slice_convert_fusion), channel_id=1, source_target_pairs={{0,16},{16,0},{1,17},{17,1},{2,18},{18,2},{3,19},{19,3},{4,20},{20... | collective-permute-start | bytes 1400840 | tf_op jit(solution)/shard_map/ppermute | solution.py:817
  259.8 10.8 %all-to-all-start = ((f32[16,48,2]{1,2,0:T(2,128)}), f32[16,48,2]{1,2,0:T(2,128)S(1)}, u32[]{:S(2)}, u32[]{:S(2)}) async-start(f32[16,48,2]{1,2,0:T(2,128)} %copy.149), calls=%async_computation | async-start | bytes 32768 | tf_op jit(solution)/shard_map/all_to_all | solution.py:812
  270.6 15.5 %all-to-all-start.4 = ((bf16[16,48,128]{2,1,0:T(8,128)(2,1)}), bf16[16,48,128]{2,1,0:T(8,128)(2,1)S(1)}, u32[]{:S(2)}, u32[]{:S(2)}) async-start(bf16[16,48,128]{2,1,0:T(8,128)(2,1)} %bitcast.20), calls=%async_computation.4 | async-start | bytes 393216 | tf_op jit(solution)/shard_map/all_to_all | solution.py:812
  282.7 42.3 %copy-start.3 = (f32[588,384]{1,0:T(8,128)S(1)}, f32[588,384]{1,0:T(8,128)}, u32[]{:S(2)}) copy-start(f32[588,384]{1,0:T(8,128)} %get-tuple-element.46) | copy-start | bytes 2709508
  320.2 6.8 %copy-start.18 = (f32[1,7,48]{2,0,1:T(1,128)S(1)}, f32[1,7,48]{2,0,1:T(1,128)}, u32[]{:S(2)}) copy-start(f32[1,7,48]{2,0,1:T(1,128)} %param.49) | copy-start | bytes 4036
  320.2 6.8 %copy-start.23 = (f32[1,7,48]{2,0,1:T(1,128)S(1)}, f32[1,7,48]{2,0,1:T(1,128)}, u32[]{:S(2)}) copy-start(f32[1,7,48]{2,0,1:T(1,128)} %param.50) | copy-start | bytes 4036
  320.2 6.8 %copy-start.24 = (f32[1,7,48]{2,0,1:T(1,128)S(1)}, f32[1,7,48]{2,0,1:T(1,128)}, u32[]{:S(2)}) copy-start(f32[1,7,48]{2,0,1:T(1,128)} %param.51) | copy-start | bytes 4036
  320.2 8.6 %copy-start.15 = (f32[1,16,48]{2,1,0:T(8,128)S(1)}, f32[1,16,48]{2,1,0:T(8,128)}, u32[]{:S(2)}) copy-start(f32[1,16,48]{2,1,0:T(8,128)} %param.46) | copy-start | bytes 9220
  320.2 8.6 %copy-start.21 = (f32[1,16,48]{2,1,0:T(8,128)S(1)}, f32[1,16,48]{2,1,0:T(8,128)}, u32[]{:S(2)}) copy-start(f32[1,16,48]{2,1,0:T(8,128)} %param.47) | copy-start | bytes 9220
  320.3 8.5 %copy-start.22 = (f32[1,16,48]{2,1,0:T(8,128)S(1)}, f32[1,16,48]{2,1,0:T(8,128)}, u32[]{:S(2)}) copy-start(f32[1,16,48]{2,1,0:T(8,128)} %param.48) | copy-start | bytes 9220
  320.3 9.2 %copy-start.14 = (f32[1,24,48]{2,1,0:T(8,128)S(1)}, f32[1,24,48]{2,1,0:T(8,128)}, u32[]{:S(2)}) copy-start(f32[1,24,48]{2,1,0:T(8,128)} %param.43) | copy-start | bytes 13828
  320.3 9.1 %copy-start.19 = (f32[1,24,48]{2,1,0:T(8,128)S(1)}, f32[1,24,48]{2,1,0:T(8,128)}, u32[]{:S(2)}) copy-start(f32[1,24,48]{2,1,0:T(8,128)} %param.44) | copy-start | bytes 13828
  320.3 9.1 %copy-start.20 = (f32[1,24,48]{2,1,0:T(8,128)S(1)}, f32[1,24,48]{2,1,0:T(8,128)}, u32[]{:S(2)}) copy-start(f32[1,24,48]{2,1,0:T(8,128)} %param.45) | copy-start | bytes 13828
  320.3 9.8 %copy-start.16 = (f32[1,48,56]{2,1,0:T(8,128)S(1)}, f32[1,48,56]{2,1,0:T(8,128)}, u32[]{:S(2)}) copy-start(f32[1,48,56]{2,1,0:T(8,128)} %param.41) | copy-start | bytes 32260
  320.3 9.8 %copy-start.17 = (f32[1,48,56]{2,1,0:T(8,128)S(1)}, f32[1,48,56]{2,1,0:T(8,128)}, u32[]{:S(2)}) copy-start(f32[1,48,56]{2,1,0:T(8,128)} %param.42) | copy-start | bytes 32260
  320.3 29.9 %all-to-all-start.1 = ((bf16[16,24,1536]{2,1,0:T(8,128)(2,1)}), bf16[16,24,1536]{2,1,0:T(8,128)(2,1)S(1)}, u32[]{:S(2)}, u32[]{:S(2)}) async-start(bf16[16,24,1536]{2,1,0:T(8,128)(2,1)} %get-tuple-element.184), calls=%async_computation.1 | async-start | bytes 2359296 | tf_op jit(solution)/shard_map/all_to_all | solution.py:812
  325.0 8.8 %copy-start.27 = (f32[24]{0:T(128)S(1)}, f32[24]{0:T(128)}, u32[]{:S(2)}) copy-start(f32[24]{0:T(128)} %param.37) | copy-start | bytes 292
  325.0 8.8 %copy-start.28 = (f32[24]{0:T(128)S(1)}, f32[24]{0:T(128)}, u32[]{:S(2)}) copy-start(f32[24]{0:T(128)} %param.38) | copy-start | bytes 292
  325.0 8.8 %copy-start.29 = (f32[24]{0:T(128)S(1)}, f32[24]{0:T(128)}, u32[]{:S(2)}) copy-start(f32[24]{0:T(128)} %param.39) | copy-start | bytes 292
  326.9 7.6 %copy-start.11 = (f32[48,384]{1,0:T(8,128)S(1)}, f32[48,384]{1,0:T(8,128)}, u32[]{:S(2)}) copy-start(f32[48,384]{1,0:T(8,128)} %param.35) | copy-start | bytes 221188
  326.9 7.6 %copy-start.12 = (f32[48,384]{1,0:T(8,128)S(1)}, f32[48,384]{1,0:T(8,128)}, u32[]{:S(2)}) copy-start(f32[48,384]{1,0:T(8,128)} %param.36) | copy-start | bytes 221188
  330.7 19.7 %copy-start.4 = (f32[24,1536]{1,0:T(8,128)S(1)}, f32[24,1536]{1,0:T(8,128)}, u32[]{:S(2)}) copy-start(f32[24,1536]{1,0:T(8,128)} %param.31) | copy-start | bytes 442372
  330.7 19.7 %copy-start.8 = (f32[24,1536]{1,0:T(8,128)S(1)}, f32[24,1536]{1,0:T(8,128)}, u32[]{:S(2)}) copy-start(f32[24,1536]{1,0:T(8,128)} %param.32) | copy-start | bytes 442372
  330.7 19.7 %copy-start.9 = (f32[24,1536]{1,0:T(8,128)S(1)}, f32[24,1536]{1,0:T(8,128)}, u32[]{:S(2)}) copy-start(f32[24,1536]{1,0:T(8,128)} %param.33) | copy-start | bytes 442372
  (7 other events, 17.9 us)
Sparse Core Ops, SparseCore 0:
  11.4 59.1 all-gather.1
  257.8 16.6 all-reduce.4

commit v2 on v1

--- a/solution.py
+++ b/solution.py
@@ -39,7 +39,9 @@
 XR = HALO + R + HALO
 RING = 4
 CUT = 1e4
-ROW_B, ROW_C, ROW_STEP, ROW_DECAY, ROW_CHAN, ROW_GAIN = 24, 40, 56, 80, 96, 103
+SENDS = WIN // 32
+MESH = pl.DeviceIdType.MESH
+ROW_B, ROW_C, ROW_STEP, ROW_DECAY, ROW_CHAN, ROW_GAIN, ROW_STATS = 24, 40, 56, 80, 96, 103, 104
 NT = (((1,), (1,)), ((), ()))
 TN = (((0,), (0,)), ((), ()))
 VMEM = pl.BlockSpec(memory_space=pltpu.VMEM)
@@ -90,8 +92,14 @@
         emb = jnp.where(lab >= 0, etab[3:4, cols], 0.0)
         for k in range(3):
             emb = jnp.where((lab == k) & (late == 1), etab[k : k + 1, cols], emb)
-        out.append(tok[:, cols].astype(F32) + emb)
+        out.append(tok[c, pl.ds(base, n), :] + emb)
     return out, live
+
+
+def lay_tokens(tok, tokf):
+    for c in range(3):
+        tokf[c, 0:SLOTS, :] = tok[:, c * 128 : c * 128 + 128].astype(F32)
+        tokf[c, SLOTS:R, :] = jnp.zeros((R - SLOTS, 128), F32)
 
 
 def row_scale(res):
@@ -116,16 +124,19 @@
 
 
 def fill_broadcast(p_ref, lane, out_ref):
-    def body(sb, _):
-        base = pl.multiple_of(sb * 128, 128)
+    def spread(base, n):
         v = p_ref[pl.ds(base, 128), :].T[lane : lane + N]
-        for j in range(128):
+        for j in range(n):
             out_ref[pl.ds(pl.multiple_of((base + j) * N, N), N), :] = (
                 jnp.broadcast_to(v[:, j : j + 1], (N, 128))
             )
+
+    def body(sb, _):
+        spread(pl.multiple_of(sb * 128, 128), 128)
         return 0
 
-    lax.fori_loop(0, 10, body, 0)
+    lax.fori_loop(0, R // 128, body, 0)
+    spread(R // 128 * 128, R % 128)
 
 
 def conv_tile(x_ref, lab_ref, st_ref, c, base, n, rev):
@@ -142,19 +153,51 @@
     return total, lagged
 
 
+def views(count, offset, stream):
+    return [count[0], offset[0, 0], offset[0, 1], offset[0, 2], stream]
+
+
+def fill_embedding(stride, etab):
+    lane = lax.broadcasted_iota(jnp.int32, (8, D), 1)
+    row = lax.broadcasted_iota(jnp.int32, (8, D), 0)
+    half = D // 2
+    j = jnp.where(lane < half, lane, lane - half).astype(F32)
+    freq = jnp.exp(-math.log(10000.0) * j / half)
+    clock = jnp.zeros((8, D), F32)
+    for k in range(3):
+        clock = jnp.where(row == k, stride[0, k].astype(F32), clock)
+    angle = clock * freq
+    etab[...] = jnp.where(lane < half, jnp.sin(angle), jnp.cos(angle))
+
+
 def fwd_kernel(
-    wide, meta, tok, etab, w1, s_ref,
-    normed_o, x_o, act_o, al_o, dl_o, p_o, st_o, res_o, stats_o, hs_o,
-    lab, dm, u, bb, cbd, hse, hso, gain_s, sem,
+    wide, count, offset, stride, tok, w1, s_ref,
+    normed_h, x_h, act_h, dl_h, p_h, st_h, res_h, other_h, stats_o, hs_o,
+    normed_o, x_o, act_o, dl_o, p_o, st_o, res_o, other_o, al_o,
+    lab, dm, u, bb, cbd, hse, hso, gain_s, tokf, etab, sem, out_sem, send, recv,
 ):
-    stream = meta[4]
+    stream, place = lax.axis_index("dir"), lax.axis_index("wide")
+    bar = pltpu.get_barrier_semaphore()
+    pl.semaphore_signal(bar, inc=1, device_id=(1 - stream, place), device_id_type=MESH)
+    meta = views(count, offset, stream)
+    fill_embedding(stride, etab)
+    lay_tokens(tok, tokf)
     st_o[...] = s_ref[...].astype(F32).T
     fill_labels(meta, lab)
     gain_s[...] = gain_row(st_o, wide)
+    saves = [
+        pltpu.make_async_copy(v, h, out_sem.at[k])
+        for k, (v, h) in enumerate(
+            zip(
+                (normed_o, x_o, act_o, dl_o, p_o, st_o, res_o, other_o),
+                (normed_h, x_h, act_h, dl_h, p_h, st_h, res_h, other_h),
+            )
+        )
+    ]
 
     def norm_tile(i, _):
         base = pl.multiple_of(i * 32, 32)
-        res, _l = residual_tile(meta, tok[pl.ds(base, 32), :], etab, base, 32)
+        res, _l = residual_tile(meta, tokf, etab, base, 32)
         scale = row_scale(res)
         for c in range(3):
             cols = slice(c * 128, c * 128 + 128)
@@ -245,12 +288,23 @@
     def _():
         soft(True)
 
+    for c in saves[:6]:
+        c.start()
     fill_broadcast(p_o, ROW_B, bb)
     hs = (hse, hso)
 
     def save(k, i):
         slot = i % RING
         return pltpu.make_async_copy(hs[k].at[slot], hs_o.at[k, i], sem.at[k, slot])
+
+    def give(i, rev):
+        row = pl.multiple_of((NP - 1 - i if rev else i) * 32, 32)
+        at = pl.multiple_of(row if rev else row - WBASE, 32)
+        k = i - (NP - SENDS)
+        return pltpu.make_async_remote_copy(
+            src_ref=res_o.at[pl.ds(row, 32), :], dst_ref=other_o.at[pl.ds(at, 32), :],
+            send_sem=send.at[k], recv_sem=recv.at[k], device_id=(1 - stream, place), device_id_type=MESH,
+        )
 
     def scan(rev):
         rate = [
@@ -303,16 +357,30 @@
             state = block(2 * i + 1, 1, slot, state, late)
             save(0, i).start()
             save(1, i).start()
+
+            @pl.when(i > NP - SENDS)
+            def _():
+                give(i - 1, rev).start()
+
             return state
 
         hso[0] = jnp.zeros((256, E), BF)
         lax.fori_loop(0, NP, pair, tuple(jnp.zeros((N, 128), F32) for _ in range(G6)))
         for c in (0, 2, 4):
             emit(NB - 1, 1, (NP - 1) % RING, c)
+        give(NP - 1, rev).start()
         for i in range(NP - RING, NP):
             save(0, i).wait()
             save(1, i).wait()
 
+        def settle(i, _):
+            give(i, rev).wait()
+            return 0
+
+        lax.fori_loop(NP - SENDS, NP, settle, 0)
+
+    pl.semaphore_wait(bar, 1)
+
     @pl.when(stream == 0)
     def _():
         scan(False)
@@ -321,137 +389,233 @@
     def _():
         scan(True)
 
-
-def forward(wide, meta, tok, etab, w1, s):
+    for c in saves[6:]:
+        c.start()
+    for c in saves:
+        c.wait()
+
+
+def forward(wide, count, offset, stride, tok, w1, s):
     S = jax.ShapeDtypeStruct
+    kept = [
+        ((R, D), BF), ((G6, XR, 128), F32), ((G6, R, 128), F32), ((G6, R, 128), F32),
+        ((1280, 128), F32), ((128, E), F32), ((R, E), BF), ((WIN, E), BF),
+    ]
     return pl.pallas_call(
         functools.partial(fwd_kernel, wide),
-        out_shape=[
-            S((R, D), BF), S((G6, XR, 128), F32), S((G6, R, 128), F32), S((R, E), BF),
-            S((G6, R, 128), F32), S((1280, 128), F32), S((128, E), F32), S((R, E), BF),
-            S((2, 8, E), F32), S((2, NP, 256, E), BF),
-        ],
-        in_specs=[SMEM] + [VMEM] * 4,
-        out_specs=[VMEM] * 9 + [ANY],
-        scratch_shapes=[
+        out_shape=[S(*k) for k in kept] + [S((2, 8, E), F32), S((2, NP, 256, E), BF)],
+        in_specs=[SMEM] * 3 + [VMEM] * 3,
+        out_specs=[ANY] * 8 + [VMEM, ANY],
+        scratch_shapes=[pltpu.VMEM(*k) for k in kept]
+        + [
+            pltpu.VMEM((R, E), BF),
             pltpu.VMEM((XR, 128), jnp.int32),
             pltpu.VMEM((G6, R, 128), F32),
             pltpu.VMEM((G6, R, 128), F32),
-            pltpu.VMEM((1280 * N, 128), F32),
+            pltpu.VMEM((R * N, 128), F32),
             pltpu.VMEM((R, 256), BF),
             pltpu.VMEM((RING, 256, E), BF),
             pltpu.VMEM((RING, 256, E), BF),
             pltpu.VMEM((8, D), F32),
+            pltpu.VMEM((3, R, 128), F32),
+            pltpu.VMEM((8, D), F32),
             pltpu.SemaphoreType.DMA((2, RING)),
+            pltpu.SemaphoreType.DMA((8,)),
+            pltpu.SemaphoreType.DMA((SENDS,)),
+            pltpu.SemaphoreType.DMA((SENDS,)),
         ],
-        compiler_params=pltpu.CompilerParams(vmem_limit_bytes=60 * 2**20),
+        compiler_params=pltpu.CompilerParams(
+            vmem_limit_bytes=60 * 2**20, collective_id=3, has_side_effects=True
+        ),
+        cost_estimate=pl.CostEstimate(flops=int(5e10), bytes_accessed=1 << 20, transcendentals=0),
         name="forward",
-    )(meta, tok, etab, w1, s)
-
-
-def mid_kernel(
-    meta, tok, etab, cot, normed, own, other, w2, wo,
-    block_o, mg_o, gpart_o, gw2_o, gwo_o,
-    cotw, gated, bgrad, ggrad, blk,
-):
+    )(count, offset, stride, tok, w1, s)
+
+
+def middle(meta, wide, tokf, etab, cot, normed, own, other, w2, wo, cotw, gated, bgrad, ggrad, blk, mg, gpart, stage, g2, block_o, sent, shared):
     stream = meta[4]
     wbase = pl.multiple_of(stream * WBASE, 32)
-    cotw[...] = jnp.zeros(cotw.shape, F32)
-    for s, off in ((0, 0), (1, WIN - HALF - 8)):
-
-        @pl.when(stream == s)
-        def _():
-            cotw[off : off + HALF, :] = cot[...].astype(F32)
-
+    lay_cotangent(stream, cot, cotw)
     win = pl.ds(wbase, WIN)
-
-    def live_of(base, n):
-        r = wbase + base + lax.broadcasted_iota(jnp.int32, (n, 128), 0)
-        return jnp.where(labels_of(meta, r)[0] >= 0, 1.0, 0.0)
 
     def tile(i, _):
         base = pl.multiple_of(i * 32, 32)
-        live = live_of(base, 32)
+        r = wbase + base + lax.broadcasted_iota(jnp.int32, (32, 128), 0)
+        live = jnp.where(labels_of(meta, r)[0] >= 0, 1.0, 0.0)
         for c in range(3):
-            cols = slice(c * 128, c * 128 + 128)
-            bgrad[pl.ds(base, 32), cols] = (live * cotw[pl.ds(base, 32), cols]).astype(BF)
+            v = live * cotw[c, pl.ds(base, 32), :]
+            ref, col = (bgrad[0], c * 128) if c < 2 else (bgrad[1], 0)
+            ref[pl.ds(base, 32), col : col + 128] = v.astype(BF)
         return 0
 
     lax.fori_loop(0, WIN // 32, tile, 0)
+
+    def branch_grad():
+        return jnp.concatenate([bgrad[0][0:WIN, :], bgrad[1][0:WIN, 0:128]], 1)
+
     for c in range(0, E, 256):
         cols = slice(c, c + 256)
         gate = dot(normed[win, :], w2[:, cols])
         mixed = own[:, cols].astype(F32) + other[:, cols].astype(F32)
         sig = sigmoid(gate)
         silu = gate * sig
-        gated[:, cols] = (mixed * silu).astype(BF)
-        up = dot_nt(bgrad[...], wo[cols, :])
-        mg_o[:, cols] = (up * silu).astype(BF)
-        ggrad[:, cols] = (up * mixed * sig * (1.0 + gate * (1.0 - sig))).astype(BF)
+        gated[0:WIN, cols] = (mixed * silu).astype(BF)
+        up = dot_nt(branch_grad(), wo[cols, :])
+        mg[:, cols] = (up * silu).astype(BF)
+        ggrad[0:WIN, cols] = (up * mixed * sig * (1.0 + gate * (1.0 - sig))).astype(BF)
+        sent(c // 256).start()
+    drow, erow = D // wide, E // wide
+    rows = 2 * drow
+    pitch = -(-rows // 8) * 8
+    for c in range(0, D, 128):
+        g = dot_tn(normed[win, c : c + 128], ggrad[0:WIN, :])
+        lay_rows(g, c, drow, lambda k, r, v: put(stage, pitch, k, r, 0, v))
+    for c in range(0, E, 256):
+        g = dot_tn(gated[0:WIN, c : c + 256], branch_grad())
+        half = erow // 2
+        lay_rows(g, c, half, lambda k, r, v: put(stage, pitch, k // 2, drow + r, (k % 2) * D, v))
+    for k in range(wide):
+        for c in range(G6):
+            at = (k * G6 + c) * pitch
+            g2[k, :, c * 128 : c * 128 + 128] = stage[at : at + rows, :].astype(BF)
+    shared()
     for c in range(0, D, 128):
         cols = slice(c, c + 128)
-        branch = dot(gated[...], wo[:, cols])
-        blk[:, cols] = branch
-        gpart_o[:, cols] = dot_nt(ggrad[...], w2[cols, :])
-        gw2_o[cols, :] = dot_tn(normed[win, cols], ggrad[...])
-    for c in range(0, E, 256):
-        gwo_o[c : c + 256, :] = dot_tn(gated[:, c : c + 256], bgrad[...])
+        blk[c // 128, 0:WIN, :] = dot(gated[0:WIN, :], wo[:, cols])
+        gpart[:, cols] = dot_nt(ggrad[0:WIN, :], w2[cols, :])
 
     def out_tile(i, _):
         base = pl.multiple_of(i * 32, 32)
         at = pl.multiple_of(wbase + base, 32)
-        res, live = residual_tile(meta, tok[pl.ds(at, 32), :], etab, at, 32)
+        res, live = residual_tile(meta, tokf, etab, at, 32)
         for c in range(3):
-            cols = slice(c * 128, c * 128 + 128)
-            blk[pl.ds(base, 32), cols] = res[c] + live * blk[pl.ds(base, 32), cols]
+            blk[c, pl.ds(base, 32), :] = res[c] + live * blk[c, pl.ds(base, 32), :]
         return 0
 
     lax.fori_loop(0, WIN // 32, out_tile, 0)
-    for s, off in ((0, 0), (1, WIN - HALF - 8)):
+    take_half(stream, blk, block_o)
+
+
+WINDOWS = ((0, 0), (1, WIN - HALF - 8))
+
+
+def lay_cotangent(stream, cot, cotw):
+    cotw[:, 0:WIN, :] = jnp.zeros((3, WIN, 128), F32)
+    for s, off in WINDOWS:
 
         @pl.when(stream == s)
         def _():
-            block_o[...] = blk[off : off + HALF, :]
-
-
-def middle(meta, tok, etab, cot, normed, own, other, w2, wo):
-    S = jax.ShapeDtypeStruct
-    return pl.pallas_call(
-        mid_kernel,
-        out_shape=[
-            S((HALF, D), F32), S((WIN, E), BF), S((WIN, D), F32), S((D, E), F32), S((E, D), F32),
-        ],
-        in_specs=[SMEM] + [VMEM] * 8,
-        out_specs=[VMEM] * 5,
-        scratch_shapes=[
-            pltpu.VMEM((WIN, D), F32), pltpu.VMEM((WIN, E), BF), pltpu.VMEM((WIN, D), BF),
-            pltpu.VMEM((WIN, E), BF), pltpu.VMEM((WIN, D), F32),
-        ],
-        compiler_params=pltpu.CompilerParams(vmem_limit_bytes=60 * 2**20),
-        name="middle",
-    )(meta, tok, etab, cot, normed, own, other, w2, wo)
+            for c in range(3):
+                cotw[c, off : off + HALF, :] = cot[:, c * 128 : c * 128 + 128].astype(F32)
+
+
+def take_half(stream, src, out):
+    for s, off in WINDOWS:
+
+        @pl.when(stream == s)
+        def _():
+            for c in range(3):
+                out[:, c * 128 : c * 128 + 128] = src[c, off : off + HALF, :]
+
+
+def put(ref, pitch, k, r, col, v):
+    for c in range(0, v.shape[1], 128):
+        at = (k * G6 + (col + c) // 128) * pitch + r
+        ref[at : at + v.shape[0], :] = v[:, c : c + 128]
+
+
+def lay_rows(v, start, size, store):
+    at = 0
+    while at < v.shape[0]:
+        k, r = divmod(start + at, size)
+        n = min(size - r, v.shape[0] - at)
+        store(k, r, v[at : at + n])
+        at += n
+
+
+def unpack(pack, w2, wo, wide):
+    drow, half = D // wide, E // wide // 2
+    per = max(1, 16 // math.gcd(16, drow))
+    for k in range(0, wide, per):
+        v = [pack[k + i].astype(F32) for i in range(per)]
+        w2[k * drow : (k + per) * drow, :] = jnp.concatenate([t[0:drow] for t in v], 0).astype(BF)
+        pieces = []
+        for t in v:
+            pieces += [t[drow : drow + half, 0:D], t[drow : drow + half, D : 2 * D]]
+        wo[2 * k * half : 2 * (k + per) * half, :] = jnp.concatenate(pieces, 0).astype(BF)
 
 
 def bwd_kernel(
-    meta, normed, x, act, al, dl, p, st, mgo, mgx, w1, hs_in,
-    npart_o, gw1_o, gs_o,
-    lab, dm, dy, dyb, ub, bb, bbd, dbm, dcm, dd, zs, dacc, pgs, hse, hso, g0, g1, z0, z1, dc, sel, sums, sem,
+    wide, count, offset, stride, tok, cot, normed, own, other, pack, stats, w1, st,
+    x_h, act_h, dl_h, p_h, hs_in,
+    block_o, tg_o, gw1_o, gs_o, gg_o, g2_o, g2x_o,
+    x, act, dl, p, w2, wo, gpart, mg, mgx, g2s, g2r, nrecv,
+    lab, dm, dy, dyb, ub, bb, bbd, dbm, dcm, dd, zs, dacc, hse, hso, g0, g1, z0, z1, sel, sums,
+    etab, gain_s, acc, sem, in_sem, mgsend, mgrecv, g2send, g2recv, swsend, swrecv,
 ):
-    stream = meta[4]
+    stream, place = lax.axis_index("dir"), lax.axis_index("wide")
+    loads = [
+        pltpu.make_async_copy(h, v, in_sem.at[k])
+        for k, (h, v) in enumerate(zip((x_h, act_h, dl_h, p_h), (x, act, dl, p)))
+    ]
+    for c in loads:
+        c.start()
+    greet(stream, place, wide)
+    meta = views(count, offset, stream)
+    wbase = pl.multiple_of(stream * WBASE, 32)
+    partner = dict(device_id=(1 - stream, place), device_id_type=MESH)
+    fill_embedding(stride, etab)
     fill_labels(meta, lab)
-
-    def lay(i, _):
-        base = pl.multiple_of(i * 32, 32)
-        for c in range(G6):
-            cols = slice(c * 128, c * 128 + 128)
-            lowrow = mgo[pl.ds(pl.multiple_of(jnp.minimum(base, WIN - 32), 32), 32), cols].astype(F32)
-            hirow = mgx[pl.ds(pl.multiple_of(jnp.maximum(base - WBASE, 0), 32), 32), cols].astype(F32)
-            v = jnp.where(base < WIN, lowrow, 0.0) + jnp.where(base >= WBASE, hirow, 0.0)
-            dy[c, pl.ds(base, 32), :] = v
-            dyb[pl.ds(base, 32), cols] = v.astype(BF)
-        return 0
-
-    lax.fori_loop(0, R // 32, lay, 0)
+    tokf, cotw, blk = zs.at[0:3], zs.at[3:6], dd.at[0:3]
+    lay_tokens(tok, tokf)
+    unpack(pack, w2, wo, wide)
+
+    def sent(k):
+        cols = slice(k * 256, k * 256 + 256)
+        return pltpu.make_async_remote_copy(
+            src_ref=mg.at[:, cols], dst_ref=mgx.at[:, cols], send_sem=mgsend.at[k], recv_sem=mgrecv.at[k], **partner
+        )
+
+    g2 = [
+        pltpu.make_async_remote_copy(
+            src_ref=g2s.at[place ^ k], dst_ref=g2r.at[k], send_sem=g2send.at[k], recv_sem=g2recv.at[k],
+            device_id=(stream, place ^ k), device_id_type=MESH,
+        )
+        for k in range(1, wide)
+    ]
+
+    def shared():
+        for c in g2:
+            c.start()
+
+    middle(
+        meta, wide, tokf, etab, cot, normed, own, other, w2, wo, cotw, ub, (dbm, dcm), dyb, blk, mg, gpart, bb, g2s,
+        block_o, sent, shared,
+    )
+    for k in range(3):
+        sent(k).wait()
+    for c in loads:
+        c.wait()
+
+    for s, lowref, highref in ((0, mg, mgx), (1, mgx, mg)):
+
+        @pl.when(stream == s)
+        def _():
+            def lay(i, _):
+                base = pl.multiple_of(i * 32, 32)
+                lowat = pl.multiple_of(jnp.minimum(base, WIN - 32), 32)
+                highat = pl.multiple_of(jnp.maximum(base - WBASE, 0), 32)
+                for c in range(G6):
+                    cols = slice(c * 128, c * 128 + 128)
+                    lowrow = lowref[pl.ds(lowat, 32), cols].astype(F32)
+                    highrow = highref[pl.ds(highat, 32), cols].astype(F32)
+                    v = jnp.where(base < WIN, lowrow, 0.0) + jnp.where(base >= WBASE, highrow, 0.0)
+                    dy[c, pl.ds(base, 32), :] = v
+                    dyb[pl.ds(base, 32), cols] = v.astype(BF)
+                return 0
+
+            lax.fori_loop(0, R // 32, lay, 0)
+
     sums[...] = jnp.zeros(sums.shape, F32)
 
     def prep(rev):
@@ -578,7 +742,7 @@
                 load(0, i - 3).start()
                 load(1, i - 3).start()
 
-            one = 1 + (i >> 20)
+            one = 1 + i // 1048576
             for k in (1, 0):
                 t = 2 * i + k
                 after = jnp.minimum(t + 1, NB - 1)
@@ -628,6 +792,7 @@
         return 0
 
     lax.fori_loop(0, R // 32, step_tile, 0)
+    pgs = bbd.at[:, 0:128]
     w_step = st[ROW_STEP : ROW_STEP + RANK, :].astype(BF)
     w_b = jnp.concatenate([st[ROW_B : ROW_B + N, :]] * N, 0).astype(BF)
     w_c = jnp.concatenate([st[ROW_C : ROW_C + N, :]] * N, 0).astype(BF)
@@ -641,6 +806,7 @@
             y = dot(sg, w_s[:, cols]) + dot(dbm[rows, :], w_b[:, cols]) + dot(dcm[rows, :], w_c[:, cols])
             dm[c, rows, :] += y[:, :128]
             dm[c + 1, rows, :] += y[:, 128:]
+    dc = dd
     dc[:, 0:HALO, :] = jnp.zeros((G6, HALO, 128), F32)
     dc[:, HALO + R : XR, :] = jnp.zeros((G6, HALO, 128), F32)
 
@@ -684,82 +850,85 @@
     def _():
         conv(True)
 
-    for h in range(2):
-        rows = slice(h * 592, h * 592 + 592)
-        npart_o[rows, :] = dot_nt(dyb[rows, :], w1[...])
+    theirs = pl.ds(pl.multiple_of((1 - stream) * WBASE, 32), WIN)
+    nsend = mg.at[:, 0:D]
+    nsend[...] = dot_nt(dyb[theirs, :], w1[...]).astype(BF)
+    nswap = pltpu.make_async_remote_copy(
+        src_ref=nsend, dst_ref=nrecv, send_sem=swsend.at[0], recv_sem=swrecv.at[0], **partner
+    )
+    nswap.start()
+    for c in g2:
+        c.wait()
+    for r in range(0, g2_o.shape[0], 24):
+        rows = slice(r, min(r + 24, g2_o.shape[0]))
+        total = g2s[place, :, :].astype(F32)[rows]
+        for k in range(1, wide):
+            total = total + g2r[k].astype(F32)[rows]
+        g2_o[rows, :] = total
+    g2swap = pltpu.make_async_remote_copy(
+        src_ref=g2_o, dst_ref=g2x_o, send_sem=swsend.at[1], recv_sem=swrecv.at[1], **partner
+    )
+    g2swap.start()
+    gpart[...] += dot_nt(dyb[pl.ds(wbase, WIN), :], w1[...])
     for c in range(0, D, 128):
         gw1_o[c : c + 128, :] = dot_tn(normed[:, c : c + 128], dyb[...])
-    top = dot_tn(pgs[...], al[...])
-    gb = dot_tn(dbm[...], al[...])
-    gc = dot_tn(dcm[...], al[...])
+    low = p[0:R, :].astype(BF)
+    gstep = dot_tn(low, ub[...])[0:RANK]
+
+    def activation(i, _):
+        rows = pl.ds(pl.multiple_of(i * 32, 32), 32)
+        for c in range(G6):
+            ub[rows, c * 128 : c * 128 + 128] = act[c, rows, :].astype(BF)
+        return 0
+
+    lax.fori_loop(0, R // 32, activation, 0)
+    top = dot_tn(pgs[...], ub[...])
+    gb = dot_tn(dbm[...], ub[...])
+    gc = dot_tn(dcm[...], ub[...])
     gb = sum(gb[k * N : k * N + N] for k in range(N))
     gc = sum(gc[k * N : k * N + N] for k in range(N))
-    low = p[0:R, :].astype(BF)
-    gstep = dot_tn(low, ub[...])[0:RANK]
     gdecay = jnp.concatenate([dacc[c] for c in range(G6)], 1) * LN2
 
     def total(k):
         return jnp.sum(sums[k], axis=0, keepdims=True)
 
     chan = [total(3 + k) for k in range(4)] + [total(2), total(1), total(0)]
-    chan = jnp.concatenate(chan + [jnp.zeros((1, E), F32)], 0)
+    fine = [jnp.sum(stats[k], axis=0, keepdims=True) * (1.0 / VIEW_TOK) for k in range(2)]
+    coarse = [v.astype(BF).astype(F32) for v in fine]
+    fine = [a - b for a, b in zip(fine, coarse)]
+    chan = jnp.concatenate(chan + [jnp.zeros((1, E), F32)] + coarse + fine, 0)
     gt = jnp.concatenate(
-        [top[0:RANK], gb, gc, gstep, gdecay, chan, jnp.zeros((128 - 104, E), F32)], 0
+        [top[0:RANK], gb, gc, gstep, gdecay, chan, jnp.zeros((128 - 108, E), F32)], 0
     )
     gs_o[...] = gt.T
 
 
-def backward(meta, normed, x, act, al, dl, p, st, mgo, mgx, w1, hs):
-    S = jax.ShapeDtypeStruct
-    big = pltpu.VMEM((G6, R, 128), F32)
-    return pl.pallas_call(
-        bwd_kernel,
-        out_shape=[S((R, D), F32), S((D, E), F32), S((E, 128), F32)],
-        in_specs=[SMEM] + [VMEM] * 10 + [ANY],
-        out_specs=[VMEM] * 3,
-        scratch_shapes=[
-            pltpu.VMEM((XR, 128), jnp.int32), big, big,
-            pltpu.VMEM((R, E), BF), pltpu.VMEM((R, E), BF),
-            pltpu.VMEM((1280 * N, 128), F32),
-            pltpu.VMEM((R, 256), BF), pltpu.VMEM((R, 256), BF), pltpu.VMEM((R, 256), BF),
-            big, big, pltpu.VMEM((G6, N, 128), F32), pltpu.VMEM((R, 128), BF),
-            pltpu.VMEM((RING, 256, E), BF), pltpu.VMEM((RING, 256, E), BF),
-            pltpu.VMEM((256, E), BF), pltpu.VMEM((256, E), BF),
-            pltpu.VMEM((256, E), BF), pltpu.VMEM((256, E), BF),
-            pltpu.VMEM((G6, XR, 128), F32), pltpu.VMEM((32, 256), BF),
-            pltpu.VMEM((7, 8, E), F32),
-            pltpu.SemaphoreType.DMA((2, RING)),
-        ],
-        compiler_params=pltpu.CompilerParams(vmem_limit_bytes=63 * 2**20),
-        name="backward",
-    )(meta, normed, x, act, al, dl, p, st, mgo, mgx, w1, hs)
-
-
-def end_kernel(wide, meta, tok, etab, cot, npart, other, gpart, st, tg_o, gg_o, cotw, out, gain_s, acc):
+    nswap.wait()
+    ending(meta, wide, tok, etab, cot, nrecv, gpart, st, zs.at[0:3], zs.at[3:6], dd.at[0:3], gain_s, acc, tg_o, gg_o)
+    g2swap.wait()
+
+
+def ending(meta, wide, tok, etab, cot, other, gpart, st, tokf, cotw, out, gain_s, acc, tg_o, gg_o):
     stream = meta[4]
     wbase = pl.multiple_of(stream * WBASE, 32)
+    lay_tokens(tok, tokf)
+    lay_cotangent(stream, cot, cotw)
     gain_s[...] = gain_row(st, wide)
     acc[...] = jnp.zeros(acc.shape, F32)
-    cotw[...] = jnp.zeros(cotw.shape, F32)
-    for s, off in ((0, 0), (1, WIN - HALF - 8)):
-
-        @pl.when(stream == s)
-        def _():
-            cotw[off : off + HALF, :] = cot[...].astype(F32)
-
     lo = stream * HALF
 
     def tile(i, _):
         base = pl.multiple_of(i * 32, 32)
         at = pl.multiple_of(wbase + base, 32)
-        res, _l = residual_tile(meta, tok[pl.ds(at, 32), :], etab, at, 32)
+        rows = pl.ds(base, 32)
+        res, _l = residual_tile(meta, tokf, etab, at, 32)
         scale = row_scale(res)
         r = at + lax.broadcasted_iota(jnp.int32, (32, 128), 0)
         mine = (r >= lo) & (r < lo + HALF)
         ng, un = [], []
         for c in range(3):
             cols = slice(c * 128, c * 128 + 128)
-            v = npart[pl.ds(at, 32), cols] + other[pl.ds(base, 32), cols].astype(F32) + gpart[pl.ds(base, 32), cols]
+            v = gpart[rows, cols] + other[rows, cols].astype(F32)
             unit = res[c] * scale
             t = jnp.where(mine, v * unit, 0.0)
             acc[:, cols] += t[0:8] + t[8:16] + t[16:24] + t[24:32]
@@ -767,32 +936,225 @@
             un.append(unit)
         mean = sum(jnp.sum(a * b, axis=1, keepdims=True) for a, b in zip(ng, un)) * (1.0 / D)
         for c in range(3):
-            cols = slice(c * 128, c * 128 + 128)
-            out[pl.ds(base, 32), cols] = cotw[pl.ds(base, 32), cols] + scale * (ng[c] - un[c] * mean)
+            out[c, rows, :] = cotw[c, rows, :] + scale * (ng[c] - un[c] * mean)
         return 0
 
     lax.fori_loop(0, WIN // 32, tile, 0)
     gg_o[...] = acc[...]
-    for s, off in ((0, 0), (1, WIN - HALF - 8)):
-
-        @pl.when(stream == s)
-        def _():
-            tg_o[...] = out[off : off + HALF, :]
-
-
-def ending(wide, meta, tok, etab, cot, npart, other, gpart, st):
+    take_half(stream, out, tg_o)
+
+
+def backward(wide, count, offset, stride, tok, cot, normed, own, other, pack, stats, w1, st, x, act, dl, p, hs):
+    S = jax.ShapeDtypeStruct
+    V = pltpu.VMEM
+    big = V((G6, R, 128), F32)
+    own_rows = pack.shape[1]
+    return pl.pallas_call(
+        functools.partial(bwd_kernel, wide),
+        out_shape=[
+            S((HALF, D), F32), S((HALF, D), F32), S((D, E), F32), S((E, 128), F32), S((8, D), F32),
+            S((own_rows, E), F32), S((own_rows, E), F32),
+        ],
+        in_specs=[SMEM] * 3 + [VMEM] * 9 + [ANY] * 5,
+        out_specs=[VMEM] * 7,
+        scratch_shapes=[
+            V((G6, XR, 128), F32), big, big, V((1280, 128), F32),
+            V((D, E), BF), V((E, D), BF), V((WIN, D), F32), V((WIN, E), BF), V((WIN, E), BF),
+            V((wide, own_rows, E), BF), V((wide, own_rows, E), BF), V((WIN, D), BF),
+            V((XR, 128), jnp.int32), big, big, V((R, E), BF), V((R, E), BF), V((R * N, 128), F32),
+            V((R, 256), BF), V((R, 256), BF), V((R, 256), BF), V((G6, XR, 128), F32), big, V((G6, N, 128), F32),
+            V((RING, 256, E), BF), V((RING, 256, E), BF),
+            V((256, E), BF), V((256, E), BF), V((256, E), BF), V((256, E), BF), V((32, 256), BF), V((7, 8, E), F32),
+            V((8, D), F32), V((8, D), F32), V((8, D), F32),
+            pltpu.SemaphoreType.DMA((2, RING)), pltpu.SemaphoreType.DMA((4,)),
+            pltpu.SemaphoreType.DMA((3,)), pltpu.SemaphoreType.DMA((3,)),
+            pltpu.SemaphoreType.DMA((wide,)), pltpu.SemaphoreType.DMA((wide,)),
+            pltpu.SemaphoreType.DMA((2,)), pltpu.SemaphoreType.DMA((2,)),
+        ],
+        compiler_params=pltpu.CompilerParams(
+            vmem_limit_bytes=63 * 2**20, collective_id=4, has_side_effects=True
+        ),
+        cost_estimate=pl.CostEstimate(flops=int(9e10), bytes_accessed=1 << 20, transcendentals=0),
+        name="backward",
+    )(count, offset, stride, tok, cot, normed, own, other, pack, stats, w1, st, x, act, dl, p, hs)
+
+
+PACK = 128
+ROWS_S = 48
+ROWS_W = 24
+
+
+def greet(d, w, wide):
+    bar = pltpu.get_barrier_semaphore()
+    for k in range(1, wide):
+        pl.semaphore_signal(bar, inc=1, device_id=(d, w ^ k), device_id_type=MESH)
+    pl.semaphore_signal(bar, inc=1, device_id=(1 - d, w), device_id_type=MESH)
+    pl.semaphore_wait(bar, wide)
+
+
+def gather_kernel(
+    wide, inp, state, step, decay, chan, gain, w1_o, s_o, stage, mine, got, send, recv, psend, precv
+):
+    d, w = lax.axis_index("dir"), lax.axis_index("wide")
+    stage[...] = jnp.zeros(stage.shape, F32)
+    stage[ROW_STEP:ROW_DECAY, 0:ROWS_S] = step[0]
+    stage[ROW_DECAY:ROW_CHAN, 0:ROWS_S] = decay[0]
+    stage[ROW_CHAN:ROW_GAIN, 0:ROWS_S] = chan[0]
+    stage[ROW_GAIN : ROW_GAIN + 1, 0:ROWS_W] = gain[...]
+    small = stage[...].T[0:ROWS_S]
+    stage[0:ROWS_S, 0:ROW_STEP] = state[0]
+    col = lax.broadcasted_iota(jnp.int32, (ROWS_S, 128), 1)
+    parts = [jnp.where(col < ROW_STEP, stage[0:ROWS_S, :], small)]
+    for c in range(3):
+        low, high = inp[:, c * 128 : c * 128 + 128], inp[:, D + c * 128 : D + c * 128 + 128]
+        parts.append(jnp.where(d == 0, low, high))
+    parts.append(jnp.zeros((PACK - ROWS_S - 3 * ROWS_W, 128), F32))
+    mine[...] = jnp.concatenate(parts, 0).astype(BF)
+    got[w] = mine[...]
+    greet(d, w, wide)
+    copies = []
+    for k in range(1, wide):
+        copies.append(
+            pltpu.make_async_remote_copy(
+                src_ref=mine, dst_ref=got.at[w], send_sem=send.at[k], recv_sem=recv.at[k],
+                device_id=(d, w ^ k), device_id_type=MESH,
+            )
+        )
+        copies[-1].start()
+    for c in copies:
+        c.wait_recv()
+    for k in range(0, wide, 2):
+        s_o[k * ROWS_S : (k + 2) * ROWS_S, :] = jnp.concatenate([got[k, 0:ROWS_S], got[k + 1, 0:ROWS_S]], 0)
+        v = [got[k + i, ROWS_S:PACK, :].astype(F32) for i in range(2)]
+        for c in range(3):
+            piece = [t[c * ROWS_W : (c + 1) * ROWS_W] for t in v]
+            piece = jnp.concatenate(piece, 0).astype(BF)
+            for s in range(2):
+
+                @pl.when(d == s)
+                def _():
+                    at = s * D + c * 128
+                    w1_o[k * ROWS_W : (k + 2) * ROWS_W, at : at + 128] = piece
+
+    cols = pl.ds(pl.multiple_of(d * D, 128), D)
+    half = pltpu.make_async_remote_copy(
+        src_ref=w1_o.at[:, cols], dst_ref=w1_o.at[:, cols], send_sem=psend, recv_sem=precv,
+        device_id=(1 - d, w), device_id_type=MESH,
+    )
+    half.start()
+    for c in copies:
+        c.wait_send()
+    half.wait()
+
+
+def gather(wide, inp, state, step, decay, chan, gain):
     S = jax.ShapeDtypeStruct
     return pl.pallas_call(
-        functools.partial(end_kernel, wide),
-        out_shape=[S((HALF, D), F32), S((8, D), F32)],
-        in_specs=[SMEM] + [VMEM] * 7,
+        functools.partial(gather_kernel, wide),
+        out_shape=[S((D, E), BF), S((E, 128), BF)],
+        in_specs=[VMEM] * 6,
         out_specs=[VMEM] * 2,
         scratch_shapes=[
-            pltpu.VMEM((WIN, D), F32), pltpu.VMEM((WIN, D), F32), pltpu.VMEM((8, D), F32), pltpu.VMEM((8, D), F32),
+            pltpu.VMEM((128, 128), F32), pltpu.VMEM((PACK, 128), BF), pltpu.VMEM((wide, PACK, 128), BF),
+            pltpu.SemaphoreType.DMA((wide,)), pltpu.SemaphoreType.DMA((wide,)),
+            pltpu.SemaphoreType.DMA, pltpu.SemaphoreType.DMA,
         ],
-        compiler_params=pltpu.CompilerParams(vmem_limit_bytes=60 * 2**20),
-        name="ending",
-    )(meta, tok, etab, cot, npart, other, gpart, st)
+        compiler_params=pltpu.CompilerParams(collective_id=1, has_side_effects=True),
+        name="gather",
+    )(inp, state, step, decay, chan, gain)
+
+
+def reduce_kernel(
+    wide, gw1, gs, gg, own_o, other_o,
+    pout, pin, out, got, gcol, send, recv, psend, precv, fsend, frecv,
+):
+    d, w = lax.axis_index("dir"), lax.axis_index("wide")
+    greet(d, w, wide)
+    for s in range(2):
+
+        @pl.when(d == s)
+        def _():
+            pout[...] = gw1[:, (1 - s) * D : (2 - s) * D].astype(BF)
+
+    pre = pltpu.make_async_remote_copy(
+        src_ref=pout, dst_ref=pin, send_sem=psend, recv_sem=precv,
+        device_id=(1 - d, w), device_id_type=MESH,
+    )
+    pre.start()
+    gcol[...] = gg[...].T
+    pre.wait()
+    copies = []
+    lane = lax.broadcasted_iota(jnp.int32, (ROWS_S, 128), 1)
+    for k in range(wide):
+        rows = slice(k * ROWS_W, (k + 1) * ROWS_W)
+        g = jnp.sum(gcol[rows, :], axis=1, keepdims=True)
+        g = jnp.concatenate([g, jnp.zeros((ROWS_S - ROWS_W, 1), F32)], 0)
+        small = jnp.where(lane == ROW_GAIN, g, gs[k * ROWS_S : (k + 1) * ROWS_S, :])
+        parts = [small]
+        at = k * ROWS_W % 16
+        base = k * ROWS_W - at
+        arrived = pin[base : base + 32, :].astype(F32)[at : at + ROWS_W]
+        for c in range(3):
+            low, high = gw1[rows, c * 128 : c * 128 + 128], gw1[rows, D + c * 128 : D + c * 128 + 128]
+            parts.append(jnp.where(d == 0, low, high) + arrived[:, c * 128 : c * 128 + 128])
+        parts.append(jnp.zeros((PACK - ROWS_S - 3 * ROWS_W, 128), F32))
+        out[k] = jnp.concatenate(parts, 0).astype(BF)
+    for k in range(1, wide):
+        copies.append(
+            pltpu.make_async_remote_copy(
+                src_ref=out.at[w ^ k], dst_ref=got.at[k], send_sem=send.at[k], recv_sem=recv.at[k],
+                device_id=(d, w ^ k), device_id_type=MESH,
+            )
+        )
+        copies[-1].start()
+    for c in copies:
+        c.wait()
+    total = out[w].astype(F32)
+    for k in range(1, wide):
+        total = total + got[k].astype(F32)
+    own_o[...] = total
+    last = pltpu.make_async_remote_copy(
+        src_ref=own_o, dst_ref=other_o, send_sem=fsend, recv_sem=frecv,
+        device_id=(1 - d, w), device_id_type=MESH,
+    )
+    last.start()
+    last.wait()
+
+
+def reduce(wide, gw1, gs, gg):
+    S = jax.ShapeDtypeStruct
+    return pl.pallas_call(
+        functools.partial(reduce_kernel, wide),
+        out_shape=[S((PACK, 128), F32), S((PACK, 128), F32)],
+        in_specs=[VMEM] * 3,
+        out_specs=[VMEM] * 2,
+        scratch_shapes=[
+            pltpu.VMEM((D, D), BF), pltpu.VMEM((D, D), BF), pltpu.VMEM((wide, PACK, 128), BF),
+            pltpu.VMEM((wide, PACK, 128), BF), pltpu.VMEM((D, 8), F32),
+            pltpu.SemaphoreType.DMA((wide,)), pltpu.SemaphoreType.DMA((wide,)),
+        ]
+        + [pltpu.SemaphoreType.DMA] * 4,
+        compiler_params=pltpu.CompilerParams(collective_id=2, has_side_effects=True),
+        name="reduce",
+    )(gw1, gs, gg)
+
+
+def gather_plain(inp, state, step, decay, chan, gain):
+    rows = state.shape[1]
+    column = jnp.concatenate([gain, jnp.zeros((rows - gain.shape[0],), F32)])[:, None]
+    small = [state[0], step[0].T, decay[0].T, chan[0].T, column, jnp.zeros((rows, 127 - ROW_GAIN), F32)]
+    small = jnp.concatenate(small, 1).astype(BF)
+    return (
+        lax.all_gather(inp[:, :E].astype(BF), "wide", axis=0, tiled=True),
+        lax.all_gather(small, "wide", axis=0, tiled=True),
+    )
+
+
+def reduce_plain(gw1, gs, gg):
+    def total(v):
+        return lax.psum_scatter(v, "wide", scatter_dimension=0, tiled=True)
+
+    return total(lax.psum(gw1, "dir")), total(gs), total(lax.psum(gg.sum(0), "dir"))
 
 
 def adam_step(weight, gradient, first_moment, second, step_rate, decay_rate):
@@ -806,90 +1168,103 @@
     return (weight, first_moment, second)
 
 
-def sum_at_owner(array, axis):
-    n = lax.axis_size(axis)
-    blocks = array.reshape(n, array.shape[0] // n, *array.shape[1:])
-    arrived = lax.all_to_all(blocks, axis, split_axis=0, concat_axis=0, tiled=True)
-    return arrived.astype(F32).sum(axis=0)
-
-
-def swap(array):
-    return lax.ppermute(array, "dir", [(0, 1), (1, 0)])
-
-
-def local(
-    tokens, cotangent, view_counts, view_strides, view_offsets,
-    in_proj, in_first, in_second, out_proj, out_first, out_second,
-    norm_gain, gain_first, gain_second, state_proj, state_first, state_second,
-    step_proj, step_first, step_second, log_decay, decay_first, decay_second,
-    channels, chan_first, chan_second,
-):
+def update_kernel(got, twin, g2, g2x, *refs):
+    stream = lax.axis_index("dir")
+    masters, outs = refs[:21], refs[21:]
+
+    def step(k, gradient, at=(slice(None),), out=None):
+        new = adam_step(
+            masters[3 * k][at], gradient, masters[3 * k + 1][at], masters[3 * k + 2][at], RATES[k], DECAYS[k]
+        )
+        for i in range(3):
+            outs[1 + 3 * k + i][at] = new[i]
+
+    mine, theirs = got[...], twin[...]
+    low, high = jnp.where(stream == 0, mine, theirs), jnp.where(stream == 0, theirs, mine)
+    for h, v in enumerate((low, high)):
+        for c in range(3):
+            at = ROWS_S + c * ROWS_W
+            col = h * D + c * 128
+            step(0, v[at : at + ROWS_W], (slice(None), slice(col, col + 128)))
+    shared = g2[...] + g2x[...]
+    step(0, shared[0:ROWS_W], (slice(None), slice(E, 2 * E)))
+    step(1, shared[ROWS_W:, 0:D], (slice(0, ROWS_W), slice(None)))
+    step(1, shared[ROWS_W:, D:], (slice(ROWS_W, 2 * ROWS_W), slice(None)))
+    t = mine.T
+    gain = t[ROW_GAIN : ROW_GAIN + 1, 0:ROWS_W] + theirs.T[ROW_GAIN : ROW_GAIN + 1, 0:ROWS_W]
+    step(2, gain)
+    step(3, mine[0:ROWS_S, 0:ROW_STEP], (0,))
+    step(4, t[ROW_STEP:ROW_DECAY, 0:ROWS_S], (0,))
+    step(5, t[ROW_DECAY:ROW_CHAN, 0:ROWS_S], (0,))
+    for k in range(7):
+        step(6, t[ROW_CHAN + k : ROW_CHAN + k + 1, 0:ROWS_S], (k,))
+    outs[0][0] = t[ROW_STATS : ROW_STATS + 2, 0:ROWS_S] + t[ROW_STATS + 2 : ROW_STATS + 4, 0:ROWS_S]
+
+
+def update(got, twin, g2, g2x, masters):
+    S = jax.ShapeDtypeStruct
+    masters = list(masters)
+    masters[6:9] = [v[None] for v in masters[6:9]]
+    masters[18:21] = [jnp.transpose(v, (1, 0, 2)) for v in masters[18:21]]
+    outs = pl.pallas_call(
+        update_kernel,
+        out_shape=[S((1, 2, ROWS_S), F32)] + [S(v.shape, F32) for v in masters],
+        in_specs=[VMEM] * 25,
+        out_specs=[VMEM] * 22,
+        name="update",
+    )(got, twin, g2, g2x, *masters)
+    stats, outs = outs[0], list(outs[1:])
+    outs[6:9] = [v[0] for v in outs[6:9]]
+    outs[18:21] = [jnp.transpose(v, (1, 0, 2)) for v in outs[18:21]]
+    return stats, outs
+
+
+def update_plain(gw1, gs, gg, g2, masters):
+    drow = masters[0].shape[0]
+    g1, small, gain = reduce_plain(gw1, gs, gg)
+    t = small.T
+    grads = (
+        jnp.concatenate([g1, g2[:drow]], 1),
+        jnp.concatenate([g2[drow:, :D], g2[drow:, D:]], 0),
+        gain,
+        small[None, :, :ROW_STEP],
+        t[None, ROW_STEP:ROW_DECAY],
+        t[None, ROW_DECAY:ROW_CHAN],
+        t[None, ROW_CHAN:ROW_GAIN],
+    )
+    outs = []
+    for k, g in enumerate(grads):
+        w, f, s2 = masters[3 * k : 3 * k + 3]
+        outs += adam_step(w, g, f, s2, RATES[k], DECAYS[k])
+    return (t[ROW_STATS : ROW_STATS + 2] + t[ROW_STATS + 2 : ROW_STATS + 4])[None], outs
+
+
+def local(tokens, cotangent, view_counts, view_strides, view_offsets, *masters):
     stream = lax.axis_index("dir")
     wide = lax.axis_size("wide")
-    rows = state_proj.shape[1]
-    own_gain = norm_gain.shape[0]
-    gain_col = jnp.concatenate([norm_gain, jnp.zeros((rows - own_gain,), F32)])[:, None]
-    small = jnp.concatenate(
-        [
-            state_proj[0], step_proj[0].T, log_decay[0].T, channels[0].T, gain_col,
-            jnp.zeros((rows, 128 - ROW_GAIN - 1), F32),
-        ],
-        1,
-    ).astype(BF)
-    w_in = lax.all_gather(in_proj.astype(BF), "wide", axis=0, tiled=True)
-    w_out = lax.all_gather(out_proj.astype(BF), "wide", axis=0, tiled=True)
-    s = lax.all_gather(small, "wide", axis=0, tiled=True)
-    w1, w2 = w_in[:, :E], w_in[:, E:]
-
-    meta = jnp.concatenate(
-        [view_counts, view_offsets[0], stream[None].astype(jnp.int32), jnp.zeros((3,), jnp.int32)]
-    )
-    half = D // 2
-    freq = jnp.exp(-math.log(10000.0) * jnp.arange(half, dtype=F32) / half)
-    angles = view_strides[0].astype(F32)[:, None] * freq[None, :]
-    etab = jnp.concatenate([jnp.sin(angles), jnp.cos(angles)], 1)
-    rest = jnp.concatenate([jnp.zeros((1, half), F32), jnp.ones((1, half), F32)], 1)
-    etab = jnp.concatenate([etab, rest, jnp.zeros((4, D), F32)], 0)
-    tok = jnp.pad(tokens[0], ((0, R - SLOTS), (0, 0)))
-    cot = cotangent[0]
-
-    normed, x, act, al, dl, p, st, res, stats, hs = forward(wide, meta, tok, etab, w1, s)
-    mine = lax.dynamic_slice_in_dim(res, stream * WBASE, WIN, 0)
-    other = swap(lax.dynamic_slice_in_dim(res, (1 - stream) * WBASE, WIN, 0))
-    block, mg, gpart, gw2, gwo = middle(meta, tok, etab, cot, normed, mine, other, w2, w_out)
-    mgx = swap(mg)
-    mg0 = jnp.where(stream == 0, mg, mgx)
-    mg1 = jnp.where(stream == 0, mgx, mg)
-    npart, gw1, gs = backward(meta, normed, x, act, al, dl, p, st, mg0, mg1, w1, hs)
-    other = swap(lax.dynamic_slice_in_dim(npart, (1 - stream) * WBASE, WIN, 0).astype(BF))
-    token_grad, gg = ending(wide, meta, tok, etab, cot, npart, other, gpart, st)
-
-    gin = jnp.concatenate([gw1, gw2], 1)
-    gin, gwo, gg = (
-        lax.psum(gin.astype(BF), "dir"),
-        lax.psum(gwo.astype(BF), "dir"),
-        lax.psum(gg.sum(0).astype(BF), "dir"),
-    )
-    shard_in = sum_at_owner(gin, "wide")
-    shard_out = sum_at_owner(gwo, "wide")
-    shard_gain = sum_at_owner(gg, "wide")
-    shard_small = sum_at_owner(gs.astype(BF), "wide")
-    small_t = shard_small.T
-    stats = stats.sum(1) / VIEW_TOK
-    stats = sum_at_owner(stats.T, "wide").T
-
-    outs = []
-    for w, g, f, s2, k in (
-        (in_proj, shard_in, in_first, in_second, 0),
-        (out_proj, shard_out, out_first, out_second, 1),
-        (norm_gain, shard_gain, gain_first, gain_second, 2),
-        (state_proj, shard_small[None, :, : ROW_STEP], state_first, state_second, 3),
-        (step_proj, small_t[None, ROW_STEP:ROW_DECAY], step_first, step_second, 4),
-        (log_decay, small_t[None, ROW_DECAY:ROW_CHAN], decay_first, decay_second, 5),
-        (channels, small_t[None, ROW_CHAN:ROW_GAIN], chan_first, chan_second, 6),
-    ):
-        outs += adam_step(w, g, f, s2, RATES[k], DECAYS[k])
-    return (block[None], token_grad[None], stats[None], *outs)
+    in_proj, out_proj, norm_gain = masters[0], masters[3], masters[6]
+    drow, erow = in_proj.shape[0], out_proj.shape[0]
+    mine = E // wide == ROWS_S and D // wide == ROWS_W
+    out_pair = jnp.concatenate([out_proj[: erow // 2], out_proj[erow // 2 :]], 1)
+    pack = jnp.concatenate([in_proj[:, E:], out_pair], 0).astype(BF)
+    pack = lax.all_gather(pack, "wide", axis=0)
+    weights = (in_proj, masters[9], masters[12], masters[15], masters[18])
+    if mine:
+        w1, s = gather(wide, *weights, norm_gain[None])
+    else:
+        w1, s = gather_plain(*weights, norm_gain)
+    about = (view_counts, view_offsets, view_strides)
+    tok, cot = tokens[0], cotangent[0]
+    normed, x, act, dl, p, st, res, other, stats, hs = forward(wide, *about, tok, w1, s)
+    own = lax.dynamic_slice_in_dim(res, stream * WBASE, WIN, 0)
+    block, token_grad, gw1, gs, gg, g2, g2x = backward(
+        wide, *about, tok, cot, normed, own, other, pack, stats, w1, st, x, act, dl, p, hs
+    )
+    if mine:
+        stats, outs = update(*reduce(wide, gw1, gs, gg), g2, g2x, masters)
+    else:
+        stats, outs = update_plain(gw1, gs, gg, g2 + g2x, masters)
+    return (block[None], token_grad[None], stats, *outs)
 
 
 def solution(mesh):

time: 359 us -> 204 us (0.57)
  blocking collectives: 127 us -> 0 us
  Pallas kernels: 135 us -> 177 us
  waiting for transfers between devices: 29.7 us -> 0.02 us
  other arithmetic: 17.4 us -> 2.43 us
  starting transfers between devices: 13.6 us -> 0.04 us
  local copies, waits for them, and re-layouts: 20.5 us -> 9.54 us
    all_gather x2 -> x0, blocking collectives: 90.7 us -> none  [the longest x1 46.5 us: local(): s = lax.all_gather(small, 'wide', axis=0, tiled=True)]
    pallas_call x4 -> x5, Pallas kernels: 135 us -> 177 us  [the longest x1 85.6 us: backward(): pl.pallas_call(functools.partial(bwd_kernel, wide), out_shape=[S((HALF, D...]
    all_to_all x2 -> x0, blocking collectives: 34.2 us -> none  [sum_at_owner(): lax.all_to_all(blocks, axis, split_axis=0, concat_axis=0, tiled=True)]
    all_to_all x3 -> x0, waiting for transfers between devices: 21.6 us -> none  [sum_at_owner(): lax.all_to_all(blocks, axis, split_axis=0, concat_axis=0, tiled=True)]
    all_to_all x3 -> x0, starting transfers between devices: 11.1 us -> none  [sum_at_owner(): lax.all_to_all(blocks, axis, split_axis=0, concat_axis=0, tiled=True)]
    all_gather x1, waiting for transfers between devices: 7.59 us -> 0.01 us  [local(): pack = lax.all_gather(pack, 'wide', axis=0)]
    sub x7 -> x0, other arithmetic: 3.98 us -> none  [adam_step(): weight - step_rate * (first_hat / (jnp.sqrt(second_hat) + EPS_ADAM) + dec...]
    unnamed x70 -> x3, local copies, waits for them, and re-layouts: 10.9 us -> 7.32 us
  transfers between devices with their start and end apart: 8 -> 1, of which waited for: 4 -> 0; matrix products, arithmetic and copies ran while one was open for 7% -> 2% of each run, Pallas kernels for 2% -> 34%
where the time goes in v2:
time: 204 us
  Pallas kernels  177 us (87%)
  between operations  14.8 us (7%)
  local copies, waits for them, and re-layouts  9.54 us (5%)
  other arithmetic  2.43 us (1%)
    pallas_call x1, Pallas kernels, backward(): pl.pallas_call(functools.partial(bwd_kernel, wide), out_shape=[S((HALF, D...  85.6 us
    pallas_call x1, Pallas kernels, forward(): pl.pallas_call(functools.partial(fwd_kernel, wide), out_shape=[S(*k) for...  46.5 us
    pallas_call x1, Pallas kernels, gather(): pl.pallas_call(functools.partial(gather_kernel, wide), out_shape=[S((D, E...  21.8 us
    pallas_call x1, Pallas kernels, reduce(): pl.pallas_call(functools.partial(reduce_kernel, wide), out_shape=[S((PACK...  20.3 us
    unnamed x3, local copies, waits for them, and re-layouts  7.32 us
  transfers between devices with their start and end apart: 1, of which 0 were waited for; matrix products, arithmetic and copies ran while one was open for 2% of the time, Pallas kernels for 34%

profile of v2, /device:TPU:0, one launch (start us, length us, event | category | flops | bytes accessed | tf_op | source)
XLA Modules:
  0.0 203.6 jit_solution(18253156197664389902)
XLA Ops:
  7.2 0.0 all-gather.2.cloned.1.call-start
  7.2 0.9 convert.14
  8.1 0.9 fusion
  9.0 0.6 pad_maximum_fusion
  9.7 0.0 all-gather.2.cloned.1.call-update
  10.3 1.3 copy.53.chan
  11.6 21.8 %gather.1 = (bf16[384,768]{1,0:T(8,128)(2,1)}, bf16[768,128]{1,0:T(8,128)(2,1)}) custom-call(f32[24,1536]{1,0:T(8,128)} %refs_0_.1, f32[1,48,56]{2,1,0:T(8,128)} %refs_9_.1, f32[1,24,48]{2,1,0:T(8,128)} %refs_12_.1, f32[1,16,48]{2,1,0:T(8,128)} %refs_15_.1, f32[1,7,48]{2,1,0:T(8,128)} %copy.53.chan, f32[1,24]{1,0:T(1,128)} %bitcast.25), custom_call_target="tpu_custom_call" | custom-call | tf_op jit(solution)/shard_map/gather/pallas_call | solution.py:1052
  33.4 46.5 %forward.1 = (bf16[1184,384]{1,0:T(8,128)(2,1)}, f32[6,1200,128]{2,1,0:T(8,128)}, f32[6,1184,128]{2,1,0:T(8,128)}, f32[6,1184,128]{2,1,0:T(8,128)}, f32[1280,128...) custom-call(s32[1]{0:T(128)S(6)} %copy.56.count, ...), custom_call_target="tpu_custom_call" | custom-call | flops 49999998976 | bytes 1048576 | tf_op jit(solution)/shard_map/forward/pallas_call | solution.py:404
  79.9 2.2 %constant_dynamic-slice_fusion.own = bf16[608,768]{1,0:T(8,128)(2,1)} fusion(bf16[1184,768]{1,0:T(8,128)(2,1)} %get-tuple-element.70, s32[]{:T(128)S(6)} %select_n.3), kind=kLoop, calls=%fused_computation.4 | loop fusion | bytes 1867780 | tf_op jit(solution)/shard_map/dynamic_slice | solution.py:1259
  82.1 0.0 all-gather.2.cloned.1.call-done.pack
  82.1 85.6 %backward.1 = (f32[588,384]{1,0:T(8,128)}, f32[588,384]{1,0:T(8,128)}, f32[384,768]{1,0:T(8,128)}, f32[768,128]{1,0:T(8,128)}, f32[8,384]{1,0:T(8,128)}, /*index=5*/f32[48,768]{1,0:T(8,128)}, f32[48,768]{1,0:T(8,128)}) custom-call(s32[1]{0:T(128)S(6)} %copy.56.count, s32[1,3]{1,0:T(1,128)} %offset.3, s32[1,3]{1,0:T(1,128)} %stride.3, ...), custom_call_target="tpu_custom_call" | custom-call | flops 89999998976 | bytes 1048576 | tf_op jit(solution)/shard_map/backward/pallas_call | solution.py:952
  167.8 3.0 %copy.54 = f32[1,588,384]{2,0,1:T(1,128)} copy(f32[1,588,384]{2,1,0:T(8,128)} %bitcast.21) | data formatting | bytes 1806336
  170.8 3.0 %copy.55 = f32[1,588,384]{2,0,1:T(1,128)} copy(f32[1,588,384]{2,1,0:T(8,128)} %bitcast.20) | data formatting | bytes 1806336
  173.8 20.3 %reduce.1 = (f32[128,128]{1,0:T(8,128)}, f32[128,128]{1,0:T(8,128)}) custom-call(f32[384,768]{1,0:T(8,128)} %get-tuple-element.81.gw1, f32[768,128]{1,0:T(8,128)} %get-tuple-element.82.gs, f32[8,384]{1,0:T(8,128)} %get-tuple-element.83.gg), custom_call_target="tpu_custom_call" | custom-call | tf_op jit(solution)/shard_map/reduce/pallas_call | solution.py:1126
  194.1 2.6 %update.1 = (f32[1,2,48]{2,1,0:T(2,128)}, f32[24,1536]{1,0:T(8,128)}, f32[24,1536]{1,0:T(8,128)}, f32[24,1536]{1,0:T(8,128)}, f32[48,384]{1,0:T(8,128)}, /*index...) custom-call(f32[128,128]{1,0:T(8,128)} %get-tuple-element.84.got, ...), custom_call_target="tpu_custom_call" | custom-call | tf_op jit(solution)/shard_map/update/pallas_call | solution.py:1209
  (1 shorter events, 0.0 us)
Async XLA Ops:
  7.2 74.9 %all-gather.2.cloned.1.call-start = ((), (), s32[]{:S(2)}) async-start(), calls=%async_computation | async-start | bytes 1253376 | tf_op jit(solution)/shard_map/all_gather | solution.py:1250
Sparse Core Ops, SparseCore 0:
  11.4 61.6 all-gather.1

commit v3 on v2

--- a/solution.py
+++ b/solution.py
@@ -123,20 +123,21 @@
     return dot(src, pick)[0:8]
 
 
-def fill_broadcast(p_ref, lane, out_ref):
-    def spread(base, n):
-        v = p_ref[pl.ds(base, 128), :].T[lane : lane + N]
-        for j in range(n):
-            out_ref[pl.ds(pl.multiple_of((base + j) * N, N), N), :] = (
-                jnp.broadcast_to(v[:, j : j + 1], (N, 128))
-            )
-
-    def body(sb, _):
-        spread(pl.multiple_of(sb * 128, 128), 128)
+def spread_tile(p_ref, lane, out_ref, base):
+    v = p_ref[pl.ds(base, 32), :].T[lane : lane + N]
+    for j in range(32):
+        out_ref[pl.ds(pl.multiple_of((base + j) * N, N), N), :] = jnp.broadcast_to(v[:, j : j + 1], (N, 128))
+
+
+def pairs(count, body):
+    def two(i, _):
+        body(2 * i)
+        body(2 * i + 1)
         return 0
 
-    lax.fori_loop(0, R // 128, body, 0)
-    spread(R // 128 * 128, R % 128)
+    lax.fori_loop(0, count // 2, two, 0)
+    if count % 2:
+        body(count - 1)
 
 
 def conv_tile(x_ref, lab_ref, st_ref, c, base, n, rev):
@@ -170,41 +171,93 @@
     etab[...] = jnp.where(lane < half, jnp.sin(angle), jnp.cos(angle))
 
 
-def fwd_kernel(
-    wide, count, offset, stride, tok, w1, s_ref,
-    normed_h, x_h, act_h, dl_h, p_h, st_h, res_h, other_h, stats_o, hs_o,
-    normed_o, x_o, act_o, dl_o, p_o, st_o, res_o, other_o, al_o,
-    lab, dm, u, bb, cbd, hse, hso, gain_s, tokf, etab, sem, out_sem, send, recv,
-):
+def fwd_kernel(wide, mine, *refs):
+    refs = list(refs)
+    count, offset, stride, tok = refs[:4]
+    given, refs = refs[4 : 4 + (7 if mine else 2)], refs[4 + (7 if mine else 2) :]
+    (
+        normed_h, x_h, act_h, dl_h, p_h, st_h, res_h, other_h, w1_h, *pack_h, stats_o, hs_o,
+    ) = refs[: 12 if mine else 11]
+    (
+        normed_o, x_o, act_o, dl_o, p_o, st_o, res_o, other_o, w1, al_o, s_ref,
+        lab, dm, u, bb, cbd, hse, hso, gain_s, tokf, etab, sem, out_sem, send, recv, *links,
+    ) = refs[12 if mine else 11 :]
     stream, place = lax.axis_index("dir"), lax.axis_index("wide")
-    bar = pltpu.get_barrier_semaphore()
-    pl.semaphore_signal(bar, inc=1, device_id=(1 - stream, place), device_id_type=MESH)
     meta = views(count, offset, stream)
+    if mine:
+        stage, first, got, second, pack, gsend, grecv, psend, precv, hsem = links
+        fill_shares(stream, given, stage, first, second)
+        got[place] = first[...]
+        pack[place] = second[...]
+        greet(stream, place, wide)
+        early, later = [], []
+        for k in range(1, wide):
+            where = dict(device_id=(stream, place ^ k), device_id_type=MESH)
+            early.append(
+                pltpu.make_async_remote_copy(
+                    src_ref=first, dst_ref=got.at[place], send_sem=gsend.at[k], recv_sem=grecv.at[k], **where
+                )
+            )
+            later.append(
+                pltpu.make_async_remote_copy(
+                    src_ref=second, dst_ref=pack.at[place], send_sem=psend.at[k], recv_sem=precv.at[k], **where
+                )
+            )
+            early[-1].start()
+    else:
+        bar = pltpu.get_barrier_semaphore()
+        pl.semaphore_signal(bar, inc=1, device_id=(1 - stream, place), device_id_type=MESH)
+        pl.semaphore_wait(bar, 1)
+        w1[...] = given[0][...]
+        s_ref[...] = given[1][...]
     fill_embedding(stride, etab)
     lay_tokens(tok, tokf)
+    fill_labels(meta, lab)
+
+    def unit_tile(i):
+        base = i * 32 if isinstance(i, int) else pl.multiple_of(i * 32, 32)
+        res, _l = residual_tile(meta, tokf, etab, base, 32)
+        scale = row_scale(res)
+        for c in range(3):
+            tokf[c, pl.ds(base, 32), :] = res[c] * scale
+
+    pairs(R // 32, unit_tile)
+    if mine:
+        for c in early:
+            c.wait_recv()
+        take_shares(stream, wide, got, w1, s_ref)
+        cols = pl.ds(pl.multiple_of(stream * D, 128), D)
+        half = pltpu.make_async_remote_copy(
+            src_ref=w1.at[:, cols], dst_ref=w1.at[:, cols], send_sem=hsem.at[0], recv_sem=hsem.at[1],
+            device_id=(1 - stream, place), device_id_type=MESH,
+        )
+        half.start()
+        for c in early:
+            c.wait_send()
+        for c in later:
+            c.start()
     st_o[...] = s_ref[...].astype(F32).T
-    fill_labels(meta, lab)
     gain_s[...] = gain_row(st_o, wide)
     saves = [
         pltpu.make_async_copy(v, h, out_sem.at[k])
         for k, (v, h) in enumerate(
             zip(
-                (normed_o, x_o, act_o, dl_o, p_o, st_o, res_o, other_o),
-                (normed_h, x_h, act_h, dl_h, p_h, st_h, res_h, other_h),
+                (normed_o, x_o, act_o, dl_o, p_o, st_o, w1, res_o, other_o),
+                (normed_h, x_h, act_h, dl_h, p_h, st_h, w1_h, res_h, other_h),
             )
         )
     ]
 
     def norm_tile(i, _):
         base = pl.multiple_of(i * 32, 32)
-        res, _l = residual_tile(meta, tokf, etab, base, 32)
-        scale = row_scale(res)
         for c in range(3):
             cols = slice(c * 128, c * 128 + 128)
-            normed_o[pl.ds(base, 32), cols] = (res[c] * scale * gain_s[0:1, cols]).astype(BF)
+            normed_o[pl.ds(base, 32), cols] = (tokf[c, pl.ds(base, 32), :] * gain_s[0:1, cols]).astype(BF)
         return 0
 
     lax.fori_loop(0, R // 32, norm_tile, 0)
+    if mine:
+        half.wait()
     x_o[:, 0:HALO, :] = jnp.zeros((G6, HALO, 128), F32)
     x_o[:, HALO + R : XR, :] = jnp.zeros((G6, HALO, 128), F32)
     for h in range(2):
@@ -263,6 +316,7 @@
             cut = jnp.where(here == before, 0.0, CUT)
             live = jnp.where(here >= 0, 1.0, 0.0)
             real = jnp.where(here >= -1, 1.0, 0.0)
+            spread_tile(p_o, ROW_B, bb, base)
             for c in range(G6):
                 cols = slice(c * 128, c * 128 + 128)
                 rows = pl.ds(base, 32)
@@ -288,9 +342,8 @@
     def _():
         soft(True)
 
-    for c in saves[:6]:
+    for c in saves[:7]:
         c.start()
-    fill_broadcast(p_o, ROW_B, bb)
     hs = (hse, hso)
 
     def save(k, i):
@@ -352,9 +405,10 @@
                 functools.partial(emit, before, 1, jnp.maximum(i - 1, 0) % RING, c)
                 for c in (0, 2, 4)
             ]
-            state = block(2 * i, 0, slot, state, late)
+            one = 1 + i // 1048576
+            state = lax.fori_loop(0, one, lambda _, v, late=late: block(2 * i, 0, slot, v, list(late)), state)
             late = [functools.partial(emit, 2 * i, 0, slot, c) for c in (0, 2, 4)]
-            state = block(2 * i + 1, 1, slot, state, late)
+            state = lax.fori_loop(0, one, lambda _, v, late=late: block(2 * i + 1, 1, slot, v, list(late)), state)
             save(0, i).start()
             save(1, i).start()
 
@@ -379,8 +433,6 @@
 
         lax.fori_loop(NP - SENDS, NP, settle, 0)
 
-    pl.semaphore_wait(bar, 1)
-
     @pl.when(stream == 0)
     def _():
         scan(False)
@@ -389,50 +441,53 @@
     def _():
         scan(True)
 
-    for c in saves[6:]:
+    for c in saves[7:]:
         c.start()
+    if mine:
+        for c in later:
+            c.wait()
+        packed = pltpu.make_async_copy(pack, pack_h[0], out_sem.at[9])
+        packed.start()
+        packed.wait()
     for c in saves:
         c.wait()
 
 
-def forward(wide, count, offset, stride, tok, w1, s):
+def forward(wide, mine, count, offset, stride, tok, *given):
     S = jax.ShapeDtypeStruct
+    V = pltpu.VMEM
     kept = [
-        ((R, D), BF), ((G6, XR, 128), F32), ((G6, R, 128), F32), ((G6, R, 128), F32),
-        ((1280, 128), F32), ((128, E), F32), ((R, E), BF), ((WIN, E), BF),
+        ((R, D), BF), ((G6, XR, 128), F32), ((G6, R, 128), F32), ((G6, R, 128), F32), ((1280, 128), F32),
+        ((128, E), F32), ((R, E), BF), ((WIN, E), BF), ((D, E), BF),
     ]
+    pack = [((wide, 2 * D // wide, E), BF)] if mine else []
+    dma = pltpu.SemaphoreType.DMA
+    links = [
+        V((128, 128), F32), V((PACK, 128), BF), V((wide, PACK, 128), BF), V(pack[0][0][1:], BF), V(*pack[0]),
+        dma((wide,)), dma((wide,)), dma((wide,)), dma((wide,)), dma((2,)),
+    ] if mine else []
     return pl.pallas_call(
-        functools.partial(fwd_kernel, wide),
-        out_shape=[S(*k) for k in kept] + [S((2, 8, E), F32), S((2, NP, 256, E), BF)],
-        in_specs=[SMEM] * 3 + [VMEM] * 3,
-        out_specs=[ANY] * 8 + [VMEM, ANY],
-        scratch_shapes=[pltpu.VMEM(*k) for k in kept]
+        functools.partial(fwd_kernel, wide, mine),
+        out_shape=[S(*k) for k in kept + pack] + [S((2, 8, E), F32), S((2, NP, 256, E), BF)],
+        in_specs=[SMEM] * 3 + [VMEM] * (1 + len(given)),
+        out_specs=[ANY] * len(kept + pack) + [VMEM, ANY],
+        scratch_shapes=[V(*k) for k in kept]
         + [
-            pltpu.VMEM((R, E), BF),
-            pltpu.VMEM((XR, 128), jnp.int32),
-            pltpu.VMEM((G6, R, 128), F32),
-            pltpu.VMEM((G6, R, 128), F32),
-            pltpu.VMEM((R * N, 128), F32),
-            pltpu.VMEM((R, 256), BF),
-            pltpu.VMEM((RING, 256, E), BF),
-            pltpu.VMEM((RING, 256, E), BF),
-            pltpu.VMEM((8, D), F32),
-            pltpu.VMEM((3, R, 128), F32),
-            pltpu.VMEM((8, D), F32),
-            pltpu.SemaphoreType.DMA((2, RING)),
-            pltpu.SemaphoreType.DMA((8,)),
-            pltpu.SemaphoreType.DMA((SENDS,)),
-            pltpu.SemaphoreType.DMA((SENDS,)),
-        ],
+            V((R, E), BF), V((E, 128), BF), V((XR, 128), jnp.int32), V((G6, R, 128), F32), V((G6, R, 128), F32),
+            V((R * N, 128), F32), V((R, 256), BF), V((RING, 256, E), BF), V((RING, 256, E), BF), V((8, D), F32),
+            V((3, R, 128), F32), V((8, D), F32),
+            dma((2, RING)), dma((10,)), dma((SENDS,)), dma((SENDS,)),
+        ]
+        + links,
         compiler_params=pltpu.CompilerParams(
             vmem_limit_bytes=60 * 2**20, collective_id=3, has_side_effects=True
         ),
         cost_estimate=pl.CostEstimate(flops=int(5e10), bytes_accessed=1 << 20, transcendentals=0),
         name="forward",
-    )(count, offset, stride, tok, w1, s)
-
-
-def middle(meta, wide, tokf, etab, cot, normed, own, other, w2, wo, cotw, gated, bgrad, ggrad, blk, mg, gpart, stage, g2, block_o, sent, shared):
+    )(count, offset, stride, tok, *given)
+
+
+def middle(meta, wide, tokf, etab, cot, normed, own, other, w2, wo, cotw, gated, bgrad, ggrad, blk, mg, gpart, stage, sent, shared):
     stream = meta[4]
     wbase = pl.multiple_of(stream * WBASE, 32)
     lay_cotangent(stream, cot, cotw)
@@ -456,7 +511,7 @@
     for c in range(0, E, 256):
         cols = slice(c, c + 256)
         gate = dot(normed[win, :], w2[:, cols])
-        mixed = own[:, cols].astype(F32) + other[:, cols].astype(F32)
+        mixed = own(cols) + other(cols)
         sig = sigmoid(gate)
         silu = gate * sig
         gated[0:WIN, cols] = (mixed * silu).astype(BF)
@@ -474,11 +529,7 @@
         g = dot_tn(gated[0:WIN, c : c + 256], branch_grad())
         half = erow // 2
         lay_rows(g, c, half, lambda k, r, v: put(stage, pitch, k // 2, drow + r, (k % 2) * D, v))
-    for k in range(wide):
-        for c in range(G6):
-            at = (k * G6 + c) * pitch
-            g2[k, :, c * 128 : c * 128 + 128] = stage[at : at + rows, :].astype(BF)
-    shared()
+    shared(rows, pitch)
     for c in range(0, D, 128):
         cols = slice(c, c + 128)
         blk[c // 128, 0:WIN, :] = dot(gated[0:WIN, :], wo[:, cols])
@@ -493,7 +544,6 @@
         return 0
 
     lax.fori_loop(0, WIN // 32, out_tile, 0)
-    take_half(stream, blk, block_o)
 
 
 WINDOWS = ((0, 0), (1, WIN - HALF - 8))
@@ -509,13 +559,24 @@
                 cotw[c, off : off + HALF, :] = cot[:, c * 128 : c * 128 + 128].astype(F32)
 
 
-def take_half(stream, src, out):
+def take_half(stream, src, out, sem):
+    def copy(off, c):
+        return pltpu.make_async_copy(
+            src.at[c, off : off + HALF, :], out.at[:, 0, c * 128 : c * 128 + 128], sem.at[c]
+        )
+
     for s, off in WINDOWS:
 
         @pl.when(stream == s)
         def _():
             for c in range(3):
-                out[:, c * 128 : c * 128 + 128] = src[c, off : off + HALF, :]
+                copy(off, c).start()
+
+    def wait():
+        for c in range(3):
+            copy(0, c).wait()
+
+    return wait
 
 
 def put(ref, pitch, k, r, col, v):
@@ -545,24 +606,48 @@
         wo[2 * k * half : 2 * (k + per) * half, :] = jnp.concatenate(pieces, 0).astype(BF)
 
 
-def bwd_kernel(
-    wide, count, offset, stride, tok, cot, normed, own, other, pack, stats, w1, st,
-    x_h, act_h, dl_h, p_h, hs_in,
-    block_o, tg_o, gw1_o, gs_o, gg_o, g2_o, g2x_o,
-    x, act, dl, p, w2, wo, gpart, mg, mgx, g2s, g2r, nrecv,
-    lab, dm, dy, dyb, ub, bb, bbd, dbm, dcm, dd, zs, dacc, hse, hso, g0, g1, z0, z1, sel, sums,
-    etab, gain_s, acc, sem, in_sem, mgsend, mgrecv, g2send, g2recv, swsend, swrecv,
-):
+def bwd_kernel(wide, mine, *refs):
+    refs = list(refs)
+    count, offset, stride, tok, cot, normed, pack, stats, w1, st, res_h, other_h, x_h, act_h, dl_h, p_h, hs_in = refs[:17]
+    if mine:
+        block_h, tg_h, own_o, twin_o, g2_o, g2x_o = refs[17:23]
+    else:
+        block_h, tg_h, gw1, gsm, gg_o, g2_o = refs[17:23]
+    (
+        x, act, dl, p, w2, wo, gpart, mg, mgx, nrecv,
+        lab, dm, dy, dyb, ub, bb, bbd, dbm, dcm, dd, zs, dacc, hse, hso, g0, g1, z0, z1, pb0, pb1, pc0, pc1, sel, sums,
+        etab, gain_s, acc, sem, in_sem, out_sem, mgsend, mgrecv, swsend, swrecv, win_sem, *links,
+    ) = refs[23:]
+    if mine:
+        g2s, g2r, gw1, gsm, pout, pin, out, got, gout, gin, g2send, g2recv, rsend, rrecv, osend, orecv = links
     stream, place = lax.axis_index("dir"), lax.axis_index("wide")
+    wbase = pl.multiple_of(stream * WBASE, 32)
     loads = [
         pltpu.make_async_copy(h, v, in_sem.at[k])
         for k, (h, v) in enumerate(zip((x_h, act_h, dl_h, p_h), (x, act, dl, p)))
     ]
-    for c in loads:
+    windows = []
+    for i, (h, v, at) in enumerate(((res_h, hse, wbase), (other_h, hso, 0))):
+        for k in range(0, WIN, 256):
+            n = min(256, WIN - k)
+            rows = pl.ds(pl.multiple_of(at + k, 32), n)
+            windows.append(
+                pltpu.make_async_copy(h.at[rows, :], v.at[k // 256, 0:n, :], win_sem.at[i, k // 256])
+            )
+    for c in windows + loads:
         c.start()
-    greet(stream, place, wide)
+
+    def window(ref, cols):
+        rows = [ref[k // 256, 0 : min(256, WIN - k), cols] for k in range(0, WIN, 256)]
+        return jnp.concatenate(rows, 0).astype(F32)
+
+    if mine:
+        greet(stream, place, wide)
+    else:
+        bar = pltpu.get_barrier_semaphore()
+        pl.semaphore_signal(bar, inc=1, device_id=(1 - stream, place), device_id_type=MESH)
+        pl.semaphore_wait(bar, 1)
     meta = views(count, offset, stream)
-    wbase = pl.multiple_of(stream * WBASE, 32)
     partner = dict(device_id=(1 - stream, place), device_id_type=MESH)
     fill_embedding(stride, etab)
     fill_labels(meta, lab)
@@ -576,26 +661,74 @@
             src_ref=mg.at[:, cols], dst_ref=mgx.at[:, cols], send_sem=mgsend.at[k], recv_sem=mgrecv.at[k], **partner
         )
 
-    g2 = [
-        pltpu.make_async_remote_copy(
-            src_ref=g2s.at[place ^ k], dst_ref=g2r.at[k], send_sem=g2send.at[k], recv_sem=g2recv.at[k],
-            device_id=(stream, place ^ k), device_id_type=MESH,
-        )
-        for k in range(1, wide)
-    ]
-
-    def shared():
+    g2 = []
+    if mine:
+        for k in range(1, wide):
+            g2.append(
+                pltpu.make_async_remote_copy(
+                    src_ref=g2s.at[place ^ k], dst_ref=g2r.at[k], send_sem=g2send.at[k], recv_sem=g2recv.at[k],
+                    device_id=(stream, place ^ k), device_id_type=MESH,
+                )
+            )
+
+    def shared(rows, pitch):
+        for k in range(wide):
+            for c in range(G6):
+                at = (k * G6 + c) * pitch
+                cols = slice(c * 128, c * 128 + 128)
+                if mine:
+                    g2s[k, :, cols] = bb[at : at + rows, :].astype(BF)
+                else:
+                    g2_o[k, :, cols] = bb[at : at + rows, :]
         for c in g2:
             c.start()
 
+    for c in windows:
+        c.wait()
     middle(
-        meta, wide, tokf, etab, cot, normed, own, other, w2, wo, cotw, ub, (dbm, dcm), dyb, blk, mg, gpart, bb, g2s,
-        block_o, sent, shared,
+        meta, wide, tokf, etab, cot, normed, lambda cols: window(hse, cols), lambda cols: window(hso, cols),
+        w2, wo, cotw, ub, (dbm, dcm), dyb, blk, mg, gpart, bb, sent, shared,
     )
+    block_out = take_half(stream, blk, block_h, out_sem.at[0])
+    for c in loads:
+        c.wait()
+
+    def prep(rev):
+        def tile(i, _):
+            base = pl.multiple_of(i * 32, 32)
+            rows = pl.ds(base, 32)
+            here = lab[pl.ds(base + HALO, 32), :]
+            before = lab[pl.ds(base + HALO + (1 if rev else -1), 32), :]
+            cut = jnp.where(here == before, 0.0, CUT)
+            spread_tile(p, ROW_C, bb, base)
+            for c in range(G6):
+                dm[c, rows, :] = dl[c, rows, :] + cut
+            return 0
+
+        lax.fori_loop(0, R // 32, tile, 0)
+
+    @pl.when(stream == 0)
+    def _():
+        prep(False)
+
+    @pl.when(stream == 1)
+    def _():
+        prep(True)
+
+    col = lax.broadcasted_iota(jnp.int32, (128, 256), 1)
+    row = lax.broadcasted_iota(jnp.int32, (128, 256), 0)
+    spread_b = jnp.where(row == ROW_B + col % N, 1.0, 0.0).astype(BF)
+    diag = (
+        lax.broadcasted_iota(jnp.int32, (592, 256), 0) % N
+        == lax.broadcasted_iota(jnp.int32, (592, 256), 1) // N
+    )
+    for h in range(2):
+        rows = slice(h * 592, h * 592 + 592)
+        bbd[rows, :] = jnp.where(diag, dot(p[rows, :].astype(BF), spread_b), 0.0).astype(BF)
     for k in range(3):
         sent(k).wait()
-    for c in loads:
-        c.wait()
+    block_out()
+    sums[...] = jnp.zeros(sums.shape, F32)
 
     for s, lowref, highref in ((0, mg, mgx), (1, mgx, mg)):
 
@@ -611,56 +744,17 @@
                     highrow = highref[pl.ds(highat, 32), cols].astype(F32)
                     v = jnp.where(base < WIN, lowrow, 0.0) + jnp.where(base >= WBASE, highrow, 0.0)
                     dy[c, pl.ds(base, 32), :] = v
-                    dyb[pl.ds(base, 32), cols] = v.astype(BF)
+                    t = v * act[c, pl.ds(base, 32), :]
+                    sums[0, :, cols] += t[0:8] + t[8:16] + t[16:24] + t[24:32]
                 return 0
 
             lax.fori_loop(0, R // 32, lay, 0)
 
-    sums[...] = jnp.zeros(sums.shape, F32)
-
-    def prep(rev):
-        def tile(i, _):
-            base = pl.multiple_of(i * 32, 32)
-            rows = pl.ds(base, 32)
-            here = lab[pl.ds(base + HALO, 32), :]
-            before = lab[pl.ds(base + HALO + (1 if rev else -1), 32), :]
-            cut = jnp.where(here == before, 0.0, CUT)
-            real = jnp.where(here >= -1, 1.0, 0.0)
-            for c in range(G6):
-                cols = slice(c * 128, c * 128 + 128)
-                dm[c, rows, :] = dl[c, rows, :] + cut
-                a = act[c, rows, :]
-                ub[rows, cols] = (dl[c, rows, :] * a * real).astype(BF)
-                t = dy[c, rows, :] * a
-                sums[0, :, cols] += t[0:8] + t[8:16] + t[16:24] + t[24:32]
-            return 0
-
-        lax.fori_loop(0, R // 32, tile, 0)
-
-    @pl.when(stream == 0)
-    def _():
-        prep(False)
-
-    @pl.when(stream == 1)
-    def _():
-        prep(True)
-
-    col = lax.broadcasted_iota(jnp.int32, (128, 256), 1)
-    row = lax.broadcasted_iota(jnp.int32, (128, 256), 0)
-    spread_b = jnp.where(row == ROW_B + col % N, 1.0, 0.0).astype(BF)
-    diag = (
-        lax.broadcasted_iota(jnp.int32, (592, 256), 0) % N
-        == lax.broadcasted_iota(jnp.int32, (592, 256), 1) // N
-    )
-    for h in range(2):
-        rows = slice(h * 592, h * 592 + 592)
-        bbd[rows, :] = jnp.where(diag, dot(p[rows, :].astype(BF), spread_b), 0.0).astype(BF)
-    fill_broadcast(p, ROW_C, bb)
     i = lax.broadcasted_iota(jnp.int32, (32, 256), 0)
     j = lax.broadcasted_iota(jnp.int32, (32, 256), 1)
     sel[...] = jnp.where(i == jnp.where(i < N, j // N, N + j % N), 1.0, 0.0).astype(BF)
     dacc[...] = jnp.zeros(dacc.shape, F32)
-    hs, gs, zz = (hse, hso), (g0, g1), (z0, z1)
+    hs, gs, zz, pb, pc = (hse, hso), (g0, g1), (z0, z1), (pb0, pb1), (pc0, pc1)
 
     def load(k, i):
         slot = i % RING
@@ -693,18 +787,22 @@
             dacc[c] += jnp.where(first, 0.0, y[N:, :128])
             dacc[c + 1] += jnp.where(first, 0.0, y[N:, 128:])
 
+        ones = jnp.ones((N, 128), BF)
+
         def b_dot(t, k):
             rows = rows16(block_of(t))
-            dbm[rows, :] = jnp.where(block_diag, dot_nt(ub[rows, :], gs[k][...]), 0.0).astype(BF)
-
-        def c_dot(t, k, slot):
+            dbm[rows, :] = jnp.where(block_diag, dot_nt(ones, pb[k][...]), 0.0).astype(BF)
+
+        def c_dot(t, k):
             rows = rows16(block_of(t))
-            dcm[rows, :] = jnp.where(block_diag, dot_nt(dyb[rows, :], hs[k][slot]), 0.0).astype(BF)
+            dcm[rows, :] = jnp.where(block_diag, dot_nt(ones, pc[k][...]), 0.0).astype(BF)
 
         def block(t, k, slot, pslot, carry, late):
             b = block_of(t)
             carry = list(carry)
             late = list(late)
+            start = 0 if rev else 15
+            now = [hs[k][slot, start * N : start * N + N, c * 128 : c * 128 + 128] for c in range(G6)]
             for n, j in enumerate(range(16) if rev else range(15, -1, -1)):
                 if n % 2 == 0 and late:
                     late.pop(0)()
@@ -716,15 +814,26 @@
                 else:
                     jp = 0 if rev else 15
                     old_ref, old_slot = hs[1 - k], pslot
+                sum_b = sum_c = None
                 for c in range(G6):
                     cols = slice(c * 128, c * 128 + 128)
                     w = dm[c, pl.ds(q, 1), :] * rate[c]
                     fade = jnp.exp2(w)
-                    g = cb * dy[c, pl.ds(q, 1), :] + carry[c]
+                    up = dy[c, pl.ds(q, 1), :]
+                    g = cb * up + carry[c]
                     carry[c] = fade * g
                     old = old_ref[old_slot, jp * N : jp * N + N, cols]
-                    gs[k][j * N : j * N + N, cols] = g.astype(BF)
+                    low = g.astype(BF)
+                    gs[k][j * N : j * N + N, cols] = low
                     zz[k][j * N : j * N + N, cols] = (w * carry[c]).astype(BF) * old
+                    drive = dl[c, pl.ds(q, 1), :] * act[c, pl.ds(q, 1), :]
+                    tb = low * jnp.broadcast_to(drive, (N, 128)).astype(BF)
+                    tc = now[c] * jnp.broadcast_to(up, (N, 128)).astype(BF)
+                    sum_b = tb if sum_b is None else sum_b + tb
+                    sum_c = tc if sum_c is None else sum_c + tc
+                    now[c] = old
+                pb[k][j * N : j * N + N, :] = sum_b
+                pc[k][j * N : j * N + N, :] = sum_c
             return tuple(carry)
 
         def pair(ii, carry):
@@ -747,9 +856,9 @@
                 t = 2 * i + k
                 after = jnp.minimum(t + 1, NB - 1)
                 first = t + 1 > NB - 1
-                late = [functools.partial(drive_dot, after, 1 - k, c) for c in (0, 2, 4)]
+                late = [functools.partial(b_dot, after, 1 - k), functools.partial(c_dot, after, 1 - k)]
+                late += [functools.partial(drive_dot, after, 1 - k, c) for c in (0, 2, 4)]
                 late += [functools.partial(step_dot, after, 1 - k, c, first) for c in (0, 2, 4)]
-                late += [functools.partial(b_dot, after, 1 - k), functools.partial(c_dot, t, k, slot)]
                 ps = slot if k == 1 else pslot
                 carry = lax.fori_loop(
                     0, one, lambda _, cc, t=t, k=k, ps=ps, late=late: block(t, k, slot, ps, cc, late), carry
@@ -761,13 +870,14 @@
             load(1, i).start()
         load(0, NP - 1).wait()
         load(1, NP - 1).wait()
-        g0[...] = jnp.zeros((256, E), BF)
-        z0[...] = jnp.zeros((256, E), BF)
+        for ref in (g0, z0, pb0, pc0):
+            ref[...] = jnp.zeros(ref.shape, BF)
         lax.fori_loop(0, NP, pair, tuple(jnp.zeros((N, 128), F32) for _ in range(G6)))
         for c in (0, 2, 4):
             drive_dot(0, 0, c)
             step_dot(0, 0, c, False)
         b_dot(0, 0)
+        c_dot(0, 0)
 
     @pl.when(stream == 0)
     def _():
@@ -857,21 +967,19 @@
         src_ref=nsend, dst_ref=nrecv, send_sem=swsend.at[0], recv_sem=swrecv.at[0], **partner
     )
     nswap.start()
-    for c in g2:
-        c.wait()
-    for r in range(0, g2_o.shape[0], 24):
-        rows = slice(r, min(r + 24, g2_o.shape[0]))
-        total = g2s[place, :, :].astype(F32)[rows]
-        for k in range(1, wide):
-            total = total + g2r[k].astype(F32)[rows]
-        g2_o[rows, :] = total
-    g2swap = pltpu.make_async_remote_copy(
-        src_ref=g2_o, dst_ref=g2x_o, send_sem=swsend.at[1], recv_sem=swrecv.at[1], **partner
-    )
-    g2swap.start()
-    gpart[...] += dot_nt(dyb[pl.ds(wbase, WIN), :], w1[...])
     for c in range(0, D, 128):
-        gw1_o[c : c + 128, :] = dot_tn(normed[:, c : c + 128], dyb[...])
+        gw1[c : c + 128, :] = dot_tn(normed[:, c : c + 128], dyb[...])
+    if mine:
+        for s in range(2):
+
+            @pl.when(stream == s)
+            def _():
+                pout[...] = gw1[:, (1 - s) * D : (2 - s) * D].astype(BF)
+
+        pre = pltpu.make_async_remote_copy(
+            src_ref=pout, dst_ref=pin, send_sem=swsend.at[1], recv_sem=swrecv.at[1], **partner
+        )
+        pre.start()
     low = p[0:R, :].astype(BF)
     gstep = dot_tn(low, ub[...])[0:RANK]
 
@@ -900,15 +1008,75 @@
     gt = jnp.concatenate(
         [top[0:RANK], gb, gc, gstep, gdecay, chan, jnp.zeros((128 - 108, E), F32)], 0
     )
-    gs_o[...] = gt.T
-
-
+    gsm[...] = gt.T
+    if mine:
+        pre.wait()
+        fill_owners(stream, wide, gsm, gw1, pin, out)
+        shares = [
+            pltpu.make_async_remote_copy(
+                src_ref=out.at[place ^ k], dst_ref=got.at[k], send_sem=rsend.at[k], recv_sem=rrecv.at[k],
+                device_id=(stream, place ^ k), device_id_type=MESH,
+            )
+            for k in range(1, wide)
+        ]
+        for c in shares:
+            c.start()
+    gpart[...] += dot_nt(dyb[pl.ds(wbase, WIN), :], w1[...])
     nswap.wait()
-    ending(meta, wide, tok, etab, cot, nrecv, gpart, st, zs.at[0:3], zs.at[3:6], dd.at[0:3], gain_s, acc, tg_o, gg_o)
+    ending(meta, wide, tok, etab, cot, nrecv, gpart, st, zs.at[0:3], zs.at[3:6], dd.at[0:3], gain_s, acc)
+    token_out = take_half(stream, dd.at[0:3], tg_h, out_sem.at[1])
+    if not mine:
+        gg_o[...] = acc[...]
+        token_out()
+        return
+    gain = jnp.sum(acc[...], axis=0, keepdims=True)
+    each = D // wide
+    for k in range(wide):
+        piece = jnp.broadcast_to(gain[:, k * each : (k + 1) * each], (16, each))
+        gout[k] = jnp.concatenate([piece, jnp.zeros((16, 128 - each), F32)], 1).astype(BF)
+    gains = [
+        pltpu.make_async_remote_copy(
+            src_ref=gout.at[place ^ k], dst_ref=gin.at[k], send_sem=osend.at[k], recv_sem=orecv.at[k],
+            device_id=(stream, place ^ k), device_id_type=MESH,
+        )
+        for k in range(1, wide)
+    ]
+    for c in gains:
+        c.start()
+    for c in g2:
+        c.wait()
+    for r in range(0, g2_o.shape[0], 24):
+        rows = slice(r, r + 24)
+        total = g2s[place].astype(F32)[rows]
+        for k in range(1, wide):
+            total = total + g2r[k].astype(F32)[rows]
+        g2_o[rows, :] = total
+    g2swap = pltpu.make_async_remote_copy(
+        src_ref=g2_o, dst_ref=g2x_o, send_sem=swsend.at[2], recv_sem=swrecv.at[2], **partner
+    )
+    g2swap.start()
+    for c in shares:
+        c.wait()
+    total = out[place].astype(F32)
+    for k in range(1, wide):
+        total = total + got[k].astype(F32)
+    own_o[...] = total
+    for c in gains:
+        c.wait()
+    total = gout[place].astype(F32)
+    for k in range(1, wide):
+        total = total + gin[k].astype(F32)
+    own_o[PACK - 8 : PACK, :] = total[0:8]
+    last = pltpu.make_async_remote_copy(
+        src_ref=own_o, dst_ref=twin_o, send_sem=swsend.at[3], recv_sem=swrecv.at[3], **partner
+    )
+    last.start()
+    token_out()
     g2swap.wait()
-
-
-def ending(meta, wide, tok, etab, cot, other, gpart, st, tokf, cotw, out, gain_s, acc, tg_o, gg_o):
+    last.wait()
+
+
+def ending(meta, wide, tok, etab, cot, other, gpart, st, tokf, cotw, out, gain_s, acc):
     stream = meta[4]
     wbase = pl.multiple_of(stream * WBASE, 32)
     lay_tokens(tok, tokf)
@@ -917,8 +1085,8 @@
     acc[...] = jnp.zeros(acc.shape, F32)
     lo = stream * HALF
 
-    def tile(i, _):
-        base = pl.multiple_of(i * 32, 32)
+    def tile(i):
+        base = i * 32 if isinstance(i, int) else pl.multiple_of(i * 32, 32)
         at = pl.multiple_of(wbase + base, 32)
         rows = pl.ds(base, 32)
         res, _l = residual_tile(meta, tokf, etab, at, 32)
@@ -937,46 +1105,49 @@
         mean = sum(jnp.sum(a * b, axis=1, keepdims=True) for a, b in zip(ng, un)) * (1.0 / D)
         for c in range(3):
             out[c, rows, :] = cotw[c, rows, :] + scale * (ng[c] - un[c] * mean)
-        return 0
-
-    lax.fori_loop(0, WIN // 32, tile, 0)
-    gg_o[...] = acc[...]
-    take_half(stream, out, tg_o)
-
-
-def backward(wide, count, offset, stride, tok, cot, normed, own, other, pack, stats, w1, st, x, act, dl, p, hs):
+
+    pairs(WIN // 32, tile)
+
+
+def backward(wide, mine, *args):
     S = jax.ShapeDtypeStruct
     V = pltpu.VMEM
+    dma = pltpu.SemaphoreType.DMA
     big = V((G6, R, 128), F32)
-    own_rows = pack.shape[1]
+    rows = 2 * D // wide
+    half = S((HALF, 1, D), F32)
+    if mine:
+        outs = [S((PACK, 128), F32), S((PACK, 128), F32), S((rows, E), F32), S((rows, E), F32)]
+        links = [
+            V((wide, rows, E), BF), V((wide, rows, E), BF), V((D, E), F32), V((E, 128), F32), V((D, D), BF), V((D, D), BF),
+            V((wide, PACK, 128), BF), V((wide, PACK, 128), BF), V((wide, 16, 128), BF), V((wide, 16, 128), BF),
+        ] + [dma((wide,))] * 6
+    else:
+        outs = [S((D, E), F32), S((E, 128), F32), S((8, D), F32), S((wide, rows, E), F32)]
+        links = []
     return pl.pallas_call(
-        functools.partial(bwd_kernel, wide),
-        out_shape=[
-            S((HALF, D), F32), S((HALF, D), F32), S((D, E), F32), S((E, 128), F32), S((8, D), F32),
-            S((own_rows, E), F32), S((own_rows, E), F32),
-        ],
-        in_specs=[SMEM] * 3 + [VMEM] * 9 + [ANY] * 5,
-        out_specs=[VMEM] * 7,
+        functools.partial(bwd_kernel, wide, mine),
+        out_shape=[half, half] + outs,
+        in_specs=[SMEM] * 3 + [VMEM] * 7 + [ANY] * 7,
+        out_specs=[ANY] * 2 + [VMEM] * 4,
         scratch_shapes=[
             V((G6, XR, 128), F32), big, big, V((1280, 128), F32),
-            V((D, E), BF), V((E, D), BF), V((WIN, D), F32), V((WIN, E), BF), V((WIN, E), BF),
-            V((wide, own_rows, E), BF), V((wide, own_rows, E), BF), V((WIN, D), BF),
+            V((D, E), BF), V((E, D), BF), V((WIN, D), F32), V((WIN, E), BF), V((WIN, E), BF), V((WIN, D), BF),
             V((XR, 128), jnp.int32), big, big, V((R, E), BF), V((R, E), BF), V((R * N, 128), F32),
             V((R, 256), BF), V((R, 256), BF), V((R, 256), BF), V((G6, XR, 128), F32), big, V((G6, N, 128), F32),
             V((RING, 256, E), BF), V((RING, 256, E), BF),
-            V((256, E), BF), V((256, E), BF), V((256, E), BF), V((256, E), BF), V((32, 256), BF), V((7, 8, E), F32),
+            V((256, E), BF), V((256, E), BF), V((256, E), BF), V((256, E), BF),
+            V((256, 128), BF), V((256, 128), BF), V((256, 128), BF), V((256, 128), BF), V((32, 256), BF), V((7, 8, E), F32),
             V((8, D), F32), V((8, D), F32), V((8, D), F32),
-            pltpu.SemaphoreType.DMA((2, RING)), pltpu.SemaphoreType.DMA((4,)),
-            pltpu.SemaphoreType.DMA((3,)), pltpu.SemaphoreType.DMA((3,)),
-            pltpu.SemaphoreType.DMA((wide,)), pltpu.SemaphoreType.DMA((wide,)),
-            pltpu.SemaphoreType.DMA((2,)), pltpu.SemaphoreType.DMA((2,)),
-        ],
+            dma((2, RING)), dma((4,)), dma((2, 3)), dma((3,)), dma((3,)), dma((4,)), dma((4,)), dma((2, 3)),
+        ]
+        + links,
         compiler_params=pltpu.CompilerParams(
             vmem_limit_bytes=63 * 2**20, collective_id=4, has_side_effects=True
         ),
         cost_estimate=pl.CostEstimate(flops=int(9e10), bytes_accessed=1 << 20, transcendentals=0),
         name="backward",
-    )(count, offset, stride, tok, cot, normed, own, other, pack, stats, w1, st, x, act, dl, p, hs)
+    )(*args)
 
 
 PACK = 128
@@ -992,14 +1163,13 @@
     pl.semaphore_wait(bar, wide)
 
 
-def gather_kernel(
-    wide, inp, state, step, decay, chan, gain, w1_o, s_o, stage, mine, got, send, recv, psend, precv
-):
-    d, w = lax.axis_index("dir"), lax.axis_index("wide")
+def fill_shares(d, given, stage, first, second):
+    inp, out, state, step, decay, chan, gain = given
     stage[...] = jnp.zeros(stage.shape, F32)
     stage[ROW_STEP:ROW_DECAY, 0:ROWS_S] = step[0]
     stage[ROW_DECAY:ROW_CHAN, 0:ROWS_S] = decay[0]
-    stage[ROW_CHAN:ROW_GAIN, 0:ROWS_S] = chan[0]
+    for k in range(7):
+        stage[ROW_CHAN + k : ROW_CHAN + k + 1, 0:ROWS_S] = chan[k]
     stage[ROW_GAIN : ROW_GAIN + 1, 0:ROWS_W] = gain[...]
     small = stage[...].T[0:ROWS_S]
     stage[0:ROWS_S, 0:ROW_STEP] = state[0]
@@ -1009,22 +1179,14 @@
         low, high = inp[:, c * 128 : c * 128 + 128], inp[:, D + c * 128 : D + c * 128 + 128]
         parts.append(jnp.where(d == 0, low, high))
     parts.append(jnp.zeros((PACK - ROWS_S - 3 * ROWS_W, 128), F32))
-    mine[...] = jnp.concatenate(parts, 0).astype(BF)
-    got[w] = mine[...]
-    greet(d, w, wide)
-    copies = []
-    for k in range(1, wide):
-        copies.append(
-            pltpu.make_async_remote_copy(
-                src_ref=mine, dst_ref=got.at[w], send_sem=send.at[k], recv_sem=recv.at[k],
-                device_id=(d, w ^ k), device_id_type=MESH,
-            )
-        )
-        copies[-1].start()
-    for c in copies:
-        c.wait_recv()
+    first[...] = jnp.concatenate(parts, 0).astype(BF)
+    pair = jnp.concatenate([out[0:ROWS_W, :], out[ROWS_W : 2 * ROWS_W, :]], 1)
+    second[...] = jnp.concatenate([inp[:, E:], pair], 0).astype(BF)
+
+
+def take_shares(d, wide, got, w1, s_ref):
     for k in range(0, wide, 2):
-        s_o[k * ROWS_S : (k + 2) * ROWS_S, :] = jnp.concatenate([got[k, 0:ROWS_S], got[k + 1, 0:ROWS_S]], 0)
+        s_ref[k * ROWS_S : (k + 2) * ROWS_S, :] = jnp.concatenate([got[k, 0:ROWS_S], got[k + 1, 0:ROWS_S]], 0)
         v = [got[k + i, ROWS_S:PACK, :].astype(F32) for i in range(2)]
         for c in range(3):
             piece = [t[c * ROWS_W : (c + 1) * ROWS_W] for t in v]
@@ -1034,63 +1196,13 @@
                 @pl.when(d == s)
                 def _():
                     at = s * D + c * 128
-                    w1_o[k * ROWS_W : (k + 2) * ROWS_W, at : at + 128] = piece
-
-    cols = pl.ds(pl.multiple_of(d * D, 128), D)
-    half = pltpu.make_async_remote_copy(
-        src_ref=w1_o.at[:, cols], dst_ref=w1_o.at[:, cols], send_sem=psend, recv_sem=precv,
-        device_id=(1 - d, w), device_id_type=MESH,
-    )
-    half.start()
-    for c in copies:
-        c.wait_send()
-    half.wait()
-
-
-def gather(wide, inp, state, step, decay, chan, gain):
-    S = jax.ShapeDtypeStruct
-    return pl.pallas_call(
-        functools.partial(gather_kernel, wide),
-        out_shape=[S((D, E), BF), S((E, 128), BF)],
-        in_specs=[VMEM] * 6,
-        out_specs=[VMEM] * 2,
-        scratch_shapes=[
-            pltpu.VMEM((128, 128), F32), pltpu.VMEM((PACK, 128), BF), pltpu.VMEM((wide, PACK, 128), BF),
-            pltpu.SemaphoreType.DMA((wide,)), pltpu.SemaphoreType.DMA((wide,)),
-            pltpu.SemaphoreType.DMA, pltpu.SemaphoreType.DMA,
-        ],
-        compiler_params=pltpu.CompilerParams(collective_id=1, has_side_effects=True),
-        name="gather",
-    )(inp, state, step, decay, chan, gain)
-
-
-def reduce_kernel(
-    wide, gw1, gs, gg, own_o, other_o,
-    pout, pin, out, got, gcol, send, recv, psend, precv, fsend, frecv,
-):
-    d, w = lax.axis_index("dir"), lax.axis_index("wide")
-    greet(d, w, wide)
-    for s in range(2):
-
-        @pl.when(d == s)
-        def _():
-            pout[...] = gw1[:, (1 - s) * D : (2 - s) * D].astype(BF)
-
-    pre = pltpu.make_async_remote_copy(
-        src_ref=pout, dst_ref=pin, send_sem=psend, recv_sem=precv,
-        device_id=(1 - d, w), device_id_type=MESH,
-    )
-    pre.start()
-    gcol[...] = gg[...].T
-    pre.wait()
-    copies = []
-    lane = lax.broadcasted_iota(jnp.int32, (ROWS_S, 128), 1)
+                    w1[k * ROWS_W : (k + 2) * ROWS_W, at : at + 128] = piece
+
+
+def fill_owners(d, wide, gs, gw1, pin, out):
     for k in range(wide):
         rows = slice(k * ROWS_W, (k + 1) * ROWS_W)
-        g = jnp.sum(gcol[rows, :], axis=1, keepdims=True)
-        g = jnp.concatenate([g, jnp.zeros((ROWS_S - ROWS_W, 1), F32)], 0)
-        small = jnp.where(lane == ROW_GAIN, g, gs[k * ROWS_S : (k + 1) * ROWS_S, :])
-        parts = [small]
+        parts = [gs[k * ROWS_S : (k + 1) * ROWS_S, :]]
         at = k * ROWS_W % 16
         base = k * ROWS_W - at
         arrived = pin[base : base + 32, :].astype(F32)[at : at + ROWS_W]
@@ -1099,44 +1211,6 @@
             parts.append(jnp.where(d == 0, low, high) + arrived[:, c * 128 : c * 128 + 128])
         parts.append(jnp.zeros((PACK - ROWS_S - 3 * ROWS_W, 128), F32))
         out[k] = jnp.concatenate(parts, 0).astype(BF)
-    for k in range(1, wide):
-        copies.append(
-            pltpu.make_async_remote_copy(
-                src_ref=out.at[w ^ k], dst_ref=got.at[k], send_sem=send.at[k], recv_sem=recv.at[k],
-                device_id=(d, w ^ k), device_id_type=MESH,
-            )
-        )
-        copies[-1].start()
-    for c in copies:
-        c.wait()
-    total = out[w].astype(F32)
-    for k in range(1, wide):
-        total = total + got[k].astype(F32)
-    own_o[...] = total
-    last = pltpu.make_async_remote_copy(
-        src_ref=own_o, dst_ref=other_o, send_sem=fsend, recv_sem=frecv,
-        device_id=(1 - d, w), device_id_type=MESH,
-    )
-    last.start()
-    last.wait()
-
-
-def reduce(wide, gw1, gs, gg):
-    S = jax.ShapeDtypeStruct
-    return pl.pallas_call(
-        functools.partial(reduce_kernel, wide),
-        out_shape=[S((PACK, 128), F32), S((PACK, 128), F32)],
-        in_specs=[VMEM] * 3,
-        out_specs=[VMEM] * 2,
-        scratch_shapes=[
-            pltpu.VMEM((D, D), BF), pltpu.VMEM((D, D), BF), pltpu.VMEM((wide, PACK, 128), BF),
-            pltpu.VMEM((wide, PACK, 128), BF), pltpu.VMEM((D, 8), F32),
-            pltpu.SemaphoreType.DMA((wide,)), pltpu.SemaphoreType.DMA((wide,)),
-        ]
-        + [pltpu.SemaphoreType.DMA] * 4,
-        compiler_params=pltpu.CompilerParams(collective_id=2, has_side_effects=True),
-        name="reduce",
-    )(gw1, gs, gg)
 
 
 def gather_plain(inp, state, step, decay, chan, gain):
@@ -1191,8 +1265,7 @@
     step(1, shared[ROWS_W:, 0:D], (slice(0, ROWS_W), slice(None)))
     step(1, shared[ROWS_W:, D:], (slice(ROWS_W, 2 * ROWS_W), slice(None)))
     t = mine.T
-    gain = t[ROW_GAIN : ROW_GAIN + 1, 0:ROWS_W] + theirs.T[ROW_GAIN : ROW_GAIN + 1, 0:ROWS_W]
-    step(2, gain)
+    step(2, mine[PACK - 8 : PACK - 7, 0:ROWS_W] + theirs[PACK - 8 : PACK - 7, 0:ROWS_W])
     step(3, mine[0:ROWS_S, 0:ROW_STEP], (0,))
     step(4, t[ROW_STEP:ROW_DECAY, 0:ROWS_S], (0,))
     step(5, t[ROW_DECAY:ROW_CHAN, 0:ROWS_S], (0,))
@@ -1240,31 +1313,32 @@
 
 
 def local(tokens, cotangent, view_counts, view_strides, view_offsets, *masters):
-    stream = lax.axis_index("dir")
     wide = lax.axis_size("wide")
-    in_proj, out_proj, norm_gain = masters[0], masters[3], masters[6]
-    drow, erow = in_proj.shape[0], out_proj.shape[0]
+    in_proj, out_proj, gain = masters[0], masters[3], masters[6]
+    erow = out_proj.shape[0]
     mine = E // wide == ROWS_S and D // wide == ROWS_W
-    out_pair = jnp.concatenate([out_proj[: erow // 2], out_proj[erow // 2 :]], 1)
-    pack = jnp.concatenate([in_proj[:, E:], out_pair], 0).astype(BF)
-    pack = lax.all_gather(pack, "wide", axis=0)
-    weights = (in_proj, masters[9], masters[12], masters[15], masters[18])
-    if mine:
-        w1, s = gather(wide, *weights, norm_gain[None])
-    else:
-        w1, s = gather_plain(*weights, norm_gain)
     about = (view_counts, view_offsets, view_strides)
     tok, cot = tokens[0], cotangent[0]
-    normed, x, act, dl, p, st, res, other, stats, hs = forward(wide, *about, tok, w1, s)
-    own = lax.dynamic_slice_in_dim(res, stream * WBASE, WIN, 0)
-    block, token_grad, gw1, gs, gg, g2, g2x = backward(
-        wide, *about, tok, cot, normed, own, other, pack, stats, w1, st, x, act, dl, p, hs
+    small = masters[9], masters[12], masters[15]
+    if mine:
+        chan = jnp.transpose(masters[18], (1, 0, 2))
+        *kept, pack, stats, hs = forward(wide, mine, *about, tok, in_proj, out_proj, *small, chan, gain[None])
+    else:
+        pair = jnp.concatenate([out_proj[: erow // 2], out_proj[erow // 2 :]], 1)
+        pack = lax.all_gather(jnp.concatenate([in_proj[:, E:], pair], 0).astype(BF), "wide", axis=0)
+        given = gather_plain(in_proj, *small, masters[18], gain)
+        *kept, stats, hs = forward(wide, mine, *about, tok, *given)
+    normed, x, act, dl, p, st, res, other, w1 = kept
+    block, token_grad, *sums = backward(
+        wide, mine, *about, tok, cot, normed, pack, stats, w1, st, res, other, x, act, dl, p, hs
     )
     if mine:
-        stats, outs = update(*reduce(wide, gw1, gs, gg), g2, g2x, masters)
+        stats, outs = update(*sums, masters)
     else:
-        stats, outs = update_plain(gw1, gs, gg, g2 + g2x, masters)
-    return (block[None], token_grad[None], stats, *outs)
+        gw1, gs, gg, g2 = sums
+        g2 = lax.psum(lax.psum_scatter(g2, "wide", scatter_dimension=0, tiled=True)[0], "dir")
+        stats, outs = update_plain(gw1, gs, gg, g2, masters)
+    return (jnp.transpose(block, (1, 0, 2)), jnp.transpose(token_grad, (1, 0, 2)), stats, *outs)
 
 
 def solution(mesh):

time: 204 us -> 166 us (0.81)
  Pallas kernels: 177 us -> 161 us
  between operations: 14.8 us -> 1.34 us
  local copies, waits for them, and re-layouts: 9.54 us -> 3.63 us
  other arithmetic: 2.43 us -> 0 us
    pallas_call x4 -> x2, Pallas kernels: 174 us -> 158 us  [the longest x1 96.1 us: backward(): pl.pallas_call(functools.partial(bwd_kernel, wide, mine), out_shape=[half...]
    unnamed x3 -> x4, local copies, waits for them, and re-layouts: 7.32 us -> 3.63 us
    dynamic_slice x1 -> x0, local copies, waits for them, and re-layouts: 2.21 us -> none  [local(): own = lax.dynamic_slice_in_dim(res, stream * WBASE, WIN, 0)]
  transfers between devices with their start and end apart: 1 -> 0, of which waited for: 0 -> 0; matrix products, arithmetic and copies ran while one was open for 2% -> 0% of each run, Pallas kernels for 34% -> 0%
where the time goes in v3:
time: 166 us
  Pallas kernels  161 us (97%)
  local copies, waits for them, and re-layouts  3.63 us (2%)
    pallas_call x1, Pallas kernels, backward(): pl.pallas_call(functools.partial(bwd_kernel, wide, mine), out_shape=[half...  96.1 us
    pallas_call x1, Pallas kernels, forward(): pl.pallas_call(functools.partial(fwd_kernel, wide, mine), out_shape=[S(*k...  62.3 us
    unnamed x4, local copies, waits for them, and re-layouts  3.63 us

profile of v3, /device:TPU:0, one launch (start us, length us, event | category | flops | bytes accessed | tf_op | source)
XLA Modules:
  0.0 166.1 jit_solution(11703238779418108068)
XLA Ops:
  1.3 62.3 %forward.1 = (bf16[1184,384]{1,0:T(8,128)(2,1)}, f32[6,1200,128]{2,1,0:T(8,128)}, f32[6,1184,128]{2,1,0:T(8,128)}, f32[6,1184,128]{2,1,0:T(8,128)}, f32[1280,128...) custom-call(s32[1]{0:T(128)S(6)} %copy.52.refs_0_, ...), custom_call_target="tpu_custom_call" | custom-call | flops 49999998976 | bytes 1048576 | tf_op jit(solution)/shard_map/forward/pallas_call | solution.py:469
  63.6 96.1 %backward.1 = (f32[588,1,384]{2,1,0:T(1,128)}, f32[588,1,384]{2,1,0:T(1,128)}, f32[128,128]{1,0:T(8,128)}, f32[128,128]{1,0:T(8,128)}, f32[48,768]{1,0:T(8,128)}, /*index=5*/f32[48,768]{1,0:T(8,128)}) custom-call(s32[1]{0:T(128)S(6)} %copy.52.refs_0_, s32[1,3]{1,0:T(1,128)} %refs_1_.4, s32[1,3]{1,0:T(1,128)} %refs_2_.4, bf16[1176,384]{1,0:T(8,128)(2,1)} %bitcast.27, ...), custom_call_target="tpu_custom_call" | custom-call | flops 89999998976 | bytes 1048576 | tf_op jit(solution)/shard_map/backward/pallas_call | solution.py:1128
  159.8 0.0 copy-start
  159.8 2.6 %update.1 = (f32[1,2,48]{2,1,0:T(2,128)}, f32[24,1536]{1,0:T(8,128)}, f32[24,1536]{1,0:T(8,128)}, f32[24,1536]{1,0:T(8,128)}, f32[48,384]{1,0:T(8,128)}, /*index...) custom-call(f32[128,128]{1,0:T(8,128)} %get-tuple-element.78.got, ...), custom_call_target="tpu_custom_call" | custom-call | tf_op jit(solution)/shard_map/update/pallas_call | solution.py:1282
  162.4 2.7 %copy.53 = f32[1,588,384]{2,0,1:T(1,128)} copy(f32[1,588,384]{2,0,1:T(1,128)} %bitcast.17) | data formatting | bytes 1806336
  165.1 0.0 copy-done
  165.1 0.9 copy.54
Async XLA Ops:
  159.8 5.4 %copy-start = (f32[588,1,384]{2,1,0:T(1,128)S(1)}, f32[588,1,384]{2,1,0:T(1,128)}, u32[]{:S(2)}) copy-start(f32[588,1,384]{2,1,0:T(1,128)} %get-tuple-element.77) | copy-start | bytes 2709508

commit v4 on v3

--- a/solution.py
+++ b/solution.py
@@ -123,10 +123,18 @@
     return dot(src, pick)[0:8]
 
 
-def spread_tile(p_ref, lane, out_ref, base):
-    v = p_ref[pl.ds(base, 32), :].T[lane : lane + N]
-    for j in range(32):
-        out_ref[pl.ds(pl.multiple_of((base + j) * N, N), N), :] = jnp.broadcast_to(v[:, j : j + 1], (N, 128))
+def turn(p_ref, lane, out_ref):
+    for sb in range(-(-R // 128)):
+        v = p_ref[sb * 128 : sb * 128 + 128, :].T[lane : lane + N]
+        for k in range(8):
+            if sb * 8 + k < NB:
+                out_ref[sb * 8 + k] = v if k == 0 else pltpu.roll(v, 128 - 16 * k, 1)
+
+
+def spread_tile(turned, b, out_ref):
+    v = turned[b]
+    for j in range(16):
+        out_ref[pl.ds(pl.multiple_of((b * 16 + j) * N, N), N), :] = jnp.broadcast_to(v[:, j : j + 1], (N, 128))
 
 
 def pairs(count, body):
@@ -140,7 +148,7 @@
         body(count - 1)
 
 
-def conv_tile(x_ref, lab_ref, st_ref, c, base, n, rev):
+def conv_tile(x_ref, lab_ref, chan, c, base, n, rev):
     cols = slice(c * 128, c * 128 + 128)
     here = lab_ref[pl.ds(base + HALO, n), :]
     lagged = [x_ref[c, pl.ds(base + HALO, n), :]]
@@ -148,9 +156,9 @@
         at = base + HALO + (j if rev else -j)
         same = lab_ref[pl.ds(at, n), :] == here
         lagged.append(jnp.where(same, x_ref[c, pl.ds(at, n), :], 0.0))
-    total = st_ref[ROW_CHAN + 4 : ROW_CHAN + 5, cols]
+    total = chan[4:5, cols]
     for j in range(4):
-        total = total + st_ref[ROW_CHAN + j : ROW_CHAN + j + 1, cols] * lagged[j]
+        total = total + chan[j : j + 1, cols] * lagged[j]
     return total, lagged
 
 
@@ -180,22 +188,28 @@
     ) = refs[: 12 if mine else 11]
     (
         normed_o, x_o, act_o, dl_o, p_o, st_o, res_o, other_o, w1, al_o, s_ref,
-        lab, dm, u, bb, cbd, hse, hso, gain_s, tokf, etab, sem, out_sem, send, recv, *links,
+        lab, dm, u, cbd, hse, hso, gain_s, tokf, etab, turned, chan_s, sem, out_sem, send, recv, *links,
     ) = refs[12 if mine else 11 :]
     stream, place = lax.axis_index("dir"), lax.axis_index("wide")
     meta = views(count, offset, stream)
     if mine:
-        stage, first, got, second, pack, gsend, grecv, psend, precv, hsem = links
-        fill_shares(stream, given, stage, first, second)
+        stage, first, got, small, gots, second, pack, gsend, grecv, ssend, srecv, psend, precv, hsem = links
+        fill_shares(stream, given, stage, first, small, second)
         got[place] = first[...]
+        gots[place] = small[...]
         pack[place] = second[...]
         greet(stream, place, wide)
-        early, later = [], []
+        early, next_, later = [], [], []
         for k in range(1, wide):
             where = dict(device_id=(stream, place ^ k), device_id_type=MESH)
             early.append(
                 pltpu.make_async_remote_copy(
                     src_ref=first, dst_ref=got.at[place], send_sem=gsend.at[k], recv_sem=grecv.at[k], **where
+                )
+            )
+            next_.append(
+                pltpu.make_async_remote_copy(
+                    src_ref=small, dst_ref=gots.at[place], send_sem=ssend.at[k], recv_sem=srecv.at[k], **where
                 )
             )
             later.append(
@@ -204,6 +218,8 @@
                 )
             )
             early[-1].start()
+        for c in next_:
+            c.start()
     else:
         bar = pltpu.get_barrier_semaphore()
         pl.semaphore_signal(bar, inc=1, device_id=(1 - stream, place), device_id_type=MESH)
@@ -225,19 +241,17 @@
     if mine:
         for c in early:
             c.wait_recv()
-        take_shares(stream, wide, got, w1, s_ref)
+        take_shares(stream, wide, got, w1, chan_s, gain_s)
         cols = pl.ds(pl.multiple_of(stream * D, 128), D)
         half = pltpu.make_async_remote_copy(
             src_ref=w1.at[:, cols], dst_ref=w1.at[:, cols], send_sem=hsem.at[0], recv_sem=hsem.at[1],
             device_id=(1 - stream, place), device_id_type=MESH,
         )
         half.start()
-        for c in early:
-            c.wait_send()
-        for c in later:
-            c.start()
-    st_o[...] = s_ref[...].astype(F32).T
-    gain_s[...] = gain_row(st_o, wide)
+    else:
+        st_o[...] = s_ref[...].astype(F32).T
+        gain_s[...] = gain_row(st_o, wide)
+        chan_s[...] = st_o[ROW_CHAN : ROW_CHAN + 8, :]
     saves = [
         pltpu.make_async_copy(v, h, out_sem.at[k])
         for k, (v, h) in enumerate(
@@ -252,7 +266,7 @@
         base = pl.multiple_of(i * 32, 32)
         for c in range(3):
             cols = slice(c * 128, c * 128 + 128)
-            normed_o[pl.ds(base, 32), cols] = (tokf[c, pl.ds(base, 32), :] * gain_s[0:1, cols]).astype(BF)
+            normed_o[pl.ds(base, 32), cols] = (tokf[c, pl.ds(base, 32), :] * gain_s[7:8, cols]).astype(BF)
         return 0
 
     lax.fori_loop(0, R // 32, norm_tile, 0)
@@ -270,7 +284,7 @@
         def tile(i, _):
             base = pl.multiple_of(i * 32, 32)
             for c in range(G6):
-                total, _l = conv_tile(x_o, lab, st_o, c, base, 32, rev)
+                total, _l = conv_tile(x_o, lab, chan_s, c, base, 32, rev)
                 act = total * sigmoid(total)
                 act_o[c, pl.ds(base, 32), :] = act
                 al_o[pl.ds(base, 32), c * 128 : c * 128 + 128] = act.astype(BF)
@@ -286,6 +300,17 @@
     def _():
         conv(True)
 
+    if mine:
+        for c in next_:
+            c.wait_recv()
+        for k in range(wide):
+            s_ref[k * ROWS_S : (k + 1) * ROWS_S, :] = gots[k]
+        for c in early + next_:
+            c.wait_send()
+        for c in later:
+            c.start()
+        st_o[...] = s_ref[...].astype(F32).T
+        st_o[ROW_CHAN : ROW_CHAN + 8, :] = chan_s[...]
     p_o[R:, :] = jnp.zeros((1280 - R, 128), F32)
     col = lax.broadcasted_iota(jnp.int32, (128, 256), 1)
     row = lax.broadcasted_iota(jnp.int32, (128, 256), 0)
@@ -307,6 +332,7 @@
             dl_o[c, rows, :] = y[:, :128]
             dl_o[c + 1, rows, :] = y[:, 128:]
     stats_o[...] = jnp.zeros(stats_o.shape, F32)
+    turn(p_o, ROW_B, turned)
 
     def soft(rev):
         def tile(i, _):
@@ -316,7 +342,6 @@
             cut = jnp.where(here == before, 0.0, CUT)
             live = jnp.where(here >= 0, 1.0, 0.0)
             real = jnp.where(here >= -1, 1.0, 0.0)
-            spread_tile(p_o, ROW_B, bb, base)
             for c in range(G6):
                 cols = slice(c * 128, c * 128 + 128)
                 rows = pl.ds(base, 32)
@@ -380,12 +405,13 @@
 
         def block(t, k, slot, state, late):
             b = block_of(t)
+            wide_b = turned[b]
             state = list(state)
             for n, j in enumerate(range(15, -1, -1) if rev else range(16)):
                 if n % 4 == 0 and late:
                     late.pop(0)()
                 q = b * 16 + j
-                drive = bb[pl.ds(pl.multiple_of(q * N, N), N), :]
+                drive = jnp.broadcast_to(wide_b[:, j : j + 1], (N, 128))
                 for c in range(G6):
                     fade = jnp.exp2(dm[c, pl.ds(q, 1), :] * rate[c])
                     state[c] = fade * state[c] + u[c, pl.ds(q, 1), :] * drive
@@ -463,8 +489,9 @@
     pack = [((wide, 2 * D // wide, E), BF)] if mine else []
     dma = pltpu.SemaphoreType.DMA
     links = [
-        V((128, 128), F32), V((PACK, 128), BF), V((wide, PACK, 128), BF), V(pack[0][0][1:], BF), V(*pack[0]),
-        dma((wide,)), dma((wide,)), dma((wide,)), dma((wide,)), dma((2,)),
+        V((128, 128), F32), V((ROWS_P, 128), BF), V((wide, ROWS_P, 128), BF), V((ROWS_S, 128), BF),
+        V((wide, ROWS_S, 128), BF), V(pack[0][0][1:], BF), V(*pack[0]),
+        dma((wide,)), dma((wide,)), dma((wide,)), dma((wide,)), dma((wide,)), dma((wide,)), dma((2,)),
     ] if mine else []
     return pl.pallas_call(
         functools.partial(fwd_kernel, wide, mine),
@@ -474,8 +501,8 @@
         scratch_shapes=[V(*k) for k in kept]
         + [
             V((R, E), BF), V((E, 128), BF), V((XR, 128), jnp.int32), V((G6, R, 128), F32), V((G6, R, 128), F32),
-            V((R * N, 128), F32), V((R, 256), BF), V((RING, 256, E), BF), V((RING, 256, E), BF), V((8, D), F32),
-            V((3, R, 128), F32), V((8, D), F32),
+            V((R, 256), BF), V((RING, 256, E), BF), V((RING, 256, E), BF), V((8, D), F32),
+            V((3, R, 128), F32), V((8, D), F32), V((NB, N, 128), F32), V((8, E), F32),
             dma((2, RING)), dma((10,)), dma((SENDS,)), dma((SENDS,)),
         ]
         + links,
@@ -616,10 +643,10 @@
     (
         x, act, dl, p, w2, wo, gpart, mg, mgx, nrecv,
         lab, dm, dy, dyb, ub, bb, bbd, dbm, dcm, dd, zs, dacc, hse, hso, g0, g1, z0, z1, pb0, pb1, pc0, pc1, sel, sums,
-        etab, gain_s, acc, sem, in_sem, out_sem, mgsend, mgrecv, swsend, swrecv, win_sem, *links,
+        etab, gain_s, acc, turned, sem, in_sem, out_sem, mgsend, mgrecv, swsend, swrecv, win_sem, *links,
     ) = refs[23:]
     if mine:
-        g2s, g2r, gw1, gsm, pout, pin, out, got, gout, gin, g2send, g2recv, rsend, rrecv, osend, orecv = links
+        g2s, g2r, gw1, gsm, pout, pin, out, got, sout, sin, gout, gin, *sems = links
     stream, place = lax.axis_index("dir"), lax.axis_index("wide")
     wbase = pl.multiple_of(stream * WBASE, 32)
     loads = [
@@ -666,10 +693,27 @@
         for k in range(1, wide):
             g2.append(
                 pltpu.make_async_remote_copy(
-                    src_ref=g2s.at[place ^ k], dst_ref=g2r.at[k], send_sem=g2send.at[k], recv_sem=g2recv.at[k],
+                    src_ref=g2s.at[place ^ k], dst_ref=g2r.at[k], send_sem=sems[0].at[k], recv_sem=sems[1].at[k],
                     device_id=(stream, place ^ k), device_id_type=MESH,
                 )
             )
+
+    def deal(src, dst, n):
+        return [
+            pltpu.make_async_remote_copy(
+                src_ref=src.at[place ^ k], dst_ref=dst.at[k], send_sem=sems[n].at[k], recv_sem=sems[n + 1].at[k],
+                device_id=(stream, place ^ k), device_id_type=MESH,
+            )
+            for k in range(1, wide)
+        ]
+
+    def collect(copies, src, dst):
+        for c in copies:
+            c.wait()
+        total = src[place].astype(F32)
+        for k in range(1, wide):
+            total = total + dst[k].astype(F32)
+        return total
 
     def shared(rows, pitch):
         for k in range(wide):
@@ -692,6 +736,7 @@
     block_out = take_half(stream, blk, block_h, out_sem.at[0])
     for c in loads:
         c.wait()
+    turn(p, ROW_C, turned)
 
     def prep(rev):
         def tile(i, _):
@@ -700,7 +745,8 @@
             here = lab[pl.ds(base + HALO, 32), :]
             before = lab[pl.ds(base + HALO + (1 if rev else -1), 32), :]
             cut = jnp.where(here == before, 0.0, CUT)
-            spread_tile(p, ROW_C, bb, base)
+            spread_tile(turned, 2 * i, bb)
+            spread_tile(turned, 2 * i + 1, bb)
             for c in range(G6):
                 dm[c, rows, :] = dl[c, rows, :] + cut
             return 0
@@ -916,6 +962,30 @@
             y = dot(sg, w_s[:, cols]) + dot(dbm[rows, :], w_b[:, cols]) + dot(dcm[rows, :], w_c[:, cols])
             dm[c, rows, :] += y[:, :128]
             dm[c + 1, rows, :] += y[:, 128:]
+    low = p[0:R, :].astype(BF)
+    gstep = dot_tn(low, ub[...])[0:RANK]
+
+    def activation(i, _):
+        rows = pl.ds(pl.multiple_of(i * 32, 32), 32)
+        for c in range(G6):
+            ub[rows, c * 128 : c * 128 + 128] = act[c, rows, :].astype(BF)
+        return 0
+
+    lax.fori_loop(0, R // 32, activation, 0)
+    top = dot_tn(pgs[...], ub[...])
+    gb = dot_tn(dbm[...], ub[...])
+    gc = dot_tn(dcm[...], ub[...])
+    gb = sum(gb[k * N : k * N + N] for k in range(N))
+    gc = sum(gc[k * N : k * N + N] for k in range(N))
+    gdecay = jnp.concatenate([dacc[c] for c in range(G6)], 1) * LN2
+    gt = jnp.concatenate([top[0:RANK], gb, gc, gstep, gdecay, jnp.zeros((128 - ROW_CHAN, E), F32)], 0)
+    gsm[...] = gt.T
+    if mine:
+        for k in range(wide):
+            sout[k] = gsm[k * ROWS_S : (k + 1) * ROWS_S, :].astype(BF)
+        smalls = deal(sout, sin, 2)
+        for c in smalls:
+            c.start()
     dc = dd
     dc[:, 0:HALO, :] = jnp.zeros((G6, HALO, 128), F32)
     dc[:, HALO + R : XR, :] = jnp.zeros((G6, HALO, 128), F32)
@@ -925,7 +995,7 @@
             base = pl.multiple_of(i * 32, 32)
             for c in range(G6):
                 cols = slice(c * 128, c * 128 + 128)
-                total, lagged = conv_tile(x, lab, st, c, base, 32, rev)
+                total, lagged = conv_tile(x, lab, st.at[ROW_CHAN : ROW_CHAN + 8], c, base, 32, rev)
                 sig = sigmoid(total)
                 v = dm[c, pl.ds(base, 32), :] * sig * (1.0 + total * (1.0 - sig))
                 dc[c, pl.ds(base + HALO, 32), :] = v
@@ -980,48 +1050,24 @@
             src_ref=pout, dst_ref=pin, send_sem=swsend.at[1], recv_sem=swrecv.at[1], **partner
         )
         pre.start()
-    low = p[0:R, :].astype(BF)
-    gstep = dot_tn(low, ub[...])[0:RANK]
-
-    def activation(i, _):
-        rows = pl.ds(pl.multiple_of(i * 32, 32), 32)
-        for c in range(G6):
-            ub[rows, c * 128 : c * 128 + 128] = act[c, rows, :].astype(BF)
-        return 0
-
-    lax.fori_loop(0, R // 32, activation, 0)
-    top = dot_tn(pgs[...], ub[...])
-    gb = dot_tn(dbm[...], ub[...])
-    gc = dot_tn(dcm[...], ub[...])
-    gb = sum(gb[k * N : k * N + N] for k in range(N))
-    gc = sum(gc[k * N : k * N + N] for k in range(N))
-    gdecay = jnp.concatenate([dacc[c] for c in range(G6)], 1) * LN2
-
     def total(k):
         return jnp.sum(sums[k], axis=0, keepdims=True)
 
-    chan = [total(3 + k) for k in range(4)] + [total(2), total(1), total(0)]
     fine = [jnp.sum(stats[k], axis=0, keepdims=True) * (1.0 / VIEW_TOK) for k in range(2)]
     coarse = [v.astype(BF).astype(F32) for v in fine]
     fine = [a - b for a, b in zip(fine, coarse)]
-    chan = jnp.concatenate(chan + [jnp.zeros((1, E), F32)] + coarse + fine, 0)
-    gt = jnp.concatenate(
-        [top[0:RANK], gb, gc, gstep, gdecay, chan, jnp.zeros((128 - 108, E), F32)], 0
-    )
-    gsm[...] = gt.T
+    chan = [total(3 + k) for k in range(4)] + [total(2), total(1), total(0)]
     if mine:
+        gpart[...] += dot_nt(dyb[pl.ds(wbase, WIN), :], w1[...])
         pre.wait()
-        fill_owners(stream, wide, gsm, gw1, pin, out)
-        shares = [
-            pltpu.make_async_remote_copy(
-                src_ref=out.at[place ^ k], dst_ref=got.at[k], send_sem=rsend.at[k], recv_sem=rrecv.at[k],
-                device_id=(stream, place ^ k), device_id_type=MESH,
-            )
-            for k in range(1, wide)
-        ]
+        fill_owners(stream, wide, gw1, pin, out)
+        shares = deal(out, got, 4)
         for c in shares:
             c.start()
-    gpart[...] += dot_nt(dyb[pl.ds(wbase, WIN), :], w1[...])
+    else:
+        rest = chan + [jnp.zeros((1, E), F32)] + coarse + fine
+        gsm[...] += jnp.concatenate([jnp.zeros((ROW_CHAN, E), F32)] + rest + [jnp.zeros((20, E), F32)], 0).T
+        gpart[...] += dot_nt(dyb[pl.ds(wbase, WIN), :], w1[...])
     nswap.wait()
     ending(meta, wide, tok, etab, cot, nrecv, gpart, st, zs.at[0:3], zs.at[3:6], dd.at[0:3], gain_s, acc)
     token_out = take_half(stream, dd.at[0:3], tg_h, out_sem.at[1])
@@ -1030,17 +1076,14 @@
         token_out()
         return
     gain = jnp.sum(acc[...], axis=0, keepdims=True)
-    each = D // wide
+    rows = jnp.concatenate(chan + [jnp.zeros((1, E), F32)] + coarse + fine + [jnp.zeros((4, E), F32)], 0)
     for k in range(wide):
-        piece = jnp.broadcast_to(gain[:, k * each : (k + 1) * each], (16, each))
-        gout[k] = jnp.concatenate([piece, jnp.zeros((16, 128 - each), F32)], 1).astype(BF)
-    gains = [
-        pltpu.make_async_remote_copy(
-            src_ref=gout.at[place ^ k], dst_ref=gin.at[k], send_sem=osend.at[k], recv_sem=orecv.at[k],
-            device_id=(stream, place ^ k), device_id_type=MESH,
-        )
-        for k in range(1, wide)
-    ]
+        piece = rows[:, k * ROWS_S : (k + 1) * ROWS_S]
+        owned = jnp.concatenate([gain[:, k * ROWS_W : (k + 1) * ROWS_W], jnp.zeros((1, ROWS_S - ROWS_W), F32)], 1)
+        at = lax.broadcasted_iota(jnp.int32, (ROWS_C, ROWS_S), 0)
+        piece = jnp.where(at == 7, jnp.broadcast_to(owned, (ROWS_C, ROWS_S)), piece)
+        gout[k] = jnp.concatenate([piece, jnp.zeros((ROWS_C, 128 - ROWS_S), F32)], 1).astype(BF)
+    gains = deal(gout, gin, 6)
     for c in gains:
         c.start()
     for c in g2:
@@ -1055,18 +1098,9 @@
         src_ref=g2_o, dst_ref=g2x_o, send_sem=swsend.at[2], recv_sem=swrecv.at[2], **partner
     )
     g2swap.start()
-    for c in shares:
-        c.wait()
-    total = out[place].astype(F32)
-    for k in range(1, wide):
-        total = total + got[k].astype(F32)
-    own_o[...] = total
-    for c in gains:
-        c.wait()
-    total = gout[place].astype(F32)
-    for k in range(1, wide):
-        total = total + gin[k].astype(F32)
-    own_o[PACK - 8 : PACK, :] = total[0:8]
+    own_o[0:ROWS_S, :] = collect(smalls, sout, sin)
+    own_o[ROWS_S:AT_C, :] = collect(shares, out, got)
+    own_o[AT_C:PACK, :] = collect(gains, gout, gin)
     last = pltpu.make_async_remote_copy(
         src_ref=own_o, dst_ref=twin_o, send_sem=swsend.at[3], recv_sem=swrecv.at[3], **partner
     )
@@ -1120,8 +1154,9 @@
         outs = [S((PACK, 128), F32), S((PACK, 128), F32), S((rows, E), F32), S((rows, E), F32)]
         links = [
             V((wide, rows, E), BF), V((wide, rows, E), BF), V((D, E), F32), V((E, 128), F32), V((D, D), BF), V((D, D), BF),
-            V((wide, PACK, 128), BF), V((wide, PACK, 128), BF), V((wide, 16, 128), BF), V((wide, 16, 128), BF),
-        ] + [dma((wide,))] * 6
+            V((wide, ROWS_P, 128), BF), V((wide, ROWS_P, 128), BF), V((wide, ROWS_S, 128), BF), V((wide, ROWS_S, 128), BF),
+            V((wide, ROWS_C, 128), BF), V((wide, ROWS_C, 128), BF),
+        ] + [dma((wide,))] * 8
     else:
         outs = [S((D, E), F32), S((E, 128), F32), S((8, D), F32), S((wide, rows, E), F32)]
         links = []
@@ -1138,7 +1173,7 @@
             V((RING, 256, E), BF), V((RING, 256, E), BF),
             V((256, E), BF), V((256, E), BF), V((256, E), BF), V((256, E), BF),
             V((256, 128), BF), V((256, 128), BF), V((256, 128), BF), V((256, 128), BF), V((32, 256), BF), V((7, 8, E), F32),
-            V((8, D), F32), V((8, D), F32), V((8, D), F32),
+            V((8, D), F32), V((8, D), F32), V((8, D), F32), V((NB, N, 128), F32),
             dma((2, RING)), dma((4,)), dma((2, 3)), dma((3,)), dma((3,)), dma((4,)), dma((4,)), dma((2, 3)),
         ]
         + links,
@@ -1150,9 +1185,12 @@
     )(*args)
 
 
-PACK = 128
+ROWS_W = 24
+ROWS_P = 80
 ROWS_S = 48
-ROWS_W = 24
+ROWS_C = 16
+PACK = ROWS_S + ROWS_P + ROWS_C
+AT_C = ROWS_S + ROWS_P
 
 
 def greet(d, w, wide):
@@ -1163,7 +1201,7 @@
     pl.semaphore_wait(bar, wide)
 
 
-def fill_shares(d, given, stage, first, second):
+def fill_shares(d, given, stage, first, small, second):
     inp, out, state, step, decay, chan, gain = given
     stage[...] = jnp.zeros(stage.shape, F32)
     stage[ROW_STEP:ROW_DECAY, 0:ROWS_S] = step[0]
@@ -1171,23 +1209,33 @@
     for k in range(7):
         stage[ROW_CHAN + k : ROW_CHAN + k + 1, 0:ROWS_S] = chan[k]
     stage[ROW_GAIN : ROW_GAIN + 1, 0:ROWS_W] = gain[...]
-    small = stage[...].T[0:ROWS_S]
-    stage[0:ROWS_S, 0:ROW_STEP] = state[0]
-    col = lax.broadcasted_iota(jnp.int32, (ROWS_S, 128), 1)
-    parts = [jnp.where(col < ROW_STEP, stage[0:ROWS_S, :], small)]
+    parts = []
     for c in range(3):
         low, high = inp[:, c * 128 : c * 128 + 128], inp[:, D + c * 128 : D + c * 128 + 128]
         parts.append(jnp.where(d == 0, low, high))
-    parts.append(jnp.zeros((PACK - ROWS_S - 3 * ROWS_W, 128), F32))
-    first[...] = jnp.concatenate(parts, 0).astype(BF)
+    first[...] = jnp.concatenate(parts + [stage[ROW_CHAN : ROW_CHAN + 8, :]], 0).astype(BF)
+    turned = stage[...].T[0:ROWS_S]
+    stage[0:ROWS_S, 0:ROW_STEP] = state[0]
+    col = lax.broadcasted_iota(jnp.int32, (ROWS_S, 128), 1)
+    small[...] = jnp.where(col < ROW_STEP, stage[0:ROWS_S, :], turned).astype(BF)
     pair = jnp.concatenate([out[0:ROWS_W, :], out[ROWS_W : 2 * ROWS_W, :]], 1)
     second[...] = jnp.concatenate([inp[:, E:], pair], 0).astype(BF)
 
 
-def take_shares(d, wide, got, w1, s_ref):
+def take_shares(d, wide, got, w1, chan_s, gain_s):
+    lane = lax.broadcasted_iota(jnp.int32, (8, 128), 1)
+
+    def lay(tiles, piece, at):
+        t, r = divmod(at, 128)
+        moved = pltpu.roll(piece, r, 1) if r else piece
+        tiles[t] = tiles[t] + jnp.where(lane >= r, moved, 0.0)
+        if t + 1 < len(tiles):
+            tiles[t + 1] = tiles[t + 1] + jnp.where(lane < r, moved, 0.0)
+
+    chan = [jnp.zeros((8, 128), F32) for _ in range(E // 128)]
+    gain = [jnp.zeros((8, 128), F32) for _ in range(D // 128)]
     for k in range(0, wide, 2):
-        s_ref[k * ROWS_S : (k + 2) * ROWS_S, :] = jnp.concatenate([got[k, 0:ROWS_S], got[k + 1, 0:ROWS_S]], 0)
-        v = [got[k + i, ROWS_S:PACK, :].astype(F32) for i in range(2)]
+        v = [got[k + i].astype(F32) for i in range(2)]
         for c in range(3):
             piece = [t[c * ROWS_W : (c + 1) * ROWS_W] for t in v]
             piece = jnp.concatenate(piece, 0).astype(BF)
@@ -1198,18 +1246,26 @@
                     at = s * D + c * 128
                     w1[k * ROWS_W : (k + 2) * ROWS_W, at : at + 128] = piece
 
-
-def fill_owners(d, wide, gs, gw1, pin, out):
+        for i in range(2):
+            lay(chan, v[i][3 * ROWS_W : ROWS_P], (k + i) * ROWS_S)
+            lay(gain, v[i][3 * ROWS_W : ROWS_P], (k + i) * ROWS_W)
+    for c, v in enumerate(chan):
+        chan_s[:, c * 128 : c * 128 + 128] = v
+    for c, v in enumerate(gain):
+        gain_s[:, c * 128 : c * 128 + 128] = v
+
+
+def fill_owners(d, wide, gw1, pin, out):
     for k in range(wide):
         rows = slice(k * ROWS_W, (k + 1) * ROWS_W)
-        parts = [gs[k * ROWS_S : (k + 1) * ROWS_S, :]]
+        parts = []
         at = k * ROWS_W % 16
         base = k * ROWS_W - at
         arrived = pin[base : base + 32, :].astype(F32)[at : at + ROWS_W]
         for c in range(3):
             low, high = gw1[rows, c * 128 : c * 128 + 128], gw1[rows, D + c * 128 : D + c * 128 + 128]
             parts.append(jnp.where(d == 0, low, high) + arrived[:, c * 128 : c * 128 + 128])
-        parts.append(jnp.zeros((PACK - ROWS_S - 3 * ROWS_W, 128), F32))
+        parts.append(jnp.zeros((ROWS_P - 3 * ROWS_W, 128), F32))
         out[k] = jnp.concatenate(parts, 0).astype(BF)
 
 
@@ -1264,14 +1320,14 @@
     step(0, shared[0:ROWS_W], (slice(None), slice(E, 2 * E)))
     step(1, shared[ROWS_W:, 0:D], (slice(0, ROWS_W), slice(None)))
     step(1, shared[ROWS_W:, D:], (slice(ROWS_W, 2 * ROWS_W), slice(None)))
-    t = mine.T
-    step(2, mine[PACK - 8 : PACK - 7, 0:ROWS_W] + theirs[PACK - 8 : PACK - 7, 0:ROWS_W])
+    t = mine[0:128].T
+    step(2, mine[AT_C + 7 : AT_C + 8, 0:ROWS_W] + theirs[AT_C + 7 : AT_C + 8, 0:ROWS_W])
     step(3, mine[0:ROWS_S, 0:ROW_STEP], (0,))
     step(4, t[ROW_STEP:ROW_DECAY, 0:ROWS_S], (0,))
     step(5, t[ROW_DECAY:ROW_CHAN, 0:ROWS_S], (0,))
     for k in range(7):
-        step(6, t[ROW_CHAN + k : ROW_CHAN + k + 1, 0:ROWS_S], (k,))
-    outs[0][0] = t[ROW_STATS : ROW_STATS + 2, 0:ROWS_S] + t[ROW_STATS + 2 : ROW_STATS + 4, 0:ROWS_S]
+        step(6, mine[AT_C + k : AT_C + k + 1, 0:ROWS_S], (k,))
+    outs[0][0] = mine[AT_C + 8 : AT_C + 10, 0:ROWS_S] + mine[AT_C + 10 : AT_C + 12, 0:ROWS_S]
 
 
 def update(got, twin, g2, g2x, masters):

time: 166 us -> 154 us (0.928)
  Pallas kernels: 161 us -> 149 us
    pallas_call x1, Pallas kernels: 62.3 us -> 54.1 us  [forward(): pl.pallas_call(functools.partial(fwd_kernel, wide, mine), out_shape=[S(*k...]
    pallas_call x1, Pallas kernels: 96.1 us -> 92.5 us  [backward(): pl.pallas_call(functools.partial(bwd_kernel, wide, mine), out_shape=[half...]
where the time goes in v4:
time: 154 us
  Pallas kernels  149 us (97%)
  local copies, waits for them, and re-layouts  3.63 us (2%)
    pallas_call x1, Pallas kernels, backward(): pl.pallas_call(functools.partial(bwd_kernel, wide, mine), out_shape=[half...  92.5 us
    pallas_call x1, Pallas kernels, forward(): pl.pallas_call(functools.partial(fwd_kernel, wide, mine), out_shape=[S(*k...  54.1 us
    unnamed x4, local copies, waits for them, and re-layouts  3.63 us

profile of v4, /device:TPU:0, one launch (start us, length us, event | category | flops | bytes accessed | tf_op | source)
XLA Modules:
  0.0 154.1 jit_solution(1863238126189001696)
XLA Ops:
  1.3 54.1 %forward.1 = (bf16[1184,384]{1,0:T(8,128)(2,1)}, f32[6,1200,128]{2,1,0:T(8,128)}, f32[6,1184,128]{2,1,0:T(8,128)}, f32[6,1184,128]{2,1,0:T(8,128)}, f32[1280,128...) custom-call(s32[1]{0:T(128)S(6)} %copy.52.refs_0_, ...), custom_call_target="tpu_custom_call" | custom-call | flops 49999998976 | bytes 1048576 | tf_op jit(solution)/shard_map/forward/pallas_call | solution.py:496
  55.4 92.5 %backward.1 = (f32[588,1,384]{2,1,0:T(1,128)}, f32[588,1,384]{2,1,0:T(1,128)}, f32[144,128]{1,0:T(8,128)}, f32[144,128]{1,0:T(8,128)}, f32[48,768]{1,0:T(8,128)}, /*index=5*/f32[48,768]{1,0:T(8,128)}) custom-call(s32[1]{0:T(128)S(6)} %copy.52.refs_0_, s32[1,3]{1,0:T(1,128)} %refs_1_.4, s32[1,3]{1,0:T(1,128)} %refs_2_.4, bf16[1176,384]{1,0:T(8,128)(2,1)} %bitcast.27, ...), custom_call_target="tpu_custom_call" | custom-call | flops 89999998976 | bytes 1048576 | tf_op jit(solution)/shard_map/backward/pallas_call | solution.py:1163
  147.9 0.0 copy-start
  147.9 2.6 %update.1 = (f32[1,2,48]{2,1,0:T(2,128)}, f32[24,1536]{1,0:T(8,128)}, f32[24,1536]{1,0:T(8,128)}, f32[24,1536]{1,0:T(8,128)}, f32[48,384]{1,0:T(8,128)}, /*index...) custom-call(f32[144,128]{1,0:T(8,128)} %get-tuple-element.78.got, ...), custom_call_target="tpu_custom_call" | custom-call | tf_op jit(solution)/shard_map/update/pallas_call | solution.py:1338
  150.5 2.7 %copy.53 = f32[1,588,384]{2,0,1:T(1,128)} copy(f32[1,588,384]{2,0,1:T(1,128)} %bitcast.17) | data formatting | bytes 1806336
  153.2 0.0 copy-done
  153.2 0.9 copy.54
Async XLA Ops:
  147.9 5.3 %copy-start = (f32[588,1,384]{2,1,0:T(1,128)S(1)}, f32[588,1,384]{2,1,0:T(1,128)}, u32[]{:S(2)}) copy-start(f32[588,1,384]{2,1,0:T(1,128)} %get-tuple-element.77) | copy-start | bytes 2709508

commit v5 on v4

--- a/solution.py
+++ b/solution.py
@@ -218,8 +218,6 @@
                 )
             )
             early[-1].start()
-        for c in next_:
-            c.start()
     else:
         bar = pltpu.get_barrier_semaphore()
         pl.semaphore_signal(bar, inc=1, device_id=(1 - stream, place), device_id_type=MESH)
@@ -241,6 +239,8 @@
     if mine:
         for c in early:
             c.wait_recv()
+        for c in next_:
+            c.start()
         take_shares(stream, wide, got, w1, chan_s, gain_s)
         cols = pl.ds(pl.multiple_of(stream * D, 128), D)
         half = pltpu.make_async_remote_copy(

time: 154 us -> 152 us (0.987)
  Pallas kernels: 149 us -> 146 us
    pallas_call x1, Pallas kernels: 92.5 us -> 88.9 us  [backward(): pl.pallas_call(functools.partial(bwd_kernel, wide, mine), out_shape=[half...]
where the time goes in v5:
time: 152 us; the launch traced here: 151 us
  Pallas kernels  146 us (96%)
  local copies, waits for them, and re-layouts  3.63 us (2%)
    pallas_call x1, Pallas kernels, backward(): pl.pallas_call(functools.partial(bwd_kernel, wide, mine), out_shape=[half...  88.9 us
    pallas_call x1, Pallas kernels, forward(): pl.pallas_call(functools.partial(fwd_kernel, wide, mine), out_shape=[S(*k...  54.9 us
    unnamed x4, local copies, waits for them, and re-layouts  3.63 us

profile of v5, /device:TPU:0, one launch (start us, length us, event | category | flops | bytes accessed | tf_op | source)
XLA Modules:
  0.0 151.3 jit_solution(9188700490432400673)
XLA Ops:
  1.3 54.9 %forward.1 = (bf16[1184,384]{1,0:T(8,128)(2,1)}, f32[6,1200,128]{2,1,0:T(8,128)}, f32[6,1184,128]{2,1,0:T(8,128)}, f32[6,1184,128]{2,1,0:T(8,128)}, f32[1280,128...) custom-call(s32[1]{0:T(128)S(6)} %copy.52.refs_0_, ...), custom_call_target="tpu_custom_call" | custom-call | flops 49999998976 | bytes 1048576 | tf_op jit(solution)/shard_map/forward/pallas_call | solution.py:496
  56.2 88.9 %backward.1 = (f32[588,1,384]{2,1,0:T(1,128)}, f32[588,1,384]{2,1,0:T(1,128)}, f32[144,128]{1,0:T(8,128)}, f32[144,128]{1,0:T(8,128)}, f32[48,768]{1,0:T(8,128)}, /*index=5*/f32[48,768]{1,0:T(8,128)}) custom-call(s32[1]{0:T(128)S(6)} %copy.52.refs_0_, s32[1,3]{1,0:T(1,128)} %refs_1_.4, s32[1,3]{1,0:T(1,128)} %refs_2_.4, bf16[1176,384]{1,0:T(8,128)(2,1)} %bitcast.27, ...), custom_call_target="tpu_custom_call" | custom-call | flops 89999998976 | bytes 1048576 | tf_op jit(solution)/shard_map/backward/pallas_call | solution.py:1163
  145.1 0.0 copy-start
  145.1 2.6 %update.1 = (f32[1,2,48]{2,1,0:T(2,128)}, f32[24,1536]{1,0:T(8,128)}, f32[24,1536]{1,0:T(8,128)}, f32[24,1536]{1,0:T(8,128)}, f32[48,384]{1,0:T(8,128)}, /*index...) custom-call(f32[144,128]{1,0:T(8,128)} %get-tuple-element.78.got, ...), custom_call_target="tpu_custom_call" | custom-call | tf_op jit(solution)/shard_map/update/pallas_call | solution.py:1338
  147.7 2.7 %copy.53 = f32[1,588,384]{2,0,1:T(1,128)} copy(f32[1,588,384]{2,0,1:T(1,128)} %bitcast.17) | data formatting | bytes 1806336
  150.4 0.0 copy-done
  150.4 0.9 copy.54
Async XLA Ops:
  145.1 5.3 %copy-start = (f32[588,1,384]{2,1,0:T(1,128)S(1)}, f32[588,1,384]{2,1,0:T(1,128)}, u32[]{:S(2)}) copy-start(f32[588,1,384]{2,1,0:T(1,128)} %get-tuple-element.77) | copy-start | bytes 2709508
